TPU v7x, 32 devices: a whole 2x2x4 slice. The times are simulated.
32 devices in a mesh: seq: 16 (over z, y, core), batch: 2 (over x).
Axes of the slice: x: 2, y: 2, z: 4, core: 2. Of those that a mesh axis runs over, the one named last changes fastest.
Arguments:
- tokens: bfloat16 [2, 2, 4096, 768], P(None, 'batch', 'seq'), may hold values from -6 to 6
- cotangent: bfloat16 [2, 2, 4096, 768], P(None, 'batch', 'seq'), may hold values from -6 to 6
- masked: int32 [2, 2, 4096], P(None, 'batch', 'seq'), may hold values from 0 to 1, as said below
- query_weight: bfloat16 [2, 768, 768], P(None, ('seq', 'batch')), may hold values from -0.21875 to 0.21875
- key_weight: bfloat16 [2, 768, 768], P(None, ('seq', 'batch')), may hold values from -0.21875 to 0.21875
- value_weight: bfloat16 [2, 768, 768], P(None, ('seq', 'batch')), may hold values from -0.21875 to 0.21875
- output_weight: bfloat16 [2, 768, 768], P(None, ('seq', 'batch')), may hold values from -0.875 to 0.875
- up_weight: bfloat16 [2, 768, 3072], P(None, ('seq', 'batch')), may hold values from -0.21875 to 0.21875
- down_weight: bfloat16 [2, 3072, 768], P(None, ('seq', 'batch')), may hold values from -0.109375 to 0.109375
- query_bias: bfloat16 [2, 768], P(None, ('seq', 'batch')), may hold values from -3 to 3
- value_bias: bfloat16 [2, 768], P(None, ('seq', 'batch')), may hold values from -3 to 3
- output_bias: bfloat16 [2, 768], P(None, ('seq', 'batch')), may hold values from -3 to 3
- up_bias: bfloat16 [2, 3072], P(None, ('seq', 'batch')), may hold values from -3 to 3
- down_bias: bfloat16 [2, 768], P(None, ('seq', 'batch')), may hold values from -3 to 3
- mixer_gain: bfloat16 [2, 768], P(None, ('seq', 'batch')), may hold values from 0.099609375 to 1.8984375
- mixer_shift: bfloat16 [2, 768], P(None, ('seq', 'batch')), may hold values from -3 to 3
- feed_gain: bfloat16 [2, 768], P(None, ('seq', 'batch')), may hold values from 0.099609375 to 1.8984375
- feed_shift: bfloat16 [2, 768], P(None, ('seq', 'batch')), may hold values from -3 to 3
- pool_key: bfloat16 [2, 5, 768], P(None, None, ('seq', 'batch')), may hold values from -3 to 3
- pool_value: bfloat16 [2, 5, 768], P(None, None, ('seq', 'batch')), may hold values from -3 to 3
Outputs:
- layer_output: bfloat16 [2, 2, 4096, 768], P(None, 'batch', 'seq')
- input_grad: bfloat16 [2, 2, 4096, 768], P(None, 'batch', 'seq')
- grad_query_weight: float32 [2, 768, 768], P(None, ('seq', 'batch'))
- grad_key_weight: float32 [2, 768, 768], P(None, ('seq', 'batch'))
- grad_value_weight: float32 [2, 768, 768], P(None, ('seq', 'batch'))
- grad_output_weight: float32 [2, 768, 768], P(None, ('seq', 'batch'))
- grad_up_weight: float32 [2, 768, 3072], P(None, ('seq', 'batch'))
- grad_down_weight: float32 [2, 3072, 768], P(None, ('seq', 'batch'))
- grad_query_bias: float32 [2, 768], P(None, ('seq', 'batch'))
- grad_value_bias: float32 [2, 768], P(None, ('seq', 'batch'))
- grad_output_bias: float32 [2, 768], P(None, ('seq', 'batch'))
- grad_up_bias: float32 [2, 3072], P(None, ('seq', 'batch'))
- grad_down_bias: float32 [2, 768], P(None, ('seq', 'batch'))
- grad_mixer_gain: float32 [2, 768], P(None, ('seq', 'batch'))
- grad_mixer_shift: float32 [2, 768], P(None, ('seq', 'batch'))
- grad_feed_gain: float32 [2, 768], P(None, ('seq', 'batch'))
- grad_feed_shift: float32 [2, 768], P(None, ('seq', 'batch'))
- grad_pool_key: float32 [2, 5, 768], P(None, None, ('seq', 'batch'))
- grad_pool_value: float32 [2, 5, 768], P(None, None, ('seq', 'batch'))
Inputs may be any that keep to these rules, and one draw needn't show every extreme that they name: `masked`: 1 marks a token whose output gradient is taken, 0 one whose is not; in each aligned block of 64 tokens of a sequence the chance of a 1 is drawn between 5 and 40 percent.
All inputs are finite; a program needn't handle non-finite values.
Results may differ from a plain program's by a relative error of at most 0.033.
Values may be sent and summed in bfloat16 or wider, within the bound.
No kernel may reach another device: no remote copies, remote signals or barrier semaphores. Data moves between devices by JAX's collectives and lax.ppermute only.
A program may use at most 256 MiB of HBM per device.

v0:
```python
import jax
import jax.numpy as jnp
from jax import lax
from jax.sharding import PartitionSpec as P

HEADS = 12
WIN = 64
PWIN = 256


norm_eps = 1e-05
gelu_coef = 0.7978845608028654
masked_score = -1e30


def passed_along(value, axis, steps):
    count = lax.axis_size(axis)
    initial, last = (max(0, -steps), min(count, count - steps))
    return lax.ppermute(value, axis, [(source, source + steps) for source in range(initial, last)])


def with_halo(block, sides, width):
    for axis, dim in sides:
        count = lax.axis_size(axis)
        forward = [(i, i + 1) for i in range(count - 1)]
        backward = [(target, source) for source, target in forward]
        low = lax.ppermute(
            lax.slice_in_dim(block, block.shape[dim] - width, None, axis=dim), axis, forward
        )
        high = lax.ppermute(lax.slice_in_dim(block, 0, width, axis=dim), axis, backward)
        block = jnp.concatenate([low, block, high], axis=dim)
    return block


def layer_norm(inputs, gain_vec, shift_vec):
    centre = inputs - jnp.mean(inputs, axis=-1, keepdims=True)
    spread = jnp.mean(centre * centre, axis=-1, keepdims=True)
    return centre * lax.rsqrt(spread + norm_eps) * gain_vec + shift_vec


def gelu_tanh(inputs):
    return (
        0.5 * inputs * (1.0 + jnp.tanh(gelu_coef * (inputs + 0.044715 * inputs * inputs * inputs)))
    )


def product(left_side, weight):
    return jnp.einsum("sbd,de->sbe", left_side, weight, preferred_element_type=jnp.float32)


def product_back(grads, weight):
    return jnp.einsum("sbe,de->sbd", grads, weight, preferred_element_type=jnp.float32)


def weight_grad(inputs, grads):
    return jnp.einsum("sbd,sbe->de", inputs, grads, preferred_element_type=jnp.float32)


def row_total(grads):
    return jnp.sum(grads.astype(jnp.float32), axis=(0, 1))


def fetch_weights(params, layer_index):
    return (
        lax.all_gather(params[0][layer_index], ("seq", "batch"), axis=0, tiled=True),
        lax.all_gather(params[1][layer_index], ("seq", "batch"), axis=0, tiled=True),
        lax.all_gather(params[2][layer_index], ("seq", "batch"), axis=0, tiled=True),
        lax.all_gather(params[3][layer_index], ("seq", "batch"), axis=0, tiled=True),
        lax.all_gather(params[4][layer_index], ("seq", "batch"), axis=0, tiled=True),
        lax.all_gather(params[5][layer_index], ("seq", "batch"), axis=0, tiled=True),
        lax.all_gather(params[6][layer_index], ("seq", "batch"), axis=0, tiled=True),
        lax.all_gather(params[7][layer_index], ("seq", "batch"), axis=0, tiled=True),
        lax.all_gather(params[8][layer_index], ("seq", "batch"), axis=0, tiled=True),
        lax.all_gather(params[9][layer_index], ("seq", "batch"), axis=0, tiled=True),
        lax.all_gather(params[10][layer_index], ("seq", "batch"), axis=0, tiled=True),
        lax.all_gather(params[11][layer_index], ("seq", "batch"), axis=0, tiled=True),
        lax.all_gather(params[12][layer_index], ("seq", "batch"), axis=0, tiled=True),
        lax.all_gather(params[13][layer_index], ("seq", "batch"), axis=0, tiled=True),
        lax.all_gather(params[14][layer_index], ("seq", "batch"), axis=0, tiled=True),
        lax.all_gather(params[15][layer_index], ("seq", "batch"), axis=1, tiled=True),
        lax.all_gather(params[16][layer_index], ("seq", "batch"), axis=1, tiled=True),
    )


def reduce_grads(grads):
    summed = (
        lax.psum_scatter(grads[0], ("seq", "batch"), scatter_dimension=0, tiled=True),
        lax.psum_scatter(grads[1], ("seq", "batch"), scatter_dimension=0, tiled=True),
        lax.psum_scatter(grads[2], ("seq", "batch"), scatter_dimension=0, tiled=True),
        lax.psum_scatter(grads[3], ("seq", "batch"), scatter_dimension=0, tiled=True),
        lax.psum_scatter(grads[4], ("seq", "batch"), scatter_dimension=0, tiled=True),
        lax.psum_scatter(grads[5], ("seq", "batch"), scatter_dimension=0, tiled=True),
        lax.psum_scatter(grads[6], ("seq", "batch"), scatter_dimension=0, tiled=True),
        lax.psum_scatter(grads[7], ("seq", "batch"), scatter_dimension=0, tiled=True),
        lax.psum_scatter(grads[8], ("seq", "batch"), scatter_dimension=0, tiled=True),
        lax.psum_scatter(grads[9], ("seq", "batch"), scatter_dimension=0, tiled=True),
        lax.psum_scatter(grads[10], ("seq", "batch"), scatter_dimension=0, tiled=True),
        lax.psum_scatter(grads[11], ("seq", "batch"), scatter_dimension=0, tiled=True),
        lax.psum_scatter(grads[12], ("seq", "batch"), scatter_dimension=0, tiled=True),
        lax.psum_scatter(grads[13], ("seq", "batch"), scatter_dimension=0, tiled=True),
        lax.psum_scatter(grads[14], ("seq", "batch"), scatter_dimension=0, tiled=True),
        lax.psum_scatter(
            jnp.transpose(grads[15]), ("seq", "batch"), scatter_dimension=0, tiled=True
        ),
        lax.psum_scatter(
            jnp.transpose(grads[16]), ("seq", "batch"), scatter_dimension=0, tiled=True
        ),
    )
    return tuple(summed[:15]) + (jnp.transpose(summed[15]), jnp.transpose(summed[16]))


def window_masks(block_len):
    seq_len = block_len * lax.axis_size("seq")
    first_row = lax.axis_index("seq") * block_len
    pooled_len = block_len // 4
    reach = PWIN // 4
    positions = first_row + jnp.arange(block_len, dtype=jnp.int32)
    near_pos = first_row - WIN + jnp.arange(block_len + 2 * WIN, dtype=jnp.int32)
    far_pos = (
        lax.axis_index("seq") * pooled_len
        - reach
        + jnp.arange(pooled_len + 2 * reach, dtype=jnp.int32)
    )
    near_mask = (
        (jnp.abs(positions[:, None] - near_pos[None, :]) <= WIN)
        & (near_pos[None, :] >= 0)
        & (near_pos[None, :] < seq_len)
    )
    far_mask = (
        (jnp.abs(positions[:, None] - 4 * far_pos[None, :]) <= PWIN)
        & (far_pos[None, :] >= 0)
        & (far_pos[None, :] < seq_len // 4)
    )
    return (near_mask, far_mask)


def pool_block(extended, kernel, block_len):
    total = jnp.zeros(extended.shape[:2] + (block_len // 4, extended.shape[3]), jnp.float32)
    for offset in range(5):
        taps_rows = extended[:, :, WIN - 2 + offset : WIN - 2 + offset + block_len : 4]
        total = total + kernel[:, offset][:, None, None, :] * taps_rows.astype(jnp.float32)
    return total


def pooled_rims(pooled_low, block_len):
    pooled_len = block_len // 4
    reach = PWIN // 4
    hop_count = (reach + pooled_len - 1) // pooled_len
    from_lower = []
    from_upper = []
    for distance in range(1, hop_count + 1):
        from_lower.append(passed_along(pooled_low, "seq", distance))
        from_upper.append(passed_along(pooled_low, "seq", -distance))
    joined = jnp.concatenate(from_lower[::-1] + [pooled_low] + from_upper, axis=2)
    return joined


def pooled_return(grad_ext, block_len):
    pooled_len = block_len // 4
    reach = PWIN // 4
    hop_count = (reach + pooled_len - 1) // pooled_len
    total = grad_ext[:, :, hop_count * pooled_len : (hop_count + 1) * pooled_len]
    for distance in range(1, hop_count + 1):
        below_part = grad_ext[
            :, :, (hop_count - distance) * pooled_len : (hop_count - distance + 1) * pooled_len
        ]
        above_part = grad_ext[
            :, :, (hop_count + distance) * pooled_len : (hop_count + distance + 1) * pooled_len
        ]
        total = total + passed_along(below_part.astype(jnp.bfloat16), "seq", -distance).astype(
            below_part.dtype
        )
        total = total + passed_along(above_part.astype(jnp.bfloat16), "seq", distance).astype(
            above_part.dtype
        )
    return total


def softmax_forward(query_heads, key_heads, allowed_mask, score_scale):
    scores = (
        jnp.einsum("sbhd,sehd->shbe", query_heads, key_heads, preferred_element_type=jnp.float32)
        * score_scale
    )
    scores = jnp.where(allowed_mask[None, None], scores, masked_score)
    row_max = jnp.max(scores, axis=-1, keepdims=True)
    row_lse = row_max + jnp.log(jnp.sum(jnp.exp(scores - row_max), axis=-1, keepdims=True))
    return (jnp.exp(scores - row_lse).astype(jnp.bfloat16), row_lse)


def softmax_backward(
    query_heads, key_heads, value_heads, grad_mixed, allowed_mask, row_lse, score_scale
):
    scores = (
        jnp.einsum("sbhd,sehd->shbe", query_heads, key_heads, preferred_element_type=jnp.float32)
        * score_scale
    )
    scores = jnp.where(allowed_mask[None, None], scores, masked_score)
    probability = jnp.exp(scores - row_lse)
    grad_probs = jnp.einsum(
        "sbhd,sehd->shbe", grad_mixed, value_heads, preferred_element_type=jnp.float32
    )
    row_dot = jnp.sum(probability * grad_probs, axis=-1, keepdims=True)
    grad_scores = (probability * (grad_probs - row_dot)).astype(jnp.bfloat16)
    grad_values = jnp.einsum(
        "shbe,sbhd->sehd",
        probability.astype(jnp.bfloat16),
        grad_mixed,
        preferred_element_type=jnp.float32,
    )
    grad_keys = (
        jnp.einsum("shbe,sbhd->sehd", grad_scores, query_heads, preferred_element_type=jnp.float32)
        * score_scale
    )
    grad_query = (
        jnp.einsum("shbe,sehd->sbhd", grad_scores, key_heads, preferred_element_type=jnp.float32)
        * score_scale
    )
    return (grad_query, grad_keys, grad_values)


def layer_forward(inputs, weights, near_mask, far_mask):
    (
        query_weight,
        key_weight,
        value_weight,
        output_weight,
        up_weight,
        down_weight,
        query_bias,
        value_bias,
        output_bias,
        up_bias,
        down_bias,
        mixer_gain,
        mixer_shift,
        feed_gain,
        feed_shift,
        pool_key,
        pool_value,
    ) = weights
    seq_count, block_len, width = inputs.shape
    head_dim = width // HEADS
    score_scale = head_dim ** (-0.5)
    inputs_low = inputs.astype(jnp.bfloat16)
    query = (product(inputs_low, query_weight) + query_bias.astype(jnp.float32)).astype(
        jnp.bfloat16
    )
    key_rows = product(inputs_low, key_weight).astype(jnp.bfloat16)
    value_rows = (product(inputs_low, value_weight) + value_bias.astype(jnp.float32)).astype(
        jnp.bfloat16
    )
    extended = with_halo(jnp.stack([key_rows, value_rows]), (("seq", 2),), WIN)
    kernel = jnp.stack([pool_key, pool_value]).astype(jnp.float32)
    pooled_low = pool_block(extended, kernel, block_len).astype(jnp.bfloat16)
    pooled_ext = pooled_rims(pooled_low, block_len)
    query_heads = query.reshape(seq_count, block_len, HEADS, head_dim)
    near_keys = extended[0].reshape(seq_count, -1, HEADS, head_dim)
    near_values = extended[1].reshape(seq_count, -1, HEADS, head_dim)
    far_keys = pooled_ext[0].reshape(seq_count, -1, HEADS, head_dim)
    far_values = pooled_ext[1].reshape(seq_count, -1, HEADS, head_dim)
    near_probs, near_lse = softmax_forward(query_heads, near_keys, near_mask, score_scale)
    far_probs, far_lse = softmax_forward(query_heads, far_keys, far_mask, score_scale)
    mixed = jnp.einsum(
        "shbe,sehd->sbhd", near_probs, near_values, preferred_element_type=jnp.float32
    )
    mixed = mixed + jnp.einsum(
        "shbe,sehd->sbhd", far_probs, far_values, preferred_element_type=jnp.float32
    )
    mixed_low = mixed.reshape(seq_count, block_len, width).astype(jnp.bfloat16)
    attention = product(mixed_low, output_weight) + output_bias.astype(jnp.float32)
    residual = inputs + attention
    hidden = layer_norm(residual, mixer_gain.astype(jnp.float32), mixer_shift.astype(jnp.float32))
    pre_act = product(hidden.astype(jnp.bfloat16), up_weight) + up_bias.astype(jnp.float32)
    act_low = gelu_tanh(pre_act).astype(jnp.bfloat16)
    feed_out = product(act_low, down_weight) + down_bias.astype(jnp.float32)
    residual_two = hidden + feed_out
    result = layer_norm(residual_two, feed_gain.astype(jnp.float32), feed_shift.astype(jnp.float32))
    kept_state = (
        inputs,
        query,
        extended,
        pooled_ext,
        near_lse,
        far_lse,
        mixed_low,
        residual,
        hidden,
        pre_act,
        residual_two,
    )
    return (result, kept_state)


def layer_backward(grad_result, kept_state, weights, near_mask, far_mask):
    (
        query_weight,
        key_weight,
        value_weight,
        output_weight,
        up_weight,
        down_weight,
        query_bias,
        value_bias,
        output_bias,
        up_bias,
        down_bias,
        mixer_gain,
        mixer_shift,
        feed_gain,
        feed_shift,
        pool_key,
        pool_value,
    ) = weights
    (
        inputs,
        query,
        extended,
        pooled_ext,
        near_lse,
        far_lse,
        mixed_low,
        residual,
        hidden,
        pre_act,
        residual_two,
    ) = kept_state
    seq_count, block_len, width = inputs.shape
    head_dim = width // HEADS
    score_scale = head_dim ** (-0.5)
    unused_out, feed_norm_back = jax.vjp(
        layer_norm, residual_two, feed_gain.astype(jnp.float32), feed_shift.astype(jnp.float32)
    )
    grad_residual_two, grad_feed_gain, grad_feed_shift = feed_norm_back(grad_result)
    grad_feed_low = grad_residual_two.astype(jnp.bfloat16)
    act_low = gelu_tanh(pre_act).astype(jnp.bfloat16)
    grad_down_weight = weight_grad(act_low, grad_feed_low)
    grad_down_bias = row_total(grad_feed_low)
    unused_act, gelu_back = jax.vjp(gelu_tanh, pre_act)
    grad_pre = gelu_back(product_back(grad_feed_low, down_weight))[0].astype(jnp.bfloat16)
    grad_up_weight = weight_grad(hidden.astype(jnp.bfloat16), grad_pre)
    grad_up_bias = row_total(grad_pre)
    grad_hidden = grad_residual_two + product_back(grad_pre, up_weight)
    unused_hidden, mixer_norm_back = jax.vjp(
        layer_norm, residual, mixer_gain.astype(jnp.float32), mixer_shift.astype(jnp.float32)
    )
    grad_residual, grad_mixer_gain, grad_mixer_shift = mixer_norm_back(grad_hidden)
    grad_attention = grad_residual.astype(jnp.bfloat16)
    grad_output_weight = weight_grad(mixed_low, grad_attention)
    grad_output_bias = row_total(grad_attention)
    grad_mixed = (
        product_back(grad_attention, output_weight)
        .astype(jnp.bfloat16)
        .reshape(seq_count, block_len, HEADS, head_dim)
    )
    query_heads = query.reshape(seq_count, block_len, HEADS, head_dim)
    near_keys = extended[0].reshape(seq_count, -1, HEADS, head_dim)
    near_values = extended[1].reshape(seq_count, -1, HEADS, head_dim)
    far_keys = pooled_ext[0].reshape(seq_count, -1, HEADS, head_dim)
    far_values = pooled_ext[1].reshape(seq_count, -1, HEADS, head_dim)
    near_grad_query, near_grad_keys, near_grad_values = softmax_backward(
        query_heads, near_keys, near_values, grad_mixed, near_mask, near_lse, score_scale
    )
    far_grad_query, far_grad_keys, far_grad_values = softmax_backward(
        query_heads, far_keys, far_values, grad_mixed, far_mask, far_lse, score_scale
    )
    grad_query = (
        (near_grad_query + far_grad_query).reshape(seq_count, block_len, width).astype(jnp.bfloat16)
    )
    grad_pooled_ext = jnp.stack([far_grad_keys, far_grad_values]).reshape(2, seq_count, -1, width)
    grad_pooled = pooled_return(grad_pooled_ext, block_len).astype(jnp.bfloat16)
    grad_kernel = jnp.stack(
        [
            jnp.einsum(
                "aspd,aspd->ad",
                grad_pooled,
                extended[:, :, WIN - 2 + offset : WIN - 2 + offset + block_len : 4],
                preferred_element_type=jnp.float32,
            )
            for offset in range(5)
        ],
        axis=1,
    )
    kernel = jnp.stack([pool_key, pool_value]).astype(jnp.float32)
    grad_extended = jnp.stack([near_grad_keys, near_grad_values]).reshape(2, seq_count, -1, width)
    for offset in range(5):
        grad_extended = grad_extended.at[
            :, :, WIN - 2 + offset : WIN - 2 + offset + block_len : 4
        ].add(kernel[:, offset][:, None, None, :] * grad_pooled.astype(jnp.float32))
    from_upper = passed_along(grad_extended[:, :, :WIN].astype(jnp.bfloat16), "seq", -1).astype(
        jnp.float32
    )
    from_lower = passed_along(
        grad_extended[:, :, block_len + WIN :].astype(jnp.bfloat16), "seq", 1
    ).astype(jnp.float32)
    grad_local = grad_extended[:, :, WIN : WIN + block_len]
    grad_local = grad_local.at[:, :, block_len - WIN :].add(from_upper)
    grad_local = grad_local.at[:, :, :WIN].add(from_lower)
    grad_pairs = grad_local.astype(jnp.bfloat16)
    inputs_low = inputs.astype(jnp.bfloat16)
    grad_query_weight = weight_grad(inputs_low, grad_query)
    grad_key_weight = weight_grad(inputs_low, grad_pairs[0])
    grad_value_weight = weight_grad(inputs_low, grad_pairs[1])
    grad_query_bias = row_total(grad_query)
    grad_value_bias = row_total(grad_pairs[1])
    grad_inputs = grad_residual + product_back(grad_query, query_weight)
    grad_inputs = (
        grad_inputs
        + product_back(grad_pairs[0], key_weight)
        + product_back(grad_pairs[1], value_weight)
    )
    layer_grads = (
        grad_query_weight,
        grad_key_weight,
        grad_value_weight,
        grad_output_weight,
        grad_up_weight,
        grad_down_weight,
        grad_query_bias,
        grad_value_bias,
        grad_output_bias,
        grad_up_bias,
        grad_down_bias,
        grad_mixer_gain,
        grad_mixer_shift,
        grad_feed_gain,
        grad_feed_shift,
        grad_kernel[0],
        grad_kernel[1],
    )
    return (grad_inputs, layer_grads)


def on_device(
    tokens,
    cotangent,
    masked,
    query_weight,
    key_weight,
    value_weight,
    output_weight,
    up_weight,
    down_weight,
    query_bias,
    value_bias,
    output_bias,
    up_bias,
    down_bias,
    mixer_gain,
    mixer_shift,
    feed_gain,
    feed_shift,
    pool_key,
    pool_value,
):
    params = (
        query_weight,
        key_weight,
        value_weight,
        output_weight,
        up_weight,
        down_weight,
        query_bias,
        value_bias,
        output_bias,
        up_bias,
        down_bias,
        mixer_gain,
        mixer_shift,
        feed_gain,
        feed_shift,
        pool_key,
        pool_value,
    )
    micro_count, seq_count, block_len, width = tokens.shape
    layer_count = query_weight.shape[0]
    near_mask, far_mask = window_masks(block_len)
    totals = [None] * layer_count
    outputs = []
    input_grads = []
    for batch_index in range(micro_count):
        current = [fetch_weights(params, layer_index) for layer_index in range(layer_count)]
        hidden_rows = tokens[batch_index].astype(jnp.float32)
        states = []
        for layer_index in range(layer_count):
            hidden_rows, kept_state = layer_forward(
                hidden_rows, current[layer_index], near_mask, far_mask
            )
            states.append(kept_state)
        outputs.append(hidden_rows.astype(jnp.bfloat16))
        grad_rows = (
            cotangent[batch_index].astype(jnp.float32)
            * masked[batch_index].astype(jnp.float32)[..., None]
        )
        for layer_index in reversed(range(layer_count)):
            grad_rows, layer_grads = layer_backward(
                grad_rows, states[layer_index], current[layer_index], near_mask, far_mask
            )
            if batch_index == 0:
                totals[layer_index] = layer_grads
            else:
                totals[layer_index] = jax.tree.map(jnp.add, totals[layer_index], layer_grads)
        input_grads.append(grad_rows.astype(jnp.bfloat16))
    totals = [reduce_grads(totals[layer_index]) for layer_index in range(layer_count)]
    results = (jnp.stack(outputs), jnp.stack(input_grads))
    stacked = tuple(
        (
            jnp.stack([totals[layer_index][position] for layer_index in range(layer_count)])
            for position in range(17)
        )
    )
    return results + stacked


def solution(mesh):
    return jax.shard_map(
        on_device,
        mesh=mesh,
        in_specs=(
            P(None, "batch", "seq", None),
            P(None, "batch", "seq", None),
            P(None, "batch", "seq"),
            P(None, ("seq", "batch"), None),
            P(None, ("seq", "batch"), None),
            P(None, ("seq", "batch"), None),
            P(None, ("seq", "batch"), None),
            P(None, ("seq", "batch"), None),
            P(None, ("seq", "batch"), None),
            P(None, ("seq", "batch")),
            P(None, ("seq", "batch")),
            P(None, ("seq", "batch")),
            P(None, ("seq", "batch")),
            P(None, ("seq", "batch")),
            P(None, ("seq", "batch")),
            P(None, ("seq", "batch")),
            P(None, ("seq", "batch")),
            P(None, ("seq", "batch")),
            P(None, None, ("seq", "batch")),
            P(None, None, ("seq", "batch")),
        ),
        out_specs=(
            P(None, "batch", "seq", None),
            P(None, "batch", "seq", None),
            P(None, ("seq", "batch"), None),
            P(None, ("seq", "batch"), None),
            P(None, ("seq", "batch"), None),
            P(None, ("seq", "batch"), None),
            P(None, ("seq", "batch"), None),
            P(None, ("seq", "batch"), None),
            P(None, ("seq", "batch")),
            P(None, ("seq", "batch")),
            P(None, ("seq", "batch")),
            P(None, ("seq", "batch")),
            P(None, ("seq", "batch")),
            P(None, ("seq", "batch")),
            P(None, ("seq", "batch")),
            P(None, ("seq", "batch")),
            P(None, ("seq", "batch")),
            P(None, None, ("seq", "batch")),
            P(None, None, ("seq", "batch")),
        ),
        check_vma=False,
    )
```

profile of v0, /device:TPU:0, one launch (start us, length us, event | category | flops | bytes accessed | tf_op | source)
XLA Modules:
  0.0 2881.4 jit_solution(16897131235672365799)
XLA Ops:
  27.9 43.0 %all-reduce.41 = (bf16[768]{0:T(1024)(128)(2,1)S(1)}, bf16[768]{0:T(1024)(128)(2,1)S(1)}, bf16[768]{0:T(1024)(128)(2,1)S(1)}, bf16[768]{0:T(1024)(128)(2,1)S(1)}...) all-reduce(bf16[768]{0:T(1024)(128)(2,1)S(1)} %dynamic-update-slice, ...), channel_id=4, replica_groups=mesh['seq'=16,'batch'=2] {'seq','batch'}, use_global_device_ids=true, to_apply=%add | all-reduce | flops 18432 | bytes 73728
  76.8 68.5 %all-gather.5 = bf16[1,5,768]{1,0,2:T(2,128)(2,1)S(1)} all-gather(bf16[1,5,24]{1,0,2:T(2,128)(2,1)S(1)} %copy.638), channel_id=7, replica_groups=mesh['seq'=16,'batch'=2] {'seq','batch'}, dimensions={2}, use_global_device_ids=true | all-gather | bytes 7920 | tf_op jit(solution)/shard_map/all_gather | solution.py:80
  145.6 65.8 %all-gather.6 = bf16[1,5,768]{1,0,2:T(2,128)(2,1)S(1)} all-gather(bf16[1,5,24]{1,0,2:T(2,128)(2,1)S(1)} %copy.639), channel_id=8, replica_groups=mesh['seq'=16,'batch'=2] {'seq','batch'}, dimensions={2}, use_global_device_ids=true | all-gather | bytes 7920 | tf_op jit(solution)/shard_map/all_gather | solution.py:81
  211.9 68.4 %all-gather.22 = bf16[1,5,768]{1,0,2:T(2,128)(2,1)S(1)} all-gather(bf16[1,5,24]{1,0,2:T(2,128)(2,1)S(1)} %copy.640), channel_id=24, replica_groups=mesh['seq'=16,'batch'=2] {'seq','batch'}, dimensions={2}, use_global_device_ids=true | all-gather | bytes 7920 | tf_op jit(solution)/shard_map/all_gather | solution.py:80
  280.6 66.9 %all-gather.23 = bf16[1,5,768]{1,0,2:T(2,128)(2,1)S(1)} all-gather(bf16[1,5,24]{1,0,2:T(2,128)(2,1)S(1)} %copy.641), channel_id=25, replica_groups=mesh['seq'=16,'batch'=2] {'seq','batch'}, dimensions={2}, use_global_device_ids=true | all-gather | bytes 7920 | tf_op jit(solution)/shard_map/all_gather | solution.py:81
  449.3 40.4 %all-gather.61.cloned.1.call-done = bf16[1,768,768]{2,1,0:T(8,128)(2,1)} async-done(((bf16[1,24,768]{2,1,0:T(8,128)(2,1)}), bf16[1,768,768]{2,1,0:T(8,128)(2,1)}) %all-gather.61.cloned.1.call-update) | async-done | bytes 1179664 | tf_op jit(solution)/shard_map/all_gather | solution.py:67
  494.6 12.1 collective-permute-start.5
  506.7 39.1 %all-gather.63.cloned.1.call-done = bf16[1,768,768]{2,1,0:T(8,128)(2,1)} async-done(((bf16[1,24,768]{2,1,0:T(8,128)(2,1)}), bf16[1,768,768]{2,1,0:T(8,128)(2,1)}) %all-gather.63.cloned.1.call-update) | async-done | bytes 1179664 | tf_op jit(solution)/shard_map/all_gather | solution.py:65
  617.1 50.7 %all-gather.67.cloned.1.call-done = bf16[1,768,3072]{2,1,0:T(8,128)(2,1)} async-done(((bf16[1,24,3072]{2,1,0:T(8,128)(2,1)}), bf16[1,768,3072]{2,1,0:T(8,128)(2,1)}) %all-gather.67.cloned.1.call-update) | async-done | bytes 4718608 | tf_op jit(solution)/shard_map/all_gather | solution.py:69
  673.3 60.4 %all-gather.69.cloned.1.call-done = bf16[1,3072,768]{2,1,0:T(8,128)(2,1)} async-done(((bf16[1,96,768]{2,1,0:T(8,128)(2,1)}), bf16[1,3072,768]{2,1,0:T(8,128)(2,1)}) %all-gather.69.cloned.1.call-update) | async-done | bytes 4718608 | tf_op jit(solution)/shard_map/all_gather | solution.py:70
  937.4 9.5 scatter_fusion.10
  946.9 9.7 scatter_fusion.11
  956.5 9.5 scatter_fusion.12
  966.0 9.5 scatter_fusion.13
  975.5 9.5 scatter_fusion.14
  1216.0 9.5 scatter_fusion.15
  1225.5 9.5 scatter_fusion.16
  1235.0 9.5 scatter_fusion.17
  1244.5 9.8 scatter_fusion.18
  1406.2 70.7 %all-reduce.44.cloned.1.call-done = (f32[768]{0:T(1024)}, f32[768]{0:T(1024)}, f32[768]{0:T(1024)}, f32[768]{0:T(1024)}, f32[768]{0:T(1024)}, /*index=5*/f32[768...) async-done(((f32[768]{0:T(1024)}, f32[768]{0:T(1024)}, ...) | async-done | bytes 135184
  1499.9 82.8 %reduce-scatter.43.cloned.1.call-done = f32[24,768]{1,0:T(8,128)} async-done(((f32[768,768]{1,0:T(8,128)}), f32[24,768]{1,0:T(8,128)}) %reduce-scatter.43.cloned.1.call-update) | async-done | bytes 73744
  1583.9 102.9 %reduce-scatter.51.cloned.1.call-done = f32[24,768]{1,0:T(8,128)} async-done(((f32[768,768]{1,0:T(8,128)}), f32[24,768]{1,0:T(8,128)}) %reduce-scatter.51.cloned.1.call-update) | async-done | bytes 73744
  1688.0 101.9 %reduce-scatter.47.cloned.1.call-done = f32[24,768]{1,0:T(8,128)} async-done(((f32[768,768]{1,0:T(8,128)}), f32[24,768]{1,0:T(8,128)}) %reduce-scatter.47.cloned.1.call-update) | async-done | bytes 73744
  1791.1 102.9 %reduce-scatter.41.cloned.1.call-done = f32[24,768]{1,0:T(8,128)} async-done(((f32[768,768]{1,0:T(8,128)}), f32[24,768]{1,0:T(8,128)}) %reduce-scatter.41.cloned.1.call-update) | async-done | bytes 73744
  1895.2 101.9 %reduce-scatter.31.cloned.1.call-done = f32[24,768]{1,0:T(8,128)} async-done(((f32[768,768]{1,0:T(8,128)}), f32[24,768]{1,0:T(8,128)}) %reduce-scatter.31.cloned.1.call-update) | async-done | bytes 73744 | tf_op jit(solution)/shard_map/reduce_scatter | solution.py:90
  1997.2 104.2 %reduce-scatter.29.cloned.1.call-done = f32[24,768]{1,0:T(8,128)} async-done(((f32[768,768]{1,0:T(8,128)}), f32[24,768]{1,0:T(8,128)}) %reduce-scatter.29.cloned.1.call-update) | async-done | bytes 73744 | tf_op jit(solution)/shard_map/reduce_scatter | solution.py:90
  2103.6 100.9 %reduce-scatter.49.cloned.1.call-done = f32[24,768]{1,0:T(8,128)} async-done(((f32[768,768]{1,0:T(8,128)}), f32[24,768]{1,0:T(8,128)}) %reduce-scatter.49.cloned.1.call-update) | async-done | bytes 73744
  2205.7 102.9 %reduce-scatter.45.cloned.1.call-done = f32[24,768]{1,0:T(8,128)} async-done(((f32[768,768]{1,0:T(8,128)}), f32[24,768]{1,0:T(8,128)}) %reduce-scatter.45.cloned.1.call-update) | async-done | bytes 73744
  2311.1 138.1 %reduce-scatter.39.cloned.1.call-done = f32[96,768]{1,0:T(8,128)} async-done(((f32[3072,768]{1,0:T(8,128)}), f32[96,768]{1,0:T(8,128)}) %reduce-scatter.39.cloned.1.call-update) | async-done | bytes 294928 | tf_op jit(solution)/shard_map/reduce_scatter | solution.py:92
  2449.2 141.5 %reduce-scatter.37.cloned.1.call-done = f32[96,768]{1,0:T(8,128)} async-done(((f32[3072,768]{1,0:T(8,128)}), f32[96,768]{1,0:T(8,128)}) %reduce-scatter.37.cloned.1.call-update) | async-done | bytes 294928 | tf_op jit(solution)/shard_map/reduce_scatter | solution.py:92
  2592.6 138.4 %reduce-scatter.35.cloned.1.call-done = f32[24,3072]{1,0:T(8,128)} async-done(((f32[768,3072]{1,0:T(8,128)}), f32[24,3072]{1,0:T(8,128)}) %reduce-scatter.35.cloned.1.call-update) | async-done | bytes 294928 | tf_op jit(solution)/shard_map/reduce_scatter | solution.py:91
  2731.0 141.5 %reduce-scatter.33.cloned.1.call-done = f32[24,3072]{1,0:T(8,128)} async-done(((f32[768,3072]{1,0:T(8,128)}), f32[24,3072]{1,0:T(8,128)}) %reduce-scatter.33.cloned.1.call-update) | async-done | bytes 294928 | tf_op jit(solution)/shard_map/reduce_scatter | solution.py:91
  (1500 shorter events, 829.4 us)
Async XLA Ops:
  7.3 341.8 %all-gather.47.cloned.1.call-start = ((), (), s32[]{:S(2)}) async-start(), calls=%async_computation.18 | async-start | bytes 1216512 | tf_op jit(solution)/shard_map/all_gather | solution.py:66
  8.8 342.1 %all-gather.49.cloned.1.call-start = ((), (), s32[]{:S(2)}) async-start(), calls=%async_computation.19 | async-start | bytes 1216512 | tf_op jit(solution)/shard_map/all_gather | solution.py:67
  10.3 347.9 %all-gather.51.cloned.1.call-start = ((), (), s32[]{:S(2)}) async-start(), calls=%async_computation.20 | async-start | bytes 1216512 | tf_op jit(solution)/shard_map/all_gather | solution.py:65
  11.8 420.6 %all-gather.53.cloned.1.call-start = ((), (), s32[]{:S(2)}) async-start(), calls=%async_computation.21 | async-start | bytes 1216512 | tf_op jit(solution)/shard_map/all_gather | solution.py:68
  13.3 421.5 %all-gather.55.cloned.1.call-start = ((), (), s32[]{:S(2)}) async-start(), calls=%async_computation.22 | async-start | bytes 4866048 | tf_op jit(solution)/shard_map/all_gather | solution.py:69
  15.1 425.2 %all-gather.57.cloned.1.call-start = ((), (), s32[]{:S(2)}) async-start(), calls=%async_computation.23 | async-start | bytes 4866048 | tf_op jit(solution)/shard_map/all_gather | solution.py:70
  16.9 430.6 %all-gather.59.cloned.1.call-start = ((), (), s32[]{:S(2)}) async-start(), calls=%async_computation.24 | async-start | bytes 1216512 | tf_op jit(solution)/shard_map/all_gather | solution.py:66
  17.6 472.1 %all-gather.61.cloned.1.call-start = ((), (), s32[]{:S(2)}) async-start(), calls=%async_computation.25 | async-start | bytes 1216512 | tf_op jit(solution)/shard_map/all_gather | solution.py:67
  18.4 527.4 %all-gather.63.cloned.1.call-start = ((), (), s32[]{:S(2)}) async-start(), calls=%async_computation.26 | async-start | bytes 1216512 | tf_op jit(solution)/shard_map/all_gather | solution.py:65
  19.1 595.4 %all-gather.65.cloned.1.call-start = ((), (), s32[]{:S(2)}) async-start(), calls=%async_computation.27 | async-start | bytes 1216512 | tf_op jit(solution)/shard_map/all_gather | solution.py:68
  19.7 648.1 %all-gather.67.cloned.1.call-start = ((), (), s32[]{:S(2)}) async-start(), calls=%async_computation.28 | async-start | bytes 4866048 | tf_op jit(solution)/shard_map/all_gather | solution.py:69
  20.4 713.2 %all-gather.69.cloned.1.call-start = ((), (), s32[]{:S(2)}) async-start(), calls=%async_computation.29 | async-start | bytes 4866048 | tf_op jit(solution)/shard_map/all_gather | solution.py:70
  21.0 1455.9 %all-reduce.44.cloned.1.call-start = ((), (), s32[]{:S(2)}) async-start(), calls=%async_computation.36 | async-start | bytes 376832
  492.4 55.9 %collective-permute-start.4 = (bf16[2,1,64,768]{3,2,1,0:T(8,128)(2,1)}, bf16[2,1,64,768]{3,2,1,0:T(8,128)(2,1)S(1)}, u32[]{:S(2)}, u32[]{:S(2)}) collective-permute-start(bf16[2,1,64,768]{3,2,1,0:T(8,128)(2,1)} %get-tuple-element.375), channel_id=1, source_target_pairs={{0,2},{2,4},{4,6},{6,8},{8,10},{10,12},{12,14},{14,16},{16,18},{18... | collective-permute-start | bytes 589832 | tf_op jit(solution)/shard_map/ppermute | solution.py:27
  494.6 53.7 %collective-permute-start.5 = (bf16[2,1,64,768]{3,2,1,0:T(8,128)(2,1)}, bf16[2,1,64,768]{3,2,1,0:T(8,128)(2,1)}, u32[]{:S(2)}, u32[]{:S(2)}) collective-permute-start(bf16[2,1,64,768]{3,2,1,0:T(8,128)(2,1)} %get-tuple-element.376), channel_id=1, source_target_pairs={{2,0},{4,2},{6,4},{8,6},{10,8},{12,10},{14,12},{16,14},{18,16},{20... | collective-permute-start | bytes 589832 | tf_op jit(solution)/shard_map/ppermute | solution.py:30
  601.7 138.1 %collective-permute-start.12 = (bf16[2,1,64,768]{3,2,1,0:T(8,128)(2,1)}, bf16[2,1,64,768]{3,2,1,0:T(8,128)(2,1)}, u32[]{:S(2)}, u32[]{:S(2)}) collective-permute-start(bf16[2,1,64,768]{3,2,1,0:T(8,128)(2,1)} %get-tuple-element.373), channel_id=1, source_target_pairs={{0,2},{2,4},{4,6},{6,8},{8,10},{10,12},{12,14},{14,16},{16,18},{18... | collective-permute-start | bytes 589832 | tf_op jit(solution)/shard_map/ppermute | solution.py:27
  605.3 134.6 %collective-permute-start.13 = (bf16[2,1,64,768]{3,2,1,0:T(8,128)(2,1)}, bf16[2,1,64,768]{3,2,1,0:T(8,128)(2,1)}, u32[]{:S(2)}, u32[]{:S(2)}) collective-permute-start(bf16[2,1,64,768]{3,2,1,0:T(8,128)(2,1)} %get-tuple-element.374), channel_id=1, source_target_pairs={{2,0},{4,2},{6,4},{8,6},{10,8},{12,10},{14,12},{16,14},{18,16},{20... | collective-permute-start | bytes 589832 | tf_op jit(solution)/shard_map/ppermute | solution.py:30
  988.5 54.2 %collective-permute-start.27 = (bf16[2,1,64,768]{3,0,2,1:T(2,128)(2,1)}, bf16[2,1,64,768]{3,0,2,1:T(2,128)(2,1)}, u32[]{:S(2)}, u32[]{:S(2)}) collective-permute-start(bf16[2,1,64,768]{3,0,2,1:T(2,128)(2,1)} %get-tuple-element.350), channel_id=1, source_target_pairs={{0,2},{2,4},{4,6},{6,8},{8,10},{10,12},{12,14},{14,16},{16,18},{18... | collective-permute-start | bytes 589832 | tf_op jit(solution)/shard_map/ppermute | solution.py:19
  1140.9 57.4 %collective-permute-start.20 = (bf16[2,1,64,768]{3,2,1,0:T(8,128)(2,1)}, bf16[2,1,64,768]{3,2,1,0:T(8,128)(2,1)}, u32[]{:S(2)}, u32[]{:S(2)}) collective-permute-start(bf16[2,1,64,768]{3,2,1,0:T(8,128)(2,1)} %get-tuple-element.381), channel_id=1, source_target_pairs={{2,0},{4,2},{6,4},{8,6},{10,8},{12,10},{14,12},{16,14},{18,16},{20... | collective-permute-start | bytes 589832 | tf_op jit(solution)/shard_map/ppermute | solution.py:19
  1142.2 56.2 %collective-permute-start.21 = (bf16[2,1,64,768]{3,2,1,0:T(8,128)(2,1)}, bf16[2,1,64,768]{3,2,1,0:T(8,128)(2,1)}, u32[]{:S(2)}, u32[]{:S(2)}) collective-permute-start(bf16[2,1,64,768]{3,2,1,0:T(8,128)(2,1)} %get-tuple-element.382), channel_id=1, source_target_pairs={{0,2},{2,4},{4,6},{6,8},{8,10},{10,12},{12,14},{14,16},{16,18},{18... | collective-permute-start | bytes 589832 | tf_op jit(solution)/shard_map/ppermute | solution.py:19
  1318.3 264.4 %reduce-scatter.43.cloned.1.call-start = ((), (), s32[]{:S(2)}) async-start(), calls=%async_computation.31 | async-start | bytes 2433024
  1322.0 364.8 %reduce-scatter.51.cloned.1.call-start = ((), (), s32[]{:S(2)}) async-start(), calls=%async_computation.35 | async-start | bytes 2433024
  1326.3 463.6 %reduce-scatter.47.cloned.1.call-start = ((), (), s32[]{:S(2)}) async-start(), calls=%async_computation.33 | async-start | bytes 2433024
  1330.6 563.5 %reduce-scatter.41.cloned.1.call-start = ((), (), s32[]{:S(2)}) async-start(), calls=%async_computation.30 | async-start | bytes 2433024
  1337.2 660.0 %reduce-scatter.31.cloned.1.call-start = ((), (), s32[]{:S(2)}) async-start(), calls=%async_computation.13 | async-start | bytes 2433024 | tf_op jit(solution)/shard_map/reduce_scatter | solution.py:90
  1341.6 759.7 %reduce-scatter.29.cloned.1.call-start = ((), (), s32[]{:S(2)}) async-start(), calls=%async_computation.12 | async-start | bytes 2433024 | tf_op jit(solution)/shard_map/reduce_scatter | solution.py:90
  1346.1 858.4 %reduce-scatter.49.cloned.1.call-start = ((), (), s32[]{:S(2)}) async-start(), calls=%async_computation.34 | async-start | bytes 2433024
  1355.0 953.6 %reduce-scatter.45.cloned.1.call-start = ((), (), s32[]{:S(2)}) async-start(), calls=%async_computation.32 | async-start | bytes 2433024
  1360.8 1088.5 %reduce-scatter.39.cloned.1.call-start = ((), (), s32[]{:S(2)}) async-start(), calls=%async_computation.17 | async-start | bytes 9732096 | tf_op jit(solution)/shard_map/reduce_scatter | solution.py:92
  1369.1 1221.5 %reduce-scatter.37.cloned.1.call-start = ((), (), s32[]{:S(2)}) async-start(), calls=%async_computation.16 | async-start | bytes 9732096 | tf_op jit(solution)/shard_map/reduce_scatter | solution.py:92
  1379.3 1351.7 %reduce-scatter.35.cloned.1.call-start = ((), (), s32[]{:S(2)}) async-start(), calls=%async_computation.15 | async-start | bytes 9732096 | tf_op jit(solution)/shard_map/reduce_scatter | solution.py:91
  1388.6 1483.9 %reduce-scatter.33.cloned.1.call-start = ((), (), s32[]{:S(2)}) async-start(), calls=%async_computation.14 | async-start | bytes 9732096 | tf_op jit(solution)/shard_map/reduce_scatter | solution.py:91
  (429 other events, 8377.4 us)
Sparse Core Ops, SparseCore 0:
  11.6 56.9 all-gather.46
  72.1 53.9 all-gather.48
  129.6 52.9 all-gather.50
  185.4 53.7 all-gather.52
  242.6 64.5 all-gather.54
  310.5 66.3 all-gather.56
  379.8 53.8 all-gather.58
  436.7 53.0 all-gather.60
  492.7 53.0 all-gather.62
  548.6 53.1 all-gather.64
  605.3 62.4 all-gather.66
  671.2 62.4 all-gather.68
  1318.4 158.4 all-reduce.43
  1482.1 100.6 reduce-scatter.42
  1588.7 98.0 reduce-scatter.50
  1692.0 97.9 reduce-scatter.46
  1795.9 98.0 reduce-scatter.40
  1899.2 97.9 reduce-scatter.30
  2003.3 98.0 reduce-scatter.28
  2106.5 97.9 reduce-scatter.48
  2210.6 97.9 reduce-scatter.44
  2314.5 134.6 reduce-scatter.38
  2456.1 134.5 reduce-scatter.36
  2596.5 134.5 reduce-scatter.34
  2737.9 134.5 reduce-scatter.32
where the time goes:
time: 2900 us; the launch traced here: 2880 us
  waiting for transfers between devices  1630 us (56%)
  blocking collectives  313 us (11%)
  other arithmetic  307 us (11%)
  matrix products  264 us (9%)
  local copies, waits for them, and re-layouts  257 us (9%)
  starting transfers between devices  94.8 us (3%)
    unnamed x32, waiting for transfers between devices  669 us
    reduce_scatter x2, waiting for transfers between devices, reduce_grads(): lax.psum_scatter(grads[4], ('seq', 'batch'), scatter_dimension=0, tiled=T...  280 us
    reduce_scatter x2, waiting for transfers between devices, reduce_grads(): lax.psum_scatter(grads[5], ('seq', 'batch'), scatter_dimension=0, tiled=T...  280 us
    reduce_scatter x2, waiting for transfers between devices, reduce_grads(): lax.psum_scatter(grads[3], ('seq', 'batch'), scatter_dimension=0, tiled=T...  206 us
    scatter-add x20, other arithmetic, layer_backward(): grad_extended = grad_extended.at[:, :, WIN - 2 + offset:WIN - 2 + offset...  150 us
    all_gather x2, blocking collectives, fetch_weights(): lax.all_gather(params[15][layer_index], ('seq', 'batch'), axis=1, tiled=T...  137 us
    all_gather x2, blocking collectives, fetch_weights(): lax.all_gather(params[16][layer_index], ('seq', 'batch'), axis=1, tiled=T...  133 us
    ppermute x24, starting transfers between devices, passed_along(): lax.ppermute(value, axis, [(source, source + steps) for source in range(i...  66.2 us
  transfers between devices with their start and end apart: 57, of which 17 were waited for; matrix products, arithmetic and copies ran while one was open for 16% of the time, Pallas kernels for 0%

commit v1 on v0

v1 whole, which is shorter than its diff:
```python
import functools

import jax
import jax.numpy as jnp
from jax import lax
from jax.experimental import pallas as pl
from jax.experimental.pallas import tpu as pltpu
from jax.sharding import PartitionSpec as P

HEADS = 12
WIN = 64
PWIN = 256
TAPS = 5
REACH = PWIN // 4
QROWS = 128
norm_eps = 1e-05
gelu_coef = 0.7978845608028654
masked_score = -1e30
f32 = jnp.float32
bf16 = jnp.bfloat16
VMEM_LIMIT = 48 * 1024 * 1024


def axis_bits():
    bits = []
    for axis in ("seq", "batch"):
        step = lax.axis_size(axis) // 2
        while step:
            bits.append((axis, step))
            step //= 2
    return bits


def path(name):
    bits = axis_bits()
    core, row = ("seq", 1), ("seq", 2)
    column = [bit for bit in bits if bit[0] == "seq" and bit[1] > 2]
    across = [bit for bit in bits if bit[0] == "batch"]
    order = {
        "y": column + across + [row],
        "x": column + [row] + across,
        "z": across + [row] + column,
        "w": [row] + column + across,
    }[name]
    return order + [core]


def exchange(value, axis, step):
    pairs = [(i, i ^ step) for i in range(lax.axis_size(axis))]
    return lax.ppermute(value, axis, pairs)


def block_order():
    bits = axis_bits()
    return [("seq", 1), ("seq", 2)] + [b for b in bits if b[0] == "batch"] + [
        b for b in bits if b[0] == "seq" and b[1] > 2
    ]


def flat_index():
    return lax.axis_index("seq") * lax.axis_size("batch") + lax.axis_index("batch")


def relative_blocks():
    spread = []
    for axis, step in block_order():
        spread.append(step * lax.axis_size("batch") if axis == "seq" else step)
    count = len(spread)
    return [
        sum(spread[k] for k in range(count) if place >> (count - 1 - k) & 1)
        for place in range(2**count)
    ]


def tied(values):
    return list(lax.optimization_barrier(tuple(values)))


class Gather:
    def __init__(self, shard, order):
        self.current, self.order = shard, order
        self.have, self.halves, self.flying = [], None, None
        self.parts, self.rows, self.cols = shard.shape

    def ready(self):
        return self.current

    def hold(self, value):
        self.current = value

    def launch(self):
        self.flying = exchange(self.current, *self.order[len(self.have)])

    def land(self):
        stage = self.order[len(self.have)]
        if stage == self.order[-1]:
            self.halves = (self.current, self.flying)
            return
        significance = block_order()
        place = significance.index(stage)
        before = sum(1 for p in self.have if p < place)
        split = (self.parts * 2**before, 1, 2 ** (len(self.have) - before) * self.rows, self.cols)
        self.have.append(place)
        joined = jnp.concatenate([self.current.reshape(split), self.flying.reshape(split)], axis=1)
        self.current = joined.reshape(self.parts, 2 ** len(self.have) * self.rows, self.cols)

    @property
    def left(self):
        return 0 if self.halves is not None else len(self.order) - len(self.have)

    @property
    def done(self):
        return self.halves is not None


class Scatter:
    def __init__(self, halves, order):
        self.keep, self.give = halves
        self.order, self.stage, self.total, self.flying = order, 0, None, None
        self.have = list(range(1, len(order)))
        self.parts, half_rows, self.cols = self.keep.shape
        self.rows = half_rows // 2 ** len(self.have)

    def ready(self):
        return self.give

    def hold(self, value):
        self.give = value

    def launch(self):
        self.flying = exchange(self.give, *self.order[self.stage])

    def land(self):
        total = self.keep.astype(f32) + self.flying.astype(f32)
        self.stage += 1
        if self.stage == len(self.order):
            self.total = total.reshape(self.parts, self.rows, self.cols)
            return
        place = self.have.index(block_order().index(self.order[self.stage]))
        self.have.pop(place)
        left = 2 ** len(self.have) * self.rows
        split = total.astype(bf16).reshape(self.parts * 2**place, 2, left >> place, self.cols)
        self.keep, self.give = [split[:, i].reshape(self.parts, left, self.cols) for i in range(2)]

    @property
    def done(self):
        return self.total is not None


def checkpoint(value, flows, begin=()):
    value, *flying = tied([value] + [flow.flying for flow in flows])
    for flow, arrived in zip(flows, flying):
        flow.flying = arrived
        flow.land()
    going = [flow for flow in flows if not flow.done] + list(begin)
    value, *ready = tied([value] + [flow.ready() for flow in going])
    for flow, part in zip(going, ready):
        flow.hold(part)
        flow.launch()
    return value


def passed_along(value, steps):
    count = lax.axis_size("seq")
    pairs = [(i, i + steps) for i in range(count) if 0 <= i + steps < count]
    return lax.ppermute(value, "seq", pairs)


def pooled_hops(size):
    return -(-REACH // size)


def pooled_rims(pooled):
    size = pooled.shape[1]
    hops = range(1, pooled_hops(size) + 1)
    low = [passed_along(pooled, hop) for hop in reversed(hops)]
    up = [passed_along(pooled, -hop) for hop in hops]
    low = low[0] if len(low) == 1 else jnp.concatenate(low, axis=1)
    up = up[0] if len(up) == 1 else jnp.concatenate(up, axis=1)
    return low[:, low.shape[1] - REACH :], up[:, :REACH]


def rims_return(rim_low, rim_up, pooled_own):
    size = pooled_own.shape[2]
    hops = pooled_hops(size)
    far_low, far_up = rim_low[:, :, WIN:], rim_up[:, :, WIN:]
    for hop in range(2, hops + 1):
        start = REACH - hop * size
        pooled_own = pooled_own + passed_along(far_low[:, :, start : start + size], -hop).astype(f32)
        start = (hop - 1) * size
        pooled_own = pooled_own + passed_along(far_up[:, :, start : start + size], hop).astype(f32)
    if hops > 1:
        near_low, near_up = rim_low[:, :, :WIN], rim_up[:, :, :WIN]
        rim_low = jnp.concatenate([near_low, far_low[:, :, REACH - size :]], axis=2)
        rim_up = jnp.concatenate([near_up, far_up[:, :, :size]], axis=2)
    return passed_along(rim_up, 1), passed_along(rim_low, -1), pooled_own


def dot_nt(a, b):
    return lax.dot_general(a, b, (((1,), (1,)), ((), ())), preferred_element_type=f32)


def dot_nn(a, b):
    return lax.dot_general(a, b, (((1,), (0,)), ((), ())), preferred_element_type=f32)


def flipped(block):
    return jnp.transpose(block.astype(f32)).astype(bf16)


def two_heads(rows):
    lane = lax.broadcasted_iota(jnp.int32, rows.shape, 1)
    none = jnp.zeros_like(rows)
    half = rows.shape[1] // 2
    return jnp.concatenate(
        [jnp.where(lane < half, rows, none), jnp.where(lane < half, none, rows)], axis=0
    )


def heads_apart(block):
    half, queries = block.shape[0] // 2, block.shape[1] // 2
    return jnp.transpose(
        jnp.concatenate([block[:half, :queries], block[half:, queries:]], axis=0)
    )


def attend_kernel(near_ref, far_ref, q_ref, k_ref, v_ref, kl_ref, vl_ref, ku_ref, vu_ref,
                  pk_ref, pv_ref, pkl_ref, pvl_ref, pku_ref, pvu_ref, mixed_ref, stat_ref):
    blocks = q_ref.shape[1] // QROWS
    pairs = q_ref.shape[2] // 128
    for pair in range(pairs):
        at = slice(128 * pair, 128 * pair + 128)
        keys = jnp.concatenate([kl_ref[0, :, at], k_ref[0, :, at], ku_ref[0, :, at]], axis=0)
        values = jnp.concatenate([vl_ref[0, :, at], v_ref[0, :, at], vu_ref[0, :, at]], axis=0)
        far_keys = jnp.concatenate([pkl_ref[0, :, at], pk_ref[0, :, at], pku_ref[0, :, at]], axis=0)
        far_values = jnp.concatenate(
            [pvl_ref[0, :, at], pv_ref[0, :, at], pvu_ref[0, :, at]], axis=0
        )
        values_t, far_values_t = flipped(values), flipped(far_values)
        for block in range(blocks):
            first = QROWS * block
            query = two_heads(q_ref[0, first : first + QROWS, at] * 0.125)
            stop = first + QROWS + 2 * WIN
            score = dot_nt(keys[first:stop], query) + near_ref[block]
            top = jnp.max(score, axis=0, keepdims=True)
            prob = jnp.exp(score - top)
            total = jnp.sum(prob, axis=0, keepdims=True)
            near_low = (prob * (1.0 / total)).astype(bf16)
            row = (pair * blocks + block) * 2
            stat_ref[0, 0, row : row + 1, :] = top + jnp.log(total)
            score = dot_nt(far_keys, query) + far_ref[block]
            top = jnp.max(score, axis=0, keepdims=True)
            prob = jnp.exp(score - top)
            total = jnp.sum(prob, axis=0, keepdims=True)
            far_low = (prob * (1.0 / total)).astype(bf16)
            stat_ref[0, 0, row + 1 : row + 2, :] = top + jnp.log(total)
            mixed = dot_nn(values_t[:, first:stop], near_low) + dot_nn(far_values_t, far_low)
            mixed_ref[0, first : first + QROWS, at] = heads_apart(mixed).astype(bf16)


def attend_back_kernel(near_ref, far_ref, stat_ref, g_ref, q_ref, k_ref, v_ref, kl_ref, vl_ref,
                       ku_ref, vu_ref, pk_ref, pv_ref, pkl_ref, pvl_ref, pku_ref, pvu_ref,
                       dq_ref, own_ref, pool_ref, low_ref, up_ref):
    blocks = q_ref.shape[1] // QROWS
    pairs = q_ref.shape[2] // 128
    length = q_ref.shape[1]
    for pair in range(pairs):
        at = slice(128 * pair, 128 * pair + 128)
        keys = jnp.concatenate([kl_ref[0, :, at], k_ref[0, :, at], ku_ref[0, :, at]], axis=0)
        values = jnp.concatenate([vl_ref[0, :, at], v_ref[0, :, at], vu_ref[0, :, at]], axis=0)
        far_keys = jnp.concatenate([pkl_ref[0, :, at], pk_ref[0, :, at], pku_ref[0, :, at]], axis=0)
        far_values = jnp.concatenate(
            [pvl_ref[0, :, at], pv_ref[0, :, at], pvu_ref[0, :, at]], axis=0
        )
        keys_t, far_keys_t = flipped(keys), flipped(far_keys)
        near_parts = ([], [])
        far_totals = [None, None]
        for block in range(blocks):
            first = QROWS * block
            query = two_heads(q_ref[0, first : first + QROWS, at] * 0.125)
            grads = two_heads(g_ref[0, first : first + QROWS, at])
            stop = first + QROWS + 2 * WIN
            row = (pair * blocks + block) * 2
            prob = jnp.exp(
                dot_nt(keys[first:stop], query) + near_ref[block] - stat_ref[0, 0, row : row + 1, :]
            )
            grad_prob = dot_nt(values[first:stop], grads)
            inner = jnp.sum(prob * grad_prob, axis=0, keepdims=True)
            grad_score = (prob * (grad_prob - inner)).astype(bf16)
            near_parts[0].append(dot_nn(grad_score, query))
            near_parts[1].append(dot_nn(prob.astype(bf16), grads))
            grad_query = dot_nn(keys_t[:, first:stop], grad_score)
            prob = jnp.exp(
                dot_nt(far_keys, query) + far_ref[block] - stat_ref[0, 0, row + 1 : row + 2, :]
            )
            grad_prob = dot_nt(far_values, grads)
            inner = jnp.sum(prob * grad_prob, axis=0, keepdims=True)
            grad_score = (prob * (grad_prob - inner)).astype(bf16)
            parts = (dot_nn(grad_score, query), dot_nn(prob.astype(bf16), grads))
            grad_query = grad_query + dot_nn(far_keys_t, grad_score)
            dq_ref[0, first : first + QROWS, at] = (heads_apart(grad_query) * 0.125).astype(bf16)
            for kind in range(2):
                far_totals[kind] = parts[kind] if block == 0 else far_totals[kind] + parts[kind]
        for kind in range(2):
            rows = []
            for chunk in range(blocks + 1):
                terms = []
                if chunk < blocks:
                    terms.append(near_parts[kind][chunk][:QROWS])
                if chunk > 0:
                    terms.append(near_parts[kind][chunk - 1][QROWS:])
                rows.append(functools.reduce(jnp.add, terms))
            rows = jnp.concatenate(rows, axis=0)
            own_ref[kind, 0, :, at] = rows[WIN : WIN + length]
            low_ref[kind, 0, :WIN, at] = rows[:WIN].astype(bf16)
            up_ref[kind, 0, :WIN, at] = rows[WIN + length :].astype(bf16)
            far = far_totals[kind]
            pool_ref[kind, 0, :, at] = far[REACH : far.shape[0] - REACH]
            low_ref[kind, 0, WIN:, at] = far[:REACH].astype(bf16)
            up_ref[kind, 0, WIN:, at] = far[far.shape[0] - REACH :].astype(bf16)


LANES = 256


def attend_specs(length, width):
    groups = width // LANES
    pooled = length // 4

    def spec(rows, shift):
        return pl.BlockSpec((1, rows, LANES), lambda g, j: (g, 0, j + shift))

    def whole(count, rows):
        return pl.BlockSpec((count, rows, 2 * QROWS), lambda g, j: (0, 0, 0))

    blocks = length // QROWS
    masks = [whole(blocks, QROWS + 2 * WIN), whole(blocks, pooled + 2 * REACH)]
    stat_rows = LANES // 128 * blocks * 2
    stat = pl.BlockSpec((1, 1, stat_rows, 2 * QROWS), lambda g, j: (g, j, 0, 0))
    operands = [spec(length, 0), spec(length, groups), spec(length, 2 * groups)]
    operands += [spec(WIN, 0), spec(WIN, groups)] * 2
    operands += [spec(pooled, 0), spec(pooled, groups)]
    operands += [spec(REACH, 0), spec(REACH, groups)] * 2
    return groups, masks, stat, stat_rows, operands, spec


def attend_operands(qkv, rows_low, rows_up, pooled, pooled_low, pooled_up):
    return (
        qkv, qkv, qkv, rows_low, rows_low, rows_up, rows_up,
        pooled, pooled, pooled_low, pooled_low, pooled_up, pooled_up,
    )


def attend(masks, operands, width):
    qkv = operands[0]
    count, length = qkv.shape[:2]
    groups, mask_specs, stat, stat_rows, specs, spec = attend_specs(length, width)
    return pl.pallas_call(
        attend_kernel,
        grid=(count, groups),
        in_specs=mask_specs + specs,
        out_specs=[spec(length, 0), stat],
        out_shape=[
            jax.ShapeDtypeStruct((count, length, width), bf16),
            jax.ShapeDtypeStruct((count, groups, stat_rows, 2 * QROWS), f32),
        ],
        compiler_params=pltpu.CompilerParams(vmem_limit_bytes=VMEM_LIMIT),
        cost_estimate=pl.CostEstimate(
            flops=count * length * width * 2000, bytes_accessed=8000000, transcendentals=3000000
        ),
        name="attend",
    )(*masks, *operands)


def attend_back(masks, stats, grad_mixed, operands):
    count, length, width = grad_mixed.shape
    groups, mask_specs, stat, stat_rows, specs, spec = attend_specs(length, width)
    pooled = length // 4

    def pair_spec(rows):
        return pl.BlockSpec((2, 1, rows, LANES), lambda g, j: (0, g, 0, j))

    return pl.pallas_call(
        attend_back_kernel,
        grid=(count, groups),
        in_specs=mask_specs + [stat, spec(length, 0)] + specs,
        out_specs=[
            spec(length, 0), pair_spec(length), pair_spec(pooled),
            pair_spec(WIN + REACH), pair_spec(WIN + REACH),
        ],
        out_shape=[
            jax.ShapeDtypeStruct((count, length, width), bf16),
            jax.ShapeDtypeStruct((2, count, length, width), f32),
            jax.ShapeDtypeStruct((2, count, pooled, width), f32),
            jax.ShapeDtypeStruct((2, count, WIN + REACH, width), bf16),
            jax.ShapeDtypeStruct((2, count, WIN + REACH, width), bf16),
        ],
        compiler_params=pltpu.CompilerParams(vmem_limit_bytes=VMEM_LIMIT),
        cost_estimate=pl.CostEstimate(
            flops=count * length * width * 5000, bytes_accessed=12000000, transcendentals=3000000
        ),
        name="attend_back",
    )(*masks, stats, grad_mixed, *operands)


def window_masks(length):
    blocks = length // QROWS
    index, devices = lax.axis_index("seq"), lax.axis_size("seq")

    def bias(width, offset, scale, reach):
        key = lax.broadcasted_iota(jnp.int32, (blocks, width, QROWS), 1)
        query = lax.broadcasted_iota(jnp.int32, (blocks, width, QROWS), 2)
        block = lax.broadcasted_iota(jnp.int32, (blocks, width, QROWS), 0)
        key = key - offset + (block * QROWS if scale == 1 else 0)
        query = query + block * QROWS
        size = length // scale
        allowed = jnp.abs(query - scale * key) <= reach
        place = key + index * size
        allowed &= (place >= 0) & (place < size * devices)
        one = jnp.where(allowed, 0.0, masked_score).astype(f32)
        return jnp.concatenate([one, one], axis=2)

    return bias(QROWS + 2 * WIN, WIN, 1, WIN), bias(length // 4 + 2 * REACH, REACH, 4, PWIN)


def tap_select(length):
    pooled = length // 4
    row = jnp.arange(TAPS * pooled, dtype=jnp.int32)
    column = jnp.arange(length, dtype=jnp.int32)
    source = 4 * (row % pooled) + row // pooled - 2
    return (source[:, None] == column[None, :]).astype(bf16)


def pool_kernel(select_ref, kernel_ref, rows_ref, low_ref, pooled_ref):
    pooled = pooled_ref.shape[1]
    for group in range(rows_ref.shape[0]):
        taps = dot_nn(select_ref[...], rows_ref[group])
        total = kernel_ref[0, 0:1, :] * taps[:pooled]
        for tap in range(1, TAPS):
            total = total + kernel_ref[0, tap : tap + 1, :] * taps[tap * pooled : (tap + 1) * pooled]
        low = low_ref[group].astype(f32)
        edge = kernel_ref[0, 0:1, :] * low[14:15] + kernel_ref[0, 1:2, :] * low[15:16]
        row = lax.broadcasted_iota(jnp.int32, total.shape, 0)
        pooled_ref[group] = (total + jnp.where(row == 0, edge, 0.0)).astype(bf16)


def pool(select, kernel, qkv, rows_low, width):
    count, length = qkv.shape[:2]
    groups = width // LANES
    return pl.pallas_call(
        pool_kernel,
        grid=(2 * groups,),
        in_specs=[
            pl.BlockSpec(select.shape, lambda j: (0, 0)),
            pl.BlockSpec((1, 8, LANES), lambda j: (j // groups, 0, j % groups)),
            pl.BlockSpec((count, length, LANES), lambda j: (0, 0, j + groups)),
            pl.BlockSpec((count, 16, LANES), lambda j: (0, WIN // 16 - 1, j)),
        ],
        out_specs=pl.BlockSpec((count, length // 4, LANES), lambda j: (0, 0, j)),
        out_shape=jax.ShapeDtypeStruct((count, length // 4, 2 * width), bf16),
        compiler_params=pltpu.CompilerParams(vmem_limit_bytes=VMEM_LIMIT),
        cost_estimate=pl.CostEstimate(
            flops=count * length * width * 1300, bytes_accessed=2500000, transcendentals=0
        ),
        name="pool",
    )(select, kernel, qkv, rows_low)


def pool_back_kernel(select_ref, spread_ref, kernel_ref, rows_ref, low_rows_ref, own_ref, pool_ref,
                     low_ref, up_ref, grad_ref, tail_ref, taps_ref):
    pooled = pool_ref.shape[2]
    length = rows_ref.shape[1]
    tap_row = lax.broadcasted_iota(jnp.int32, (8, LANES), 0)
    tail_row = lax.broadcasted_iota(jnp.int32, (16, LANES), 0)
    taps_total = jnp.zeros((8, LANES), f32)
    for group in range(rows_ref.shape[0]):
        grads = pool_ref[0, group] + low_ref[0, group, WIN:].astype(f32)
        grads = (grads + up_ref[0, group, WIN:].astype(f32)).astype(bf16).astype(f32)
        taps = dot_nn(select_ref[...], rows_ref[group])
        low_rows = low_rows_ref[group].astype(f32)
        edge = grads[0:1]
        spread = []
        for tap in range(TAPS):
            line = jnp.sum(grads * taps[tap * pooled : (tap + 1) * pooled], axis=0, keepdims=True)
            if tap < 2:
                line = line + edge * low_rows[14 + tap : 15 + tap]
            taps_total = taps_total + jnp.where(tap_row == tap, line, 0.0)
            spread.append(grads * kernel_ref[0, tap : tap + 1, :])
        spread = jnp.concatenate(spread, axis=0)
        high = spread.astype(bf16)
        rest = (spread - high.astype(f32)).astype(bf16)
        total = own_ref[0, group] + dot_nn(spread_ref[...], high) + dot_nn(spread_ref[...], rest)
        grad_ref[0, group] = total
        grad_ref[0, group, :WIN] = total[:WIN] + low_ref[0, group, :WIN].astype(f32)
        grad_ref[0, group, length - WIN :] = total[length - WIN :] + up_ref[0, group, :WIN].astype(f32)
        tail = jnp.where(tail_row == 14, edge * kernel_ref[0, 0:1, :], 0.0)
        tail = tail + jnp.where(tail_row == 15, edge * kernel_ref[0, 1:2, :], 0.0)
        tail_ref[0, group] = tail.astype(bf16)
    taps_ref[0] = taps_total


def pool_back(select, kernel, qkv, rows_low, own, pooled_own, from_low, from_up):
    count, length, width = own.shape[1:]
    groups = width // LANES
    pooled = length // 4

    def pair_spec(rows):
        return pl.BlockSpec((1, count, rows, LANES), lambda j: (j // groups, 0, 0, j % groups))

    return pl.pallas_call(
        pool_back_kernel,
        grid=(2 * groups,),
        in_specs=[
            pl.BlockSpec(select.shape, lambda j: (0, 0)),
            pl.BlockSpec(select.shape[::-1], lambda j: (0, 0)),
            pl.BlockSpec((1, 8, LANES), lambda j: (j // groups, 0, j % groups)),
            pl.BlockSpec((count, length, LANES), lambda j: (0, 0, j + groups)),
            pl.BlockSpec((count, 16, LANES), lambda j: (0, WIN // 16 - 1, j)),
            pair_spec(length), pair_spec(pooled),
            pair_spec(from_low.shape[2]), pair_spec(from_up.shape[2]),
        ],
        out_specs=[
            pair_spec(length), pair_spec(16),
            pl.BlockSpec((1, 8, LANES), lambda j: (j // groups, 0, j % groups)),
        ],
        out_shape=[
            jax.ShapeDtypeStruct((2, count, length, width), f32),
            jax.ShapeDtypeStruct((2, count, 16, width), bf16),
            jax.ShapeDtypeStruct((2, 8, width), f32),
        ],
        compiler_params=pltpu.CompilerParams(vmem_limit_bytes=VMEM_LIMIT),
        cost_estimate=pl.CostEstimate(
            flops=count * length * width * 4000, bytes_accessed=9000000, transcendentals=0
        ),
        name="pool_back",
    )(select, select.T, kernel, qkv, rows_low, own, pooled_own, from_low, from_up)


def matmul(a, b):
    return jnp.dot(a, b, preferred_element_type=f32)


def matmul_t(a, b):
    return lax.dot_general(a, b, (((1,), (1,)), ((), ())), preferred_element_type=f32)


def weight_grad(a, b):
    return lax.dot_general(a, b, (((0,), (0,)), ((), ())), preferred_element_type=f32)


def normalised(rows):
    centre = rows - jnp.mean(rows, axis=-1, keepdims=True)
    inverse = lax.rsqrt(jnp.mean(centre * centre, axis=-1, keepdims=True) + norm_eps)
    return centre * inverse, inverse


def normalised_back(grads, gain, norm, inverse):
    scaled = grads * gain
    mean = jnp.mean(scaled, axis=-1, keepdims=True)
    inner = jnp.mean(scaled * norm, axis=-1, keepdims=True)
    return (scaled - mean - norm * inner) * inverse


def gelu_both(value):
    inside = jnp.tanh(gelu_coef * (value + 0.044715 * value * value * value))
    act = 0.5 * value * (1.0 + inside)
    slope = 0.5 * (1.0 + inside) + 0.5 * value * (1.0 - inside * inside) * gelu_coef * (
        1.0 + 3 * 0.044715 * value * value
    )
    return act, slope


def small_index():
    return flat_index().reshape(1).astype(jnp.int32)


def place_kernel(blocks, index_ref, mine_ref, other_ref, out_ref):
    half = len(blocks) // 2
    for place, bits in enumerate(blocks):
        source = mine_ref if place < half else other_ref
        out_ref[0, index_ref[0] ^ bits] = source[0, place % half]


def in_place(halves, block_cols, skip=0, take=None):
    blocks = relative_blocks()
    half = len(blocks) // 2
    all_parts, half_rows, cols = halves[0].shape
    parts = take or all_parts
    rows = half_rows // half
    spec = pl.BlockSpec((1, half, rows, block_cols), lambda p, j, index: (p + skip, 0, 0, j))
    whole = pl.pallas_call(
        functools.partial(place_kernel, blocks),
        grid_spec=pltpu.PrefetchScalarGridSpec(
            num_scalar_prefetch=1,
            grid=(parts, cols // block_cols),
            in_specs=[spec, spec],
            out_specs=pl.BlockSpec(
                (1, 2 * half, rows, block_cols), lambda p, j, index: (p, 0, 0, j)
            ),
        ),
        out_shape=jax.ShapeDtypeStruct((parts, 2 * half, rows, cols), halves[0].dtype),
        compiler_params=pltpu.CompilerParams(vmem_limit_bytes=VMEM_LIMIT),
        cost_estimate=pl.CostEstimate(
            flops=0, bytes_accessed=8 * parts * half_rows * cols, transcendentals=0
        ),
        name="in_place",
    )(small_index(), *[h.reshape(all_parts, half, rows, cols) for h in halves])
    return whole.reshape(parts * 2 * half_rows, cols)


def store_blocks(blocks, index, total_ref, keep_ref, give_ref):
    half = len(blocks) // 2
    rows = total_ref.shape[0] // len(blocks)
    for place, bits in enumerate(blocks):
        target = keep_ref if place < half else give_ref
        start = pl.multiple_of((index ^ bits) * rows, 8)
        target[0, place % half] = total_ref[pl.ds(start, rows), :].astype(bf16)


def weight_grads_kernel(blocks, plan, index_ref, *refs):
    operands, (keep_ref, give_ref, total_ref) = refs[:-3], refs[-3:]
    width = total_ref.shape[0]
    for step, (left, left_at, right, right_at) in enumerate(plan):

        @pl.when(pl.program_id(0) == step)
        def _():
            rows = operands[left][:, left_at * width : (left_at + 1) * width]
            grads = operands[right][:, right_at * width : (right_at + 1) * width]
            total_ref[...] = weight_grad(rows, grads)

    store_blocks(blocks, index_ref[0], total_ref, keep_ref, give_ref)


def turned(whole):
    bits = axis_bits()
    cols = whole.shape[1]
    split = whole.reshape((2,) * len(bits) + (-1, cols))
    for place, (axis, step) in enumerate(bits):
        mine = (lax.axis_index(axis) // step) % 2
        split = jnp.where(mine == 1, jnp.flip(split, place), split)
    order = [bits.index(bit) for bit in block_order()]
    split = split.transpose(*order, len(bits), len(bits) + 1)
    return split.reshape(1, 2, -1, cols)


def weight_grads(operands, plan, width, stacked=False):
    blocks = relative_blocks()
    half = len(blocks) // 2
    rows = width // len(blocks)
    count = len(plan)
    if rows % 8:
        pieces = []
        for left, left_at, right, right_at in plan:
            left_rows = operands[left][:, left_at * width : (left_at + 1) * width]
            grads = operands[right][:, right_at * width : (right_at + 1) * width]
            pieces.append(turned(weight_grad(left_rows, grads).astype(bf16)))
        joined = jnp.concatenate(pieces, axis=0 if stacked else 3)
        return joined[:, 0], joined[:, 1]
    if stacked:
        shape, spec = (count, half, rows, width), lambda j, index: (j, 0, 0, 0)
    else:
        shape, spec = (1, half, rows, count * width), lambda j, index: (0, 0, 0, j)
    out = jax.ShapeDtypeStruct(shape, bf16)
    spec = pl.BlockSpec((1, half, rows, width), spec)
    tokens = operands[0].shape[0]
    pair = pl.pallas_call(
        functools.partial(weight_grads_kernel, blocks, plan),
        grid_spec=pltpu.PrefetchScalarGridSpec(
            num_scalar_prefetch=1,
            grid=(count,),
            in_specs=[pl.BlockSpec(a.shape, lambda j, index: (0, 0)) for a in operands],
            out_specs=[spec, spec],
            scratch_shapes=[pltpu.VMEM((width, width), f32)],
        ),
        out_shape=[out, out],
        compiler_params=pltpu.CompilerParams(vmem_limit_bytes=VMEM_LIMIT),
        cost_estimate=pl.CostEstimate(
            flops=2 * tokens * width * width * count,
            bytes_accessed=2 * sum(a.size for a in operands) + 2 * count * width * width,
            transcendentals=0,
        ),
        name="weight_grads",
    )(small_index(), *operands)
    return [side.reshape(shape[0], half * rows, shape[3]) for side in pair]


def units_back_kernel(spread_ref, *refs):
    parts, out_ref = refs[:-1], refs[-1]
    total = None
    for part, rows_ref in enumerate(parts):
        left = rows_ref[...]
        for _ in range(3):
            piece = left.astype(bf16)
            left = left - piece.astype(f32)
            term = dot_nn(piece, spread_ref[part])
            total = term if total is None else total + term
    out_ref[...] = total


def units_back(rows, ratio, shard_rows):
    count, cols = rows.shape
    block = cols // ratio // 2
    source = jnp.arange(block, dtype=jnp.int32)
    target = jnp.arange(ratio * block, dtype=jnp.int32)
    device, rest = target // (ratio * shard_rows), target % (ratio * shard_rows)
    wanted = device * shard_rows + rest % shard_rows
    spread = jnp.stack([
        (source[:, None] == wanted[None, :]) & (rest[None, :] // shard_rows == part)
        for part in range(ratio)
    ]).astype(bf16)
    return pl.pallas_call(
        units_back_kernel,
        grid=(2,),
        in_specs=[pl.BlockSpec(spread.shape, lambda j: (0, 0, 0))] + [
            pl.BlockSpec((count, block), functools.partial(lambda part, j: (0, 2 * part + j), part))
            for part in range(ratio)
        ],
        out_specs=pl.BlockSpec((count, ratio * block), lambda j: (0, j)),
        out_shape=jax.ShapeDtypeStruct((count, cols), f32),
        compiler_params=pltpu.CompilerParams(vmem_limit_bytes=VMEM_LIMIT),
        name="units_back",
    )(spread, *[rows] * ratio)


SMALL_COLUMNS = 128


def small_grads_kernel(blocks, layers, index_ref, *refs):
    sources, (keep_ref, give_ref, lines_ref, columns_ref) = refs[:-4], refs[-4:]
    lines_ref[...] = jnp.zeros_like(lines_ref)
    width = lines_ref.shape[1]
    each = len(sources) // layers
    at = 0
    for layer in range(layers):
        *vectors, up_ref, taps_ref = sources[layer * each : (layer + 1) * each]
        for vector in vectors:
            lines_ref[at : at + 1, :] = vector[...]
            at += 1
        for kind in range(2):
            lines_ref[at : at + TAPS, :] = taps_ref[kind, :TAPS]
            at += TAPS
        for part in range(up_ref.shape[1] // width):
            lines_ref[at : at + 1, :] = up_ref[:, part * width : (part + 1) * width]
            at += 1
    columns_ref[...] = jnp.transpose(lines_ref[...])
    store_blocks(blocks, index_ref[0], columns_ref, keep_ref, give_ref)


def small_grads(per_layer, width):
    blocks = relative_blocks()
    half = len(blocks) // 2
    rows = width // len(blocks)
    if rows % 8:
        lines = []
        for *vectors, up, taps in per_layer:
            lines += vectors + [taps[0, :TAPS], taps[1, :TAPS], up.reshape(-1, width)]
        lines = jnp.concatenate(lines, axis=0)
        lines = jnp.pad(lines, ((0, SMALL_COLUMNS - lines.shape[0]), (0, 0))).T.astype(bf16)
        lines = turned(lines)
        return lines[:, 0], lines[:, 1]
    flat = [a for arrays in per_layer for a in arrays]
    out = jax.ShapeDtypeStruct((1, half, rows, SMALL_COLUMNS), bf16)
    pair = pl.pallas_call(
        functools.partial(small_grads_kernel, blocks, len(per_layer)),
        in_specs=[pl.BlockSpec(memory_space=pltpu.SMEM)]
        + [pl.BlockSpec(memory_space=pltpu.VMEM)] * len(flat),
        out_specs=[pl.BlockSpec(memory_space=pltpu.VMEM)] * 2,
        out_shape=[out, out],
        scratch_shapes=[pltpu.VMEM((SMALL_COLUMNS, width), f32), pltpu.VMEM((width, SMALL_COLUMNS), f32)],
        compiler_params=pltpu.CompilerParams(vmem_limit_bytes=VMEM_LIMIT),
        name="small_grads",
    )(small_index(), *flat)
    return [side.reshape(1, half * rows, SMALL_COLUMNS) for side in pair]


def layer_forward(x, weights, masks, select, count, at):
    qkv_weight, late_weights, small = weights
    width = x.shape[1]
    length = x.shape[0] // count
    x_low = x.astype(bf16)
    bias = jnp.concatenate([small["query_bias"], jnp.zeros((width,), f32), small["value_bias"]])
    qkv = matmul(x_low, qkv_weight)
    qkv = at("projected", (qkv + bias).astype(bf16).reshape(count, length, -1))
    rows_low = passed_along(qkv[:, length - WIN :, width:], 1)
    rows_up = passed_along(qkv[:, :WIN, width:], -1)
    pooled = at("pooled", pool(select, small["taps"], qkv, rows_low, width))
    pooled_low, pooled_up = pooled_rims(pooled)
    pooled_up = at("attending", pooled_up)
    operands = attend_operands(qkv, rows_low, rows_up, pooled, pooled_low, pooled_up)
    mixed, stats = attend(masks, operands, width)
    mixed = at("attended", mixed.reshape(count * length, width))
    out_weight, up_weight, down_weight = late_weights()
    norm, inverse = normalised(x + matmul(mixed, out_weight) + small["output_bias"])
    hidden = norm * small["mixer_gain"] + small["mixer_shift"]
    hidden = at("mixed", hidden)
    hidden_low = hidden.astype(bf16)
    act, slope = gelu_both(matmul(hidden_low, up_weight) + small["up_bias"])
    act_low, slope = act.astype(bf16), slope.astype(bf16)
    norm_two, inverse_two = normalised(hidden + matmul(act_low, down_weight) + small["down_bias"])
    y = at("fed", norm_two * small["feed_gain"] + small["feed_shift"])
    kept = (x_low, operands, stats, mixed, norm, inverse, hidden_low, act_low, slope,
            norm_two, inverse_two)
    return y, kept, (qkv_weight, out_weight, up_weight, down_weight, small)


def layer_backward(grads, kept, weights, masks, select, count, at):
    qkv_weight, out_weight, up_weight, down_weight, small = weights
    (x_low, operands, stats, mixed, norm, inverse, hidden_low, act_low, slope,
     norm_two, inverse_two) = kept
    rows, width = grads.shape
    length = rows // count
    ratio = act_low.shape[1] // width

    def total(value):
        return jnp.sum(value.astype(f32), axis=0, keepdims=True)

    feed_gain, feed_shift = total(grads * norm_two), total(grads)
    grad_two = normalised_back(grads, small["feed_gain"], norm_two, inverse_two)
    feed_low = grad_two.astype(bf16)
    feed_low = at("down", feed_low, (act_low, feed_low))
    grad_pre = (slope.astype(f32) * matmul_t(feed_low, down_weight)).astype(bf16)
    grad_pre = at("up", grad_pre, (hidden_low, grad_pre))
    grad_hidden = grad_two + matmul_t(grad_pre, up_weight)
    mixer_gain, mixer_shift = total(grad_hidden * norm), total(grad_hidden)
    grad_one = normalised_back(grad_hidden, small["mixer_gain"], norm, inverse)
    attention_low = grad_one.astype(bf16)
    grad_mixed = matmul_t(attention_low, out_weight).astype(bf16).reshape(count, length, width)
    grad_mixed = at("attending", grad_mixed)
    grad_query, own, pooled_own, rim_low, rim_up = attend_back(masks, stats, grad_mixed, operands)
    grad_query = grad_query.reshape(rows, width)
    from_low, from_up, pooled_own = rims_return(rim_low, rim_up, pooled_own)
    pooled_own = at("attended", pooled_own, (x_low, grad_query, mixed, attention_low))
    own, tail, taps = pool_back(
        select, small["taps"], operands[0], operands[3], own, pooled_own, from_low, from_up
    )
    tail = passed_along(tail, -1).astype(f32)
    own = at("pooled", own)
    own = own + jnp.pad(tail, ((0, 0), (0, 0), (length - 16, 0), (0, 0)))
    own = own.astype(bf16).reshape(2, rows, width)
    grad_qkv = (grad_query, own[0], own[1])
    grad_x = grad_one + matmul_t(jnp.concatenate(grad_qkv, axis=1), qkv_weight)
    small_sums = [
        total(grad_query), total(own[1]), total(attention_low), total(feed_low),
        mixer_gain, mixer_shift, feed_gain, feed_shift, total(grad_pre), taps,
    ]
    return grad_x, (x_low, *grad_qkv, mixed, attention_low), small_sums


def pack_small(vectors, up_biases, taps):
    columns = []
    for layer in range(vectors[0].shape[0]):
        rows = vectors[0].shape[1]
        columns.append(jnp.stack([v[layer] for v in vectors]))
        columns.append(taps[0][layer])
        columns.append(taps[1][layer])
        columns.append(up_biases[layer].reshape(-1, rows))
    packed = jnp.concatenate(columns, axis=0)
    return jnp.pad(packed, ((0, SMALL_COLUMNS - packed.shape[0]), (0, 0))).T


def unpack_small(columns, layers, ratio):
    width = columns.shape[0]
    lines = columns.astype(f32).T
    per_layer = 8 + 2 * TAPS + ratio
    pad = ((0, 8 - TAPS), (0, 0))
    result = []
    for layer in range(layers):
        piece = lines[layer * per_layer : (layer + 1) * per_layer]
        result.append({
            "query_bias": piece[0],
            "value_bias": piece[1],
            "output_bias": piece[2],
            "down_bias": piece[3],
            "mixer_gain": piece[4],
            "mixer_shift": piece[5],
            "feed_gain": piece[6],
            "feed_shift": piece[7],
            "taps": jnp.stack([
                jnp.pad(piece[8 : 8 + TAPS], pad), jnp.pad(piece[8 + TAPS : 8 + 2 * TAPS], pad),
            ]),
            "up_bias": piece[8 + 2 * TAPS :].reshape(ratio * width),
        })
    return result


def on_device(
    tokens, cotangent, masked, query_weight, key_weight, value_weight, output_weight, up_weight,
    down_weight, query_bias, value_bias, output_bias, up_bias, down_bias, mixer_gain, mixer_shift,
    feed_gain, feed_shift, pool_key, pool_value,
):
    micro, seqs, length, width = tokens.shape
    count = micro * seqs
    layers = query_weight.shape[0]
    devices = lax.axis_size("seq") * lax.axis_size("batch")
    shard_rows = width // devices
    small_shard = pack_small(
        (query_bias, value_bias, output_bias, down_bias, mixer_gain, mixer_shift, feed_gain,
         feed_shift), up_bias, (pool_key, pool_value),
    )
    masks = window_masks(length)
    select = tap_select(length)
    ratio = up_weight.shape[2] // width

    def units_apart(rows):
        split = rows.reshape(rows.shape[0], devices, ratio, shard_rows)
        return split.transpose(0, 2, 1, 3).reshape(rows.shape)

    up_shards = [units_apart(up_weight[layer]) for layer in range(layers)]
    down_shards = [down_weight[layer].reshape(ratio, shard_rows, width) for layer in range(layers)]
    shard = jnp.concatenate(
        [query_weight[0], key_weight[0], value_weight[0], small_shard], axis=1
    )
    first = Gather(shard[None], path("y"))

    later = [
        Gather(jnp.concatenate(
            [query_weight[layer], key_weight[layer], value_weight[layer]], axis=1
        )[None], path("z"))
        for layer in range(1, layers)
    ]
    x = tokens.reshape(count * length, width).astype(f32)
    feeds = []
    for layer in range(layers):
        shard = jnp.concatenate(
            [output_weight[layer], up_shards[layer], *down_shards[layer]], axis=1
        )
        feeds.append(lax.all_gather(shard, ("seq", "batch"), axis=0, tiled=True))
    x = checkpoint(x, [], [first])
    while first.left > 1:
        x = checkpoint(x, [first])
    x = checkpoint(x, [first], later)
    first_whole = in_place(first.halves, first.cols)
    smalls = unpack_small(first_whole[:, 3 * width :], layers, ratio)

    def late_weights(layer):
        whole = feeds[layer]
        down_whole = whole[:, (1 + ratio) * width :].reshape(width, ratio, width)
        return (
            whole[:, :width], whole[:, width : (1 + ratio) * width],
            down_whole.transpose(1, 0, 2).reshape(-1, width),
        )

    def landed(value, flows, left):
        while True:
            behind = [flow for flow in flows if flow.left > left]
            if not behind:
                return value
            value = checkpoint(value, behind)

    def forward_at(layer):
        following = later[layer : layer + 1]

        def at(name, value):
            if name in ("projected", "pooled", "attended"):
                return checkpoint(value, following)
            if name == "fed":
                return landed(value, following, 0)
            return value

        return at

    states, weights = [], []
    for layer in range(layers):
        if layer == 0:
            qkv_weight = first_whole[:, : 3 * width]
        else:
            qkv_weight = in_place(later[layer - 1].halves, width)
        late = functools.partial(late_weights, layer)
        x, kept, whole = layer_forward(
            x, (qkv_weight, late, smalls[layer]), masks, select, count, forward_at(layer)
        )
        states.append(kept)
        weights.append(whole)
    layer_output = x.astype(bf16).reshape(tokens.shape)
    grads = cotangent.astype(f32) * masked.astype(f32)[..., None]
    grads = grads.reshape(count * length, width)
    flows = {}
    plans = {
        "down": ["up", "attended", "pooled", "end", "next down", "never"],
        "up": ["attending", "pooled", "end", "next up", "next attending", "never"],
        "in": ["next down", "next attended", "next pooled", "never"],
        "query": ["pooled", "never"],
    }

    def due(layer, name):
        result = []
        for (kind, owner), flow in flows.items():
            when = plans[kind][min(flow.stage, len(plans[kind]) - 1)]
            if not flow.done and when == ("next " if owner > layer else "") + name:
                result.append(flow)
            elif not flow.done and owner > layer + 1:
                result.append(flow)
        return result

    def backward_at(layer):
        def at(name, value, given=None):
            landing, begin = due(layer, name), []
            if name == "down":
                plan = [(0, part, 1, 0) for part in range(ratio)]
                flow = Scatter(weight_grads(given, plan, width, stacked=True), path("y")[::-1])
                flows[name, layer] = flow
                begin.append(flow)
            if name == "up":
                plan = [(0, 0, 1, part) for part in range(ratio)]
                flow = Scatter(weight_grads(given, plan, width), path("x")[::-1])
                flows[name, layer] = flow
                begin.append(flow)
            if name == "attended" and layer == 0:
                plan = [(0, 0, 1, 0), (2, 0, 3, 0)]
                flow = Scatter(weight_grads(given, plan, width), path("z")[::-1])
                flows["query", layer] = flow
                begin.append(flow)
            return checkpoint(value, landing, begin)

        return at

    small_sums = [None] * layers
    for layer in reversed(range(layers)):
        grads, given, small_sums[layer] = layer_backward(
            grads, states[layer], weights[layer], masks, select, count, backward_at(layer)
        )
        if layer > 0:
            plan = [(0, 0, 1 + i, 0) for i in range(3)] + [(4, 0, 5, 0)]
            flow = Scatter(weight_grads(given, plan, width), path("z")[::-1])
            flows["in", layer] = flow
            grads = checkpoint(grads, due(layer, "end"), [flow])
    halves = weight_grads((given[0], *given[2:4]), [(0, 0, 1, 0), (0, 0, 2, 0)], width)
    sides = small_grads(small_sums, width)
    joined = [jnp.concatenate(parts, axis=2) for parts in zip(halves, sides)]
    last = Scatter(joined, path("y")[::-1])
    flows["last", 0] = last
    marker = checkpoint(last.keep[:1, :1, :1], [], [last])
    while True:
        flying = [flow for flow in flows.values() if not flow.done]
        if not flying:
            break
        marker = checkpoint(marker, flying)
    totals = []
    for layer in range(layers):
        if layer > 0:
            whole = flows["in", layer].total[0]
            parts = [whole[:, i * width : (i + 1) * width] for i in range(4)]
        else:
            whole = flows["query", 0].total[0]
            end = last.total[0]
            parts = [whole[:, :width], end[:, :width], end[:, width : 2 * width], whole[:, width:]]
        parts.append(flows["up", layer].total[0])
        parts.append(flows["down", layer].total.reshape(ratio * shard_rows, width))
        totals.append(parts)
    up_totals = units_back(
        jnp.concatenate([parts[4] for parts in totals]), ratio, shard_rows
    ).reshape(layers, shard_rows, ratio * width)
    input_grad = grads.astype(bf16).reshape(tokens.shape)
    lines = last.total[0, :, 2 * width :].T
    per_layer = 8 + 2 * TAPS + ratio
    lines = lines[: layers * per_layer].reshape(layers, per_layer, shard_rows)
    vectors = [lines[:, i] for i in range(8)]
    after = 8 + 2 * TAPS
    grad_up_bias = lines[:, after:].reshape(layers, -1)
    return (
        layer_output, input_grad,
        *[jnp.stack([t[i] for t in totals]) if i != 4 else up_totals for i in range(6)],
        vectors[0], vectors[1], vectors[2], grad_up_bias, *vectors[3:],
        lines[:, 8 : 8 + TAPS], lines[:, 8 + TAPS : after],
    )


def solution(mesh):
    rows = P(None, "batch", "seq", None)
    matrix = P(None, ("seq", "batch"), None)
    vector = P(None, ("seq", "batch"))
    taps = P(None, None, ("seq", "batch"))
    params = (matrix,) * 6 + (vector,) * 9 + (taps,) * 2
    return jax.shard_map(
        on_device,
        mesh=mesh,
        in_specs=(rows, rows, P(None, "batch", "seq")) + params,
        out_specs=(rows, rows) + params,
        check_vma=False,
    )
```

time: 2900 us -> 639 us (0.22)
  waiting for transfers between devices: 1630 us -> 197 us
  blocking collectives: 313 us -> 0 us
  other arithmetic: 307 us -> 60.1 us
  local copies, waits for them, and re-layouts: 257 us -> 61.3 us
  matrix products: 264 us -> 69 us
  Pallas kernels: 0 us -> 126 us
    reduce_scatter x6 -> x0, waiting for transfers between devices: 766 us -> none  [the longest x2 280 us: reduce_grads(): lax.psum_scatter(grads[4], ('seq', 'batch'), scatter_dimension=0, tiled=T...]
    unnamed x32 -> x2, waiting for transfers between devices: 669 us -> 0.68 us
    all_gather x4 -> x0, blocking collectives: 270 us -> none  [the longest x2 137 us: fetch_weights(): lax.all_gather(params[15][layer_index], ('seq', 'batch'), axis=1, tiled=T...]
    dot_general x120 -> x16, matrix products: 264 us -> 69 us  [the longest x8 40.3 us: matmul_t(): lax.dot_general(a, b, (((1,), (1,)), ((), ())), preferred_element_type=f32)]
    ppermute x32 -> x59, waiting for transfers between devices: 0.08 us -> 190 us  [the longest x45 183 us: exchange(): return lax.ppermute(value, axis, pairs)]
    all_gather x12 -> x2, waiting for transfers between devices: 191 us -> 6.15 us  [on_device(): feeds.append(lax.all_gather(shard, ('seq', 'batch'), axis=0, tiled=True))]
    scatter-add x28 -> x0, other arithmetic: 163 us -> none  [the longest x20 150 us: layer_backward(): grad_extended = grad_extended.at[:, :, WIN - 2 + offset:WIN - 2 + offset...]
    pallas_call x0 -> x19, Pallas kernels: none -> 126 us  [the longest x2 38.6 us: attend_back(): pl.pallas_call(attend_back_kernel, grid=(count, groups), in_specs=mask_sp...]
  transfers between devices with their start and end apart: 57 -> 61, of which waited for: 17 -> 28; matrix products, arithmetic and copies ran while one was open for 16% -> 19% of each run, Pallas kernels for 0% -> 16%
where the time goes in v1:
time: 639 us; the launch traced here: 630 us
  waiting for transfers between devices  197 us (31%)
  Pallas kernels  126 us (20%)
  starting transfers between devices  100 us (16%)
  matrix products  69 us (11%)
  local copies, waits for them, and re-layouts  61.3 us (10%)
  other arithmetic  60.1 us (9%)
  between operations  16.9 us (3%)
    ppermute x45, waiting for transfers between devices, exchange(): return lax.ppermute(value, axis, pairs)  183 us
    ppermute x45, starting transfers between devices, exchange(): return lax.ppermute(value, axis, pairs)  66.1 us
    dot_general x8, matrix products, matmul_t(): lax.dot_general(a, b, (((1,), (1,)), ((), ())), preferred_element_type=f32)  40.3 us
    pallas_call x2, Pallas kernels, attend_back(): pl.pallas_call(attend_back_kernel, grid=(count, groups), in_specs=mask_sp...  38.6 us
    pallas_call x7, Pallas kernels, weight_grads(): pl.pallas_call(functools.partial(weight_grads_kernel, blocks, plan), grid...  33.9 us
    ppermute x14, starting transfers between devices, passed_along(): return lax.ppermute(value, 'seq', pairs)  33.8 us
    dot_general x8, matrix products, matmul(): return jnp.dot(a, b, preferred_element_type=f32)  28.6 us
    convert_element_type x28, other arithmetic, land(): total.astype(bf16)  25 us
  transfers between devices with their start and end apart: 61, of which 28 were waited for; matrix products, arithmetic and copies ran while one was open for 19% of the time, Pallas kernels for 16%

profile of v1, /device:TPU:0, one launch (start us, length us, event | category | flops | bytes accessed | tf_op | source)
XLA Modules:
  0.0 630.1 jit_solution(11980863665923908448)
XLA Ops:
  22.5 5.7 collective-permute-done
  29.0 12.3 %collective-permute-done.1 = bf16[1,48,2432]{2,1,0:T(8,128)(2,1)S(1)} collective-permute-done((bf16[1,48,2432]{2,1,0:T(8,128)(2,1)S(1)}, bf16[1,48,2432]{2,1,0:T(8,128)(2,1)S(1)}, u32[]{:S(2)}, u32[]{:S(2)}) %collective-permute-start.1) | collective-permute-done | bytes 233504 | tf_op jit(solution)/shard_map/ppermute | solution.py:50
  42.8 15.6 %collective-permute-done.2 = bf16[1,96,2432]{2,1,0:T(8,128)(2,1)S(1)} collective-permute-done((bf16[1,96,2432]{2,1,0:T(8,128)(2,1)S(1)}, bf16[1,96,2432]{2,1,0:T(8,128)(2,1)S(1)}, u32[]{:S(2)}, u32[]{:S(2)}) %collective-permute-start.2) | collective-permute-done | bytes 466976 | tf_op jit(solution)/shard_map/ppermute | solution.py:50
  60.0 17.6 %collective-permute-done.3 = bf16[1,192,2432]{2,1,0:T(8,128)(2,1)S(1)} collective-permute-done((bf16[1,192,2432]{2,1,0:T(8,128)(2,1)S(1)}, bf16[1,192,2432]{2,1,0:T(8,128)(2,1)S(1)}, u32[]{:S(2)}, u32[]{:S(2)}) %collective-permute-start.3) | collective-permute-done | bytes 933920 | tf_op jit(solution)/shard_map/ppermute | solution.py:50
  108.1 10.0 %collective-permute-start.9 = (bf16[2,64,1536]{2,1,0:T(8,128)(2,1)}, bf16[2,64,1536]{2,1,0:T(8,128)(2,1)}, u32[]{:S(2)}, u32[]{:S(2)}) collective-permute-start(bf16[2,64,1536]{2,1,0:T(8,128)(2,1)} %pool.2.pk_ref.pv_ref), channel_id=1, source_target_pairs={{0,2},{2,4},{4,6},{6,8},{8,10},{10,12},{12,14},{14,16},{16,18},{18... | collective-permute-start | bytes 1179656 | tf_op jit(solution)/shard_map/ppermute | solution.py:166
  119.6 8.7 %collective-permute-start.11 = (bf16[1,96,2304]{2,1,0:T(8,128)(2,1)}, bf16[1,96,2304]{2,1,0:T(8,128)(2,1)}, u32[]{:S(2)}, u32[]{:S(2)}) collective-permute-start(bf16[1,96,2304]{2,1,0:T(8,128)(2,1)} %bitcast.39), channel_id=1, source_target_pairs={{0,16},{2,18},{4,20},{6,22},{8,24},{10,26},{12,28},{14,30},{16,0},... | collective-permute-start | bytes 1327112 | tf_op jit(solution)/shard_map/ppermute | solution.py:50
  130.8 11.1 %attend.2 = (bf16[2,256,768]{2,1,0:T(8,128)(2,1)S(1)}, f32[2,3,8,256]{3,2,1,0:T(8,128)S(1)}) custom-call(f32[2,256,256]{2,1,0:T(8,128)S(1)} %pad_maximum_fusion.7.near_ref, f32[2,192,256]{2,1,0:T(8,128)S(1)} %copy-done.6, bf16[2,256,2304]{2,1,0:T(8,128)(2,1)S(1)} %bitcast.442, bf16[2,256,2304]{2,1,0:T(8,128)(2,1)S(1)} %bitcast.443, ...), custom_call_target="tpu_custom_call" | custom-call | flops 786432000 | bytes 8000000 | tf_op jit(solution)/shard_map/attend/pallas_call | solution.py:358
  141.9 17.5 %collective-permute-done.11 = bf16[1,96,2304]{2,1,0:T(8,128)(2,1)} collective-permute-done((bf16[1,96,2304]{2,1,0:T(8,128)(2,1)}, bf16[1,96,2304]{2,1,0:T(8,128)(2,1)}, u32[]{:S(2)}, u32[]{:S(2)}) %collective-permute-start.11) | collective-permute-done | bytes 442400 | tf_op jit(solution)/shard_map/ppermute | solution.py:50
  180.1 10.6 %collective-permute-done.12 = bf16[1,192,2304]{2,1,0:T(8,128)(2,1)S(1)} collective-permute-done((bf16[1,192,2304]{2,1,0:T(8,128)(2,1)S(1)}, bf16[1,192,2304]{2,1,0:T(8,128)(2,1)S(1)}, u32[]{:S(2)}, u32[]{:S(2)}) %collective-permute-start.12) | collective-permute-done | bytes 884768 | tf_op jit(solution)/shard_map/ppermute | solution.py:50
  222.5 6.1 all-gather.5.cloned.1.call-done
  233.5 11.3 %attend.3 = (bf16[2,256,768]{2,1,0:T(8,128)(2,1)S(1)}, f32[2,3,8,256]{3,2,1,0:T(8,128)S(1)}) custom-call(f32[2,256,256]{2,1,0:T(8,128)S(1)} %copy-done.5, f32[2,192,256]{2,1,0:T(8,128)S(1)} %copy-done.7, bf16[2,256,2304]{2,1,0:T(8,128)(2,1)S(1)} %bitcast.451, bf16[2,256,2304]{2,1,0:T(8,128)(2,1)S(1)} %bitcast.452, bf16[2,256,2304]{2,1,0:T(8,128)(2,1)S(1)} %bitcast.453, ...), custom_call_target="tpu_custom_call" | custom-call | flops 786432000 | bytes 8000000 | tf_op jit(solution)/shard_map/attend/pallas_call | solution.py:358
  261.6 6.0 weight_grads.7
  268.0 8.9 %multiply_convert_fusion.1.refs_1_ = bf16[512,3072]{1,0:T(8,128)(2,1)} fusion(bf16[512,768]{1,0:T(8,128)(2,1)S(1)} %get-tuple-element.226.refs_1_, bf16[3072,768]{1,0:T(8,128)(2,1)S(1)} %bitcast.524, f32[512,3072]{1,0:T(8,128)} %get-tuple-element.597, f32[3072]{0:T(1024)S(1)} %copy-done.91), kind=kOutput, calls=%fused_computation.20 | convolution fusion | flops 2450522112 | bytes 14954496 | tf_op jit(solution)/shard_map/dot_general | solution.py:544
  276.8 6.1 weight_grads.8
  288.1 6.6 %multiply_reduce_fusion = (f32[768]{0:T(1024)S(1)}, f32[512]{0:T(512)S(1)}, f32[512]{0:T(512)S(1)}, f32[768]{0:T(1024)S(1)}, f32[512,768]{1,0:T(8,128)}) fusion(f32[512,768]{1,0:T(8,128)S(1)} %get-tuple-element.595, f32[512]{0:T(512)S(1)} %add_rsqrt_fusion.1, f32[512]{0:T(512)S(1)} %broadcast_multiply_fusion.8, f32[768]{0:T(1024)S(1)} %copy-done.77, ...), kind=kOutput, calls=%fused_computation.86 | convolution fusion | flops 2419848704 | bytes 12600320 | tf_op jit(solution)/shard_map/dot_general | solution.py:544
  302.6 19.4 %attend_back.2 = (bf16[2,256,768]{2,1,0:T(8,128)(2,1)S(1)}, f32[2,2,256,768]{3,2,1,0:T(8,128)}, f32[2,2,64,768]{3,2,1,0:T(8,128)S(1)}, bf16[2,2,128,768]{3,2,1,0:T(8,128)(2,1)S(1)}, bf16[2,2,128,768]{3,2,1,0:T(8,128)(2,1)S(1)}) custom-call(f32[2,256,256]{2,1,0:T(8,128)S(1)} %copy-done.5, f32[2,192,256]{2,1,0:T(8,128)S(1)} %copy-done.7, ...), custom_call_target="tpu_custom_call" | custom-call | flops 1966080000 | bytes 12000000 | tf_op jit(solution)/shard_map/attend_back/pallas_call | solution.py:383
  329.3 6.8 %pool_back.2 = (f32[2,2,256,768]{3,2,1,0:T(8,128)}, bf16[2,2,16,768]{3,2,1,0:T(8,128)(2,1)S(1)}, f32[2,8,768]{2,1,0:T(8,128)S(1)}) custom-call(bf16[320,256]{1,0:T(8,128)(2,1)S(1)} %copy-done.10, bf16[256,320]{1,0:T(8,128)(2,1)S(1)} %fusion.86.spread_ref, f32[2,8,768]{2,1,0:T(8,128)S(1)} %copy-done.20, bf16[2,256,2304]{2,1,0:T(8,128)(2,1)S(1)} %bitcast.457, ...), custom_call_target="tpu_custom_call" | custom-call | flops 1572864000 | bytes 9000000 | tf_op jit(solution)/shard_map/pool_back/pallas_call | solution.py:510
  345.8 6.5 %collective-permute-done.25 = bf16[2,2,16,768]{3,2,1,0:T(8,128)(2,1)S(1)} collective-permute-done((bf16[2,2,16,768]{3,2,1,0:T(8,128)(2,1)S(1)}, bf16[2,2,16,768]{3,2,1,0:T(8,128)(2,1)S(1)}, u32[]{:S(2)}, u32[]{:S(2)}) %collective-permute-start.25) | collective-permute-done | bytes 98336 | tf_op jit(solution)/shard_map/ppermute | solution.py:166
  369.0 6.8 %collective-permute-done.27 = bf16[1,96,3072]{2,1,0:T(8,128)(2,1)S(1)} collective-permute-done((bf16[1,96,3072]{2,1,0:T(8,128)(2,1)}, bf16[1,96,3072]{2,1,0:T(8,128)(2,1)S(1)}, u32[]{:S(2)}, u32[]{:S(2)}) %collective-permute-start.27) | collective-permute-done | bytes 589856 | tf_op jit(solution)/shard_map/ppermute | solution.py:50
  382.6 6.0 weight_grads.10
  394.9 9.7 %multiply_convert_fusion.refs_1_ = bf16[512,3072]{1,0:T(8,128)(2,1)} fusion(bf16[512,768]{1,0:T(8,128)(2,1)S(1)} %get-tuple-element.269.refs_1_, bf16[3072,768]{1,0:T(8,128)(2,1)} %bitcast.518, f32[512,3072]{1,0:T(8,128)} %get-tuple-element.591, f32[3072]{0:T(1024)S(1)} %copy-done.90), kind=kOutput, calls=%fused_computation.19 | convolution fusion | flops 2450522112 | bytes 14954496 | tf_op jit(solution)/shard_map/dot_general | solution.py:544
  404.6 6.3 weight_grads.11
  419.5 6.7 %multiply_reduce_fusion.2 = (f32[768]{0:T(1024)S(1)}, f32[512]{0:T(512)S(1)}, f32[512]{0:T(512)S(1)}, f32[768]{0:T(1024)S(1)}, f32[512,768]{1,0:T(8,128)}) fusion(f32[512,768]{1,0:T(8,128)S(1)} %copy-done.32, f32[512]{0:T(512)S(1)} %copy-done.83, f32[512]{0:T(512)S(1)} %copy-done.79, f32[768]{0:T(1024)S(1)} %get-tuple-element.470, ...), kind=kOutput, calls=%fused_computation.92 | convolution fusion | flops 2419848704 | bytes 12600320 | tf_op jit(solution)/shard_map/dot_general | solution.py:544
  431.0 15.4 %collective-permute-done.32 = bf16[1,24,3072]{2,1,0:T(8,128)(2,1)S(1)} collective-permute-done((bf16[1,24,3072]{2,1,0:T(8,128)(2,1)S(1)}, bf16[1,24,3072]{2,1,0:T(8,128)(2,1)S(1)}, u32[]{:S(2)}, u32[]{:S(2)}) %collective-permute-start.32) | collective-permute-done | bytes 147488 | tf_op jit(solution)/shard_map/ppermute | solution.py:50
  450.6 19.3 %attend_back.3 = (bf16[2,256,768]{2,1,0:T(8,128)(2,1)S(1)}, f32[2,2,256,768]{3,2,1,0:T(8,128)}, f32[2,2,64,768]{3,2,1,0:T(8,128)S(1)}, bf16[2,2,128,768]{3,2,1,0:T(8,128)(2,1)S(1)}, bf16[2,2,128,768]{3,2,1,0:T(8,128)(2,1)S(1)}) custom-call(f32[2,256,256]{2,1,0:T(8,128)S(1)} %copy-done.5, f32[2,192,256]{2,1,0:T(8,128)S(1)} %copy-done.7, ...), custom_call_target="tpu_custom_call" | custom-call | flops 1966080000 | bytes 12000000 | tf_op jit(solution)/shard_map/attend_back/pallas_call | solution.py:383
  488.2 5.8 collective-permute-start.38
  496.2 6.8 %pool_back.3 = (f32[2,2,256,768]{3,2,1,0:T(8,128)}, bf16[2,2,16,768]{3,2,1,0:T(8,128)(2,1)S(1)}, f32[2,8,768]{2,1,0:T(8,128)S(1)}) custom-call(bf16[320,256]{1,0:T(8,128)(2,1)S(1)} %copy-done.10, bf16[256,320]{1,0:T(8,128)(2,1)S(1)} %fusion.86.spread_ref, f32[2,8,768]{2,1,0:T(8,128)S(1)} %copy-done.18, bf16[2,256,2304]{2,1,0:T(8,128)(2,1)S(1)} %bitcast.448, ...), custom_call_target="tpu_custom_call" | custom-call | flops 1572864000 | bytes 9000000 | tf_op jit(solution)/shard_map/pool_back/pallas_call | solution.py:510
  504.5 23.1 %collective-permute-done.38 = bf16[1,96,3072]{2,1,0:T(8,128)(2,1)S(1)} collective-permute-done((bf16[1,96,3072]{2,1,0:T(8,128)(2,1)}, bf16[1,96,3072]{2,1,0:T(8,128)(2,1)S(1)}, u32[]{:S(2)}, u32[]{:S(2)}) %collective-permute-start.38) | collective-permute-done | bytes 589856 | tf_op jit(solution)/shard_map/ppermute | solution.py:50
  544.5 5.8 collective-permute-done.43
  552.1 9.7 %collective-permute-done.45 = bf16[1,96,3072]{2,1,0:T(8,128)(2,1)S(1)} collective-permute-done((bf16[1,96,3072]{2,1,0:T(8,128)(2,1)S(1)}, bf16[1,96,3072]{2,1,0:T(8,128)(2,1)S(1)}, u32[]{:S(2)}, u32[]{:S(2)}) %collective-permute-start.45) | collective-permute-done | bytes 589856 | tf_op jit(solution)/shard_map/ppermute | solution.py:50
  576.4 6.2 collective-permute-done.50
  601.9 5.9 units_back.1
  (614 shorter events, 293.0 us)
Async XLA Ops:
  7.2 153.7 %all-gather.3.cloned.1.call-start = ((), (), s32[]{:S(2)}) async-start(), calls=%async_computation | async-start | bytes 10948608 | tf_op jit(solution)/shard_map/all_gather | solution.py:927
  15.4 213.3 %all-gather.5.cloned.1.call-start = ((), (), s32[]{:S(2)}) async-start(), calls=%async_computation.1 | async-start | bytes 10948608 | tf_op jit(solution)/shard_map/all_gather | solution.py:927
  41.3 17.1 %collective-permute-start.2 = (bf16[1,96,2432]{2,1,0:T(8,128)(2,1)S(1)}, bf16[1,96,2432]{2,1,0:T(8,128)(2,1)S(1)}, u32[]{:S(2)}, u32[]{:S(2)}) collective-permute-start(bf16[1,96,2432]{2,1,0:T(8,128)(2,1)S(1)} %bitcast.550), channel_id=1, source_target_pairs={{0,1},{1,0},{2,3},{3,2},{4,5},{5,4},{6,7},{7,6},{8,9},{9,8},{10,11... | collective-permute-start | bytes 1400840 | tf_op jit(solution)/shard_map/ppermute | solution.py:50
  58.5 19.2 %collective-permute-start.3 = (bf16[1,192,2432]{2,1,0:T(8,128)(2,1)S(1)}, bf16[1,192,2432]{2,1,0:T(8,128)(2,1)S(1)}, u32[]{:S(2)}, u32[]{:S(2)}) collective-permute-start(bf16[1,192,2432]{2,1,0:T(8,128)(2,1)S(1)} %bitcast.531), channel_id=1, source_target_pairs={{0,4},{2,6},{4,0},{6,2},{8,12},{10,14},{12,8},{14,10},{16,20},{18,... | collective-permute-start | bytes 2801672 | tf_op jit(solution)/shard_map/ppermute | solution.py:50
  101.5 28.2 %collective-permute-start.7 = (bf16[2,64,1536]{2,1,0:T(8,128)(2,1)}, bf16[2,64,1536]{2,1,0:T(8,128)(2,1)}, u32[]{:S(2)}, u32[]{:S(2)}) collective-permute-start(bf16[2,64,1536]{2,1,0:T(8,128)(2,1)} %get-tuple-element.494), channel_id=1, source_target_pairs={{2,0},{4,2},{6,4},{8,6},{10,8},{12,10},{14,12},{16,14},{18,16},{20... | collective-permute-start | bytes 1179656 | tf_op jit(solution)/shard_map/ppermute | solution.py:166
  108.1 21.7 %collective-permute-start.9 = (bf16[2,64,1536]{2,1,0:T(8,128)(2,1)}, bf16[2,64,1536]{2,1,0:T(8,128)(2,1)}, u32[]{:S(2)}, u32[]{:S(2)}) collective-permute-start(bf16[2,64,1536]{2,1,0:T(8,128)(2,1)} %pool.2.pk_ref.pv_ref), channel_id=1, source_target_pairs={{0,2},{2,4},{4,6},{6,8},{8,10},{10,12},{12,14},{14,16},{16,18},{18... | collective-permute-start | bytes 1179656 | tf_op jit(solution)/shard_map/ppermute | solution.py:166
  119.6 39.8 %collective-permute-start.11 = (bf16[1,96,2304]{2,1,0:T(8,128)(2,1)}, bf16[1,96,2304]{2,1,0:T(8,128)(2,1)}, u32[]{:S(2)}, u32[]{:S(2)}) collective-permute-start(bf16[1,96,2304]{2,1,0:T(8,128)(2,1)} %bitcast.39), channel_id=1, source_target_pairs={{0,16},{2,18},{4,20},{6,22},{8,24},{10,26},{12,28},{14,30},{16,0},... | collective-permute-start | bytes 1327112 | tf_op jit(solution)/shard_map/ppermute | solution.py:50
  160.8 29.9 %collective-permute-start.12 = (bf16[1,192,2304]{2,1,0:T(8,128)(2,1)S(1)}, bf16[1,192,2304]{2,1,0:T(8,128)(2,1)S(1)}, u32[]{:S(2)}, u32[]{:S(2)}) collective-permute-start(bf16[1,192,2304]{2,1,0:T(8,128)(2,1)S(1)} %bitcast.535), channel_id=1, source_target_pairs={{0,8},{2,10},{4,12},{6,14},{8,0},{10,2},{12,4},{14,6},{16,24},{18,... | collective-permute-start | bytes 2654216 | tf_op jit(solution)/shard_map/ppermute | solution.py:50
  208.6 24.9 %collective-permute-start.15 = (bf16[2,64,1536]{2,1,0:T(8,128)(2,1)}, bf16[2,64,1536]{2,1,0:T(8,128)(2,1)}, u32[]{:S(2)}, u32[]{:S(2)}) collective-permute-start(bf16[2,64,1536]{2,1,0:T(8,128)(2,1)} %get-tuple-element.492), channel_id=1, source_target_pairs={{2,0},{4,2},{6,4},{8,6},{10,8},{12,10},{14,12},{16,14},{18,16},{20... | collective-permute-start | bytes 1179656 | tf_op jit(solution)/shard_map/ppermute | solution.py:166
  212.6 20.9 %collective-permute-start.16 = (bf16[2,64,1536]{2,1,0:T(8,128)(2,1)S(1)}, bf16[2,64,1536]{2,1,0:T(8,128)(2,1)}, u32[]{:S(2)}, u32[]{:S(2)}) collective-permute-start(bf16[2,64,1536]{2,1,0:T(8,128)(2,1)S(1)} %pool.3.pk_ref.pv_ref), channel_id=1, source_target_pairs={{0,2},{2,4},{4,6},{6,8},{8,10},{10,12},{12,14},{14,16},{16,18},{18... | collective-permute-start | bytes 1179656 | tf_op jit(solution)/shard_map/ppermute | solution.py:166
  286.7 35.3 %collective-permute-start.20 = (bf16[4,192,768]{2,1,0:T(8,128)(2,1)}, bf16[4,192,768]{2,1,0:T(8,128)(2,1)}, u32[]{:S(2)}, u32[]{:S(2)}) collective-permute-start(bf16[4,192,768]{2,1,0:T(8,128)(2,1)} %slice_bitcast_fusion.3), channel_id=1, source_target_pairs={{0,4},{2,6},{4,0},{6,2},{8,12},{10,14},{12,8},{14,10},{16,20},{18,... | collective-permute-start | bytes 3538952 | tf_op jit(solution)/shard_map/ppermute | solution.py:50
  301.8 40.4 %collective-permute-start.24 = (bf16[1,192,3072]{2,1,0:T(8,128)(2,1)}, bf16[1,192,3072]{2,1,0:T(8,128)(2,1)}, u32[]{:S(2)}, u32[]{:S(2)}) collective-permute-start(bf16[1,192,3072]{2,1,0:T(8,128)(2,1)} %bitcast.82), channel_id=1, source_target_pairs={{0,1},{1,0},{2,3},{3,2},{4,5},{5,4},{6,7},{7,6},{8,9},{9,8},{10,11... | collective-permute-start | bytes 3538952 | tf_op jit(solution)/shard_map/ppermute | solution.py:50
  336.1 16.2 %collective-permute-start.25 = (bf16[2,2,16,768]{3,2,1,0:T(8,128)(2,1)S(1)}, bf16[2,2,16,768]{3,2,1,0:T(8,128)(2,1)S(1)}, u32[]{:S(2)}, u32[]{:S(2)}) collective-permute-start(bf16[2,2,16,768]{3,2,1,0:T(8,128)(2,1)S(1)} %get-tuple-element.255), channel_id=1, source_target_pairs={{2,0},{4,2},{6,4},{8,6},{10,8},{12,10},{14,12},{16,14},{18,16},{20... | collective-permute-start | bytes 294920 | tf_op jit(solution)/shard_map/ppermute | solution.py:166
  352.6 16.4 %collective-permute-start.26 = (bf16[4,48,768]{2,1,0:T(8,128)(2,1)}, bf16[4,48,768]{2,1,0:T(8,128)(2,1)S(1)}, u32[]{:S(2)}, u32[]{:S(2)}) collective-permute-start(bf16[4,48,768]{2,1,0:T(8,128)(2,1)} %bitcast.89), channel_id=1, source_target_pairs={{0,8},{2,10},{4,12},{6,14},{8,0},{10,2},{12,4},{14,6},{16,24},{18,... | collective-permute-start | bytes 884744 | tf_op jit(solution)/shard_map/ppermute | solution.py:50
  357.4 18.4 %collective-permute-start.27 = (bf16[1,96,3072]{2,1,0:T(8,128)(2,1)}, bf16[1,96,3072]{2,1,0:T(8,128)(2,1)S(1)}, u32[]{:S(2)}, u32[]{:S(2)}) collective-permute-start(bf16[1,96,3072]{2,1,0:T(8,128)(2,1)} %slice_bitcast_fusion.11), channel_id=1, source_target_pairs={{0,4},{2,6},{4,0},{6,2},{8,12},{10,14},{12,8},{14,10},{16,20},{18,... | collective-permute-start | bytes 1769480 | tf_op jit(solution)/shard_map/ppermute | solution.py:50
  392.9 17.9 %collective-permute-start.31 = (bf16[4,384,768]{2,1,0:T(8,128)(2,1)S(1)}, bf16[4,384,768]{2,1,0:T(8,128)(2,1)}, u32[]{:S(2)}, u32[]{:S(2)}) collective-permute-start(bf16[4,384,768]{2,1,0:T(8,128)(2,1)S(1)} %bitcast.482), channel_id=1, source_target_pairs={{0,2},{2,0},{4,6},{6,4},{8,10},{10,8},{12,14},{14,12},{16,18},{18,... | collective-permute-start | bytes 7077896 | tf_op jit(solution)/shard_map/ppermute | solution.py:50
  393.2 17.7 %collective-permute-start.30 = (bf16[1,48,3072]{2,1,0:T(8,128)(2,1)}, bf16[1,48,3072]{2,1,0:T(8,128)(2,1)S(1)}, u32[]{:S(2)}, u32[]{:S(2)}) collective-permute-start(bf16[1,48,3072]{2,1,0:T(8,128)(2,1)} %bitcast.100), channel_id=1, source_target_pairs={{0,8},{2,10},{4,12},{6,14},{8,0},{10,2},{12,4},{14,6},{16,24},{18,... | collective-permute-start | bytes 884744 | tf_op jit(solution)/shard_map/ppermute | solution.py:50
  414.5 31.9 %collective-permute-start.33 = (bf16[1,384,3072]{2,1,0:T(8,128)(2,1)S(1)}, bf16[1,384,3072]{2,1,0:T(8,128)(2,1)}, u32[]{:S(2)}, u32[]{:S(2)}) collective-permute-start(bf16[1,384,3072]{2,1,0:T(8,128)(2,1)S(1)} %bitcast.481), channel_id=1, source_target_pairs={{0,2},{2,0},{4,6},{6,4},{8,10},{10,8},{12,14},{14,12},{16,18},{18,... | collective-permute-start | bytes 7077896 | tf_op jit(solution)/shard_map/ppermute | solution.py:50
  416.9 53.0 %collective-permute-start.34 = (bf16[1,192,3072]{2,1,0:T(8,128)(2,1)}, bf16[1,192,3072]{2,1,0:T(8,128)(2,1)}, u32[]{:S(2)}, u32[]{:S(2)}) collective-permute-start(bf16[1,192,3072]{2,1,0:T(8,128)(2,1)} %bitcast.104), channel_id=1, source_target_pairs={{0,8},{2,10},{4,12},{6,14},{8,0},{10,2},{12,4},{14,6},{16,24},{18,... | collective-permute-start | bytes 3538952 | tf_op jit(solution)/shard_map/ppermute | solution.py:50
  417.2 29.2 %collective-permute-start.32 = (bf16[1,24,3072]{2,1,0:T(8,128)(2,1)S(1)}, bf16[1,24,3072]{2,1,0:T(8,128)(2,1)S(1)}, u32[]{:S(2)}, u32[]{:S(2)}) collective-permute-start(bf16[1,24,3072]{2,1,0:T(8,128)(2,1)S(1)} %slice_bitcast_fusion.28), channel_id=1, source_target_pairs={{0,16},{2,18},{4,20},{6,22},{8,24},{10,26},{12,28},{14,30},{16,0},... | collective-permute-start | bytes 442376 | tf_op jit(solution)/shard_map/ppermute | solution.py:50
  418.7 51.2 %collective-permute-start.35 = (bf16[4,192,768]{2,1,0:T(8,128)(2,1)}, bf16[4,192,768]{2,1,0:T(8,128)(2,1)}, u32[]{:S(2)}, u32[]{:S(2)}) collective-permute-start(bf16[4,192,768]{2,1,0:T(8,128)(2,1)} %slice_bitcast_fusion.1), channel_id=1, source_target_pairs={{0,4},{2,6},{4,0},{6,2},{8,12},{10,14},{12,8},{14,10},{16,20},{18,... | collective-permute-start | bytes 3538952 | tf_op jit(solution)/shard_map/ppermute | solution.py:50
  478.5 15.5 %collective-permute-start.36 = (bf16[2,2,128,768]{3,2,1,0:T(8,128)(2,1)S(1)}, bf16[2,2,128,768]{3,2,1,0:T(8,128)(2,1)S(1)}, u32[]{:S(2)}, u32[]{:S(2)}) collective-permute-start(bf16[2,2,128,768]{3,2,1,0:T(8,128)(2,1)S(1)} %get-tuple-element.295), channel_id=1, source_target_pairs={{0,2},{2,4},{4,6},{6,8},{8,10},{10,12},{12,14},{14,16},{16,18},{18... | collective-permute-start | bytes 2359304 | tf_op jit(solution)/shard_map/ppermute | solution.py:166
  481.0 46.6 %collective-permute-start.40 = (bf16[1,192,3072]{2,1,0:T(8,128)(2,1)}, bf16[1,192,3072]{2,1,0:T(8,128)(2,1)}, u32[]{:S(2)}, u32[]{:S(2)}) collective-permute-start(bf16[1,192,3072]{2,1,0:T(8,128)(2,1)} %bitcast.117), channel_id=1, source_target_pairs={{0,1},{1,0},{2,3},{3,2},{4,5},{5,4},{6,7},{7,6},{8,9},{9,8},{10,11... | collective-permute-start | bytes 3538952 | tf_op jit(solution)/shard_map/ppermute | solution.py:50
  483.0 44.6 %collective-permute-start.41 = (bf16[1,384,1536]{2,1,0:T(8,128)(2,1)S(1)}, bf16[1,384,1536]{2,1,0:T(8,128)(2,1)}, u32[]{:S(2)}, u32[]{:S(2)}) collective-permute-start(bf16[1,384,1536]{2,1,0:T(8,128)(2,1)S(1)} %bitcast.485), channel_id=1, source_target_pairs={{0,2},{2,0},{4,6},{6,4},{8,10},{10,8},{12,14},{14,12},{16,18},{18,... | collective-permute-start | bytes 3538952 | tf_op jit(solution)/shard_map/ppermute | solution.py:50
  488.2 39.3 %collective-permute-start.38 = (bf16[1,96,3072]{2,1,0:T(8,128)(2,1)}, bf16[1,96,3072]{2,1,0:T(8,128)(2,1)S(1)}, u32[]{:S(2)}, u32[]{:S(2)}) collective-permute-start(bf16[1,96,3072]{2,1,0:T(8,128)(2,1)} %bitcast.121), channel_id=1, source_target_pairs={{0,16},{2,18},{4,20},{6,22},{8,24},{10,26},{12,28},{14,30},{16,0},... | collective-permute-start | bytes 1769480 | tf_op jit(solution)/shard_map/ppermute | solution.py:50
  494.0 33.5 %collective-permute-start.39 = (bf16[4,96,768]{2,1,0:T(8,128)(2,1)}, bf16[4,96,768]{2,1,0:T(8,128)(2,1)S(1)}, u32[]{:S(2)}, u32[]{:S(2)}) collective-permute-start(bf16[4,96,768]{2,1,0:T(8,128)(2,1)} %slice_bitcast_fusion.9), channel_id=1, source_target_pairs={{0,1},{1,0},{2,3},{3,2},{4,5},{5,4},{6,7},{7,6},{8,9},{9,8},{10,11... | collective-permute-start | bytes 1769480 | tf_op jit(solution)/shard_map/ppermute | solution.py:50
  503.0 31.8 %collective-permute-start.42 = (bf16[2,2,16,768]{3,2,1,0:T(8,128)(2,1)S(1)}, bf16[2,2,16,768]{3,2,1,0:T(8,128)(2,1)S(1)}, u32[]{:S(2)}, u32[]{:S(2)}) collective-permute-start(bf16[2,2,16,768]{3,2,1,0:T(8,128)(2,1)S(1)} %get-tuple-element.309), channel_id=1, source_target_pairs={{2,0},{4,2},{6,4},{8,6},{10,8},{12,10},{14,12},{16,14},{18,16},{20... | collective-permute-start | bytes 294920 | tf_op jit(solution)/shard_map/ppermute | solution.py:166
  538.6 25.9 %collective-permute-start.47 = (bf16[1,384,1664]{2,1,0:T(8,128)(2,1)S(1)}, bf16[1,384,1664]{2,1,0:T(8,128)(2,1)S(1)}, u32[]{:S(2)}, u32[]{:S(2)}) collective-permute-start(bf16[1,384,1664]{2,1,0:T(8,128)(2,1)S(1)} %pad_maximum_fusion.2), channel_id=1, source_target_pairs={{0,2},{2,0},{4,6},{6,4},{8,10},{10,8},{12,14},{14,12},{16,18},{18,... | collective-permute-start | bytes 3833864 | tf_op jit(solution)/shard_map/ppermute | solution.py:50
  544.3 17.6 %collective-permute-start.45 = (bf16[1,96,3072]{2,1,0:T(8,128)(2,1)S(1)}, bf16[1,96,3072]{2,1,0:T(8,128)(2,1)S(1)}, u32[]{:S(2)}, u32[]{:S(2)}) collective-permute-start(bf16[1,96,3072]{2,1,0:T(8,128)(2,1)S(1)} %copy-done.64), channel_id=1, source_target_pairs={{0,4},{2,6},{4,0},{6,2},{8,12},{10,14},{12,8},{14,10},{16,20},{18,... | collective-permute-start | bytes 1769480 | tf_op jit(solution)/shard_map/ppermute | solution.py:50
  544.3 20.1 %collective-permute-start.46 = (bf16[1,192,1536]{2,1,0:T(8,128)(2,1)S(1)}, bf16[1,192,1536]{2,1,0:T(8,128)(2,1)S(1)}, u32[]{:S(2)}, u32[]{:S(2)}) collective-permute-start(bf16[1,192,1536]{2,1,0:T(8,128)(2,1)S(1)} %bitcast.586), channel_id=1, source_target_pairs={{0,8},{2,10},{4,12},{6,14},{8,0},{10,2},{12,4},{14,6},{16,24},{18,... | collective-permute-start | bytes 1769480 | tf_op jit(solution)/shard_map/ppermute | solution.py:50
  568.5 19.3 %collective-permute-start.51 = (bf16[1,96,1536]{2,1,0:T(8,128)(2,1)S(1)}, bf16[1,96,1536]{2,1,0:T(8,128)(2,1)S(1)}, u32[]{:S(2)}, u32[]{:S(2)}) collective-permute-start(bf16[1,96,1536]{2,1,0:T(8,128)(2,1)S(1)} %bitcast.593), channel_id=1, source_target_pairs={{0,16},{2,18},{4,20},{6,22},{8,24},{10,26},{12,28},{14,30},{16,0},... | collective-permute-start | bytes 884744 | tf_op jit(solution)/shard_map/ppermute | solution.py:50
  570.5 17.4 %collective-permute-start.52 = (bf16[1,192,1664]{2,1,0:T(8,128)(2,1)S(1)}, bf16[1,192,1664]{2,1,0:T(8,128)(2,1)S(1)}, u32[]{:S(2)}, u32[]{:S(2)}) collective-permute-start(bf16[1,192,1664]{2,1,0:T(8,128)(2,1)S(1)} %slice_bitcast_fusion.5), channel_id=1, source_target_pairs={{0,4},{2,6},{4,0},{6,2},{8,12},{10,14},{12,8},{14,10},{16,20},{18,... | collective-permute-start | bytes 1916936 | tf_op jit(solution)/shard_map/ppermute | solution.py:50
  (155 other events, 1104.5 us)
Sparse Core Ops, SparseCore 0:
  15.5 99.5 all-gather.2
  118.0 110.6 all-gather.4

commit v2 on v1

--- a/solution.py
+++ b/solution.py
@@ -39,7 +39,7 @@
     order = {
         "y": column + across + [row],
         "x": column + [row] + across,
-        "z": across + [row] + column,
+        "z": column[:-1] + across + [row] + column[-1:],
         "w": [row] + column + across,
     }[name]
     return order + [core]
@@ -131,28 +131,33 @@
         self.flying = exchange(self.give, *self.order[self.stage])
 
     def land(self):
-        total = self.keep.astype(f32) + self.flying.astype(f32)
         self.stage += 1
         if self.stage == len(self.order):
+            total = self.keep.astype(f32) + self.flying.astype(f32)
             self.total = total.reshape(self.parts, self.rows, self.cols)
             return
         place = self.have.index(block_order().index(self.order[self.stage]))
         self.have.pop(place)
         left = 2 ** len(self.have) * self.rows
-        split = total.astype(bf16).reshape(self.parts * 2**place, 2, left >> place, self.cols)
-        self.keep, self.give = [split[:, i].reshape(self.parts, left, self.cols) for i in range(2)]
+        split = (self.parts * 2**place, 2, left >> place, self.cols)
+        keep, got = self.keep.reshape(split), self.flying.reshape(split)
+        self.keep, self.give = [
+            (keep[:, side].astype(f32) + got[:, side].astype(f32)).astype(bf16).reshape(
+                self.parts, left, self.cols
+            ) for side in range(2)
+        ]
 
     @property
     def done(self):
         return self.total is not None
 
 
-def checkpoint(value, flows, begin=()):
+def checkpoint(value, flows, begin=(), waiting=()):
     value, *flying = tied([value] + [flow.flying for flow in flows])
     for flow, arrived in zip(flows, flying):
         flow.flying = arrived
         flow.land()
-    going = [flow for flow in flows if not flow.done] + list(begin)
+    going = [flow for flow in flows if not flow.done and flow not in waiting] + list(begin)
     value, *ready = tied([value] + [flow.ready() for flow in going])
     for flow, part in zip(going, ready):
         flow.hold(part)
@@ -372,35 +377,55 @@
     )(*masks, *operands)
 
 
-def attend_back(masks, stats, grad_mixed, operands):
-    count, length, width = grad_mixed.shape
+def attend_back(masks, stats, grad_mixed, operands, first, count, before=None):
+    every, length, width = grad_mixed.shape
     groups, mask_specs, stat, stat_rows, specs, spec = attend_specs(length, width)
     pooled = length // 4
 
     def pair_spec(rows):
         return pl.BlockSpec((2, 1, rows, LANES), lambda g, j: (0, g, 0, j))
 
+    def moved(block):
+        index_map = block.index_map
+        return pl.BlockSpec(block.block_shape, lambda g, j: index_map(g + first, j))
+
+    in_specs = [stat, spec(length, 0)] + specs
+    out_specs = [
+        spec(length, 0), pair_spec(length), pair_spec(pooled),
+        pair_spec(WIN + REACH), pair_spec(WIN + REACH),
+    ]
+    out_specs = [moved(block) for block in out_specs[:1]] + [
+        pl.BlockSpec(
+            block.block_shape, functools.partial(lambda g, j: (0, g + first, 0, j))
+        ) for block in out_specs[1:]
+    ]
+    before = before or []
+    kernel_inputs = len(mask_specs) + len(in_specs)
+
+    def kernel(*refs):
+        attend_back_kernel(*refs[:kernel_inputs], *refs[kernel_inputs + len(before) :])
+
     return pl.pallas_call(
-        attend_back_kernel,
+        kernel,
         grid=(count, groups),
-        in_specs=mask_specs + [stat, spec(length, 0)] + specs,
-        out_specs=[
-            spec(length, 0), pair_spec(length), pair_spec(pooled),
-            pair_spec(WIN + REACH), pair_spec(WIN + REACH),
+        in_specs=mask_specs + [moved(block) for block in in_specs]
+        + [pl.BlockSpec(memory_space=pl.ANY)] * len(before),
+        out_specs=out_specs,
+        out_shape=[
+            jax.ShapeDtypeStruct((every, length, width), bf16),
+            jax.ShapeDtypeStruct((2, every, length, width), f32),
+            jax.ShapeDtypeStruct((2, every, pooled, width), f32),
+            jax.ShapeDtypeStruct((2, every, WIN + REACH, width), bf16),
+            jax.ShapeDtypeStruct((2, every, WIN + REACH, width), bf16),
         ],
-        out_shape=[
-            jax.ShapeDtypeStruct((count, length, width), bf16),
-            jax.ShapeDtypeStruct((2, count, length, width), f32),
-            jax.ShapeDtypeStruct((2, count, pooled, width), f32),
-            jax.ShapeDtypeStruct((2, count, WIN + REACH, width), bf16),
-            jax.ShapeDtypeStruct((2, count, WIN + REACH, width), bf16),
-        ],
+        input_output_aliases={kernel_inputs + i: i for i in range(len(before))},
         compiler_params=pltpu.CompilerParams(vmem_limit_bytes=VMEM_LIMIT),
         cost_estimate=pl.CostEstimate(
-            flops=count * length * width * 5000, bytes_accessed=12000000, transcendentals=3000000
+            flops=count * length * width * 5000, bytes_accessed=6000000 * count,
+            transcendentals=1500000 * count,
         ),
         name="attend_back",
-    )(*masks, stats, grad_mixed, *operands)
+    )(*masks, stats, grad_mixed, *operands, *before)
 
 
 def window_masks(length):
@@ -562,12 +587,11 @@
 
 
 def gelu_both(value):
-    inside = jnp.tanh(gelu_coef * (value + 0.044715 * value * value * value))
-    act = 0.5 * value * (1.0 + inside)
-    slope = 0.5 * (1.0 + inside) + 0.5 * value * (1.0 - inside * inside) * gelu_coef * (
-        1.0 + 3 * 0.044715 * value * value
-    )
-    return act, slope
+    square = value * value
+    inside = jnp.tanh(value * (gelu_coef + (gelu_coef * 0.044715) * square))
+    half = 0.5 * value
+    bend = gelu_coef + (3 * 0.044715 * gelu_coef) * square
+    return half + half * inside, 0.5 + 0.5 * inside + half * (1.0 - inside * inside) * bend
 
 
 def small_index():
@@ -684,6 +708,224 @@
     return [side.reshape(shape[0], half * rows, shape[3]) for side in pair]
 
 
+ROWS = 128
+EDGES = ("output_bias", "down_bias", "mixer_gain", "mixer_shift", "feed_gain", "feed_shift")
+
+
+def by_rows(count, body, rows=ROWS):
+    for first in range(0, count, rows):
+        body(slice(first, first + rows))
+
+
+def feed_kernel(x_ref, mixed_ref, vectors_ref, bias_ref, out_ref, up_ref, down_ref,
+                norm_ref, inverse_ref, low_ref, act_ref, slope_ref, norm_two_ref, inverse_two_ref,
+                y_ref, hidden_ref, total_ref):
+    step, last = pl.program_id(0), pl.num_programs(0) - 1
+    count = x_ref.shape[0]
+
+    def vector(name):
+        at = EDGES.index(name)
+        return vectors_ref[at : at + 1, :]
+
+    @pl.when(step == 0)
+    def _():
+        total_ref[...] = dot_nn(mixed_ref[...], out_ref[...])
+
+        def body(at):
+            norm, inverse = normalised(x_ref[at, :] + total_ref[at, :] + vector("output_bias"))
+            hidden = norm * vector("mixer_gain") + vector("mixer_shift")
+            norm_ref[at, :], inverse_ref[at, :] = norm, inverse
+            hidden_ref[at, :] = hidden
+            low_ref[at, :] = hidden.astype(bf16)
+            total_ref[at, :] = jnp.zeros_like(hidden)
+
+        by_rows(count, body)
+
+    def units(at):
+        act, slope = gelu_both(dot_nn(low_ref[at, :], up_ref[...]) + bias_ref[...])
+        act = act.astype(bf16)
+        act_ref[at, :], slope_ref[at, :] = act, slope.astype(bf16)
+        total_ref[at, :] += dot_nn(act, down_ref[...])
+
+    by_rows(count, units, 256)
+
+    @pl.when(step == last)
+    def _():
+        def body(at):
+            rows = hidden_ref[at, :] + total_ref[at, :] + vector("down_bias")
+            norm, inverse = normalised(rows)
+            norm_two_ref[at, :], inverse_two_ref[at, :] = norm, inverse
+            y_ref[at, :] = norm * vector("feed_gain") + vector("feed_shift")
+
+        by_rows(count, body)
+
+
+def feed_forward(x, mixed, small, whole, ratio):
+    count, width = x.shape
+    rows = pl.BlockSpec((count, width), lambda j: (0, 0))
+    line = pl.BlockSpec((count, 1), lambda j: (0, 0))
+    part = pl.BlockSpec((count, width), lambda j: (0, j))
+
+    def weight(shift, moves):
+        return pl.BlockSpec((width, width), lambda j: (0, shift + moves * j))
+
+    def shape(cols, kind):
+        return jax.ShapeDtypeStruct((count, cols), kind)
+
+    return pl.pallas_call(
+        feed_kernel,
+        grid=(ratio,),
+        in_specs=[
+            rows, rows, pl.BlockSpec((8, width), lambda j: (0, 0)),
+            pl.BlockSpec((1, width), lambda j: (0, j)),
+            weight(0, 0), weight(1, 1), weight(1 + ratio, 1),
+        ],
+        out_specs=[rows, line, rows, part, part, rows, line, rows],
+        out_shape=[
+            shape(width, f32), shape(1, f32), shape(width, bf16), shape(ratio * width, bf16),
+            shape(ratio * width, bf16), shape(width, f32), shape(1, f32), shape(width, f32),
+        ],
+        scratch_shapes=[pltpu.VMEM((count, width), f32)] * 2,
+        compiler_params=pltpu.CompilerParams(vmem_limit_bytes=VMEM_LIMIT),
+        cost_estimate=pl.CostEstimate(
+            flops=2 * count * width * width * (1 + 2 * ratio), transcendentals=count * width * ratio,
+            bytes_accessed=2 * whole.size + 4 * count * width * ratio + 20 * count * width,
+        ),
+        name="feed_forward",
+    )(x, mixed, small["vectors"], small["up_bias"], whole, whole, whole)
+
+
+def feed_back_kernel(blocks, index_ref, grads_ref, norm_ref, inverse_ref, norm_two_ref,
+                     inverse_two_ref, vectors_ref, low_ref, act_ref, slope_ref, out_ref, up_ref,
+                     down_ref, one_ref, attention_ref, mixed_ref, sums_ref, bias_ref, *rest):
+    outs, (feed_ref, hidden_ref, total_ref, pre_ref, turn_ref) = rest[:-5], rest[-5:]
+    step, last = pl.program_id(0), pl.num_programs(0) - 1
+    count, width = grads_ref.shape
+
+    def vector(name):
+        at = EDGES.index(name)
+        return vectors_ref[at : at + 1, :]
+
+    def add(name, rows):
+        at = EDGES.index(name)
+        sums_ref[at : at + 1, :] += jnp.sum(rows, axis=0, keepdims=True)
+
+    def store(pair):
+        if blocks is None:
+            pair[0][0] = total_ref[...].astype(bf16)
+        else:
+            store_blocks(blocks, index_ref[0], total_ref, *pair)
+
+    @pl.when(step == 0)
+    def _():
+        sums_ref[...] = jnp.zeros_like(sums_ref)
+        turn_ref[...] = jnp.transpose(low_ref[...])
+
+        def body(at):
+            grads, norm = grads_ref[at, :], norm_two_ref[at, :]
+            add("feed_gain", grads * norm)
+            add("feed_shift", grads)
+            back = normalised_back(grads, vector("feed_gain"), norm, inverse_two_ref[at, :])
+            hidden_ref[at, :] = back
+            back = back.astype(bf16)
+            feed_ref[at, :] = back
+            add("down_bias", back.astype(f32))
+
+        by_rows(count, body)
+
+    pre_ref[...] = (
+        slope_ref[...].astype(f32) * dot_nt(feed_ref[...], down_ref[...])
+    ).astype(bf16)
+    bias_ref[...] = jnp.sum(pre_ref[...].astype(f32), axis=0, keepdims=True)
+    hidden_ref[...] += dot_nt(pre_ref[...], up_ref[...])
+    total_ref[...] = weight_grad(act_ref[...], feed_ref[...])
+    store(outs[: len(outs) // 2])
+    total_ref[...] = dot_nn(turn_ref[...], pre_ref[...])
+    store(outs[len(outs) // 2 :])
+
+    @pl.when(step == last)
+    def _():
+        def body(at):
+            grads, norm = hidden_ref[at, :], norm_ref[at, :]
+            add("mixer_gain", grads * norm)
+            add("mixer_shift", grads)
+            back = normalised_back(grads, vector("mixer_gain"), norm, inverse_ref[at, :])
+            one_ref[at, :] = back
+            back = back.astype(bf16)
+            attention_ref[at, :] = back
+            add("output_bias", back.astype(f32))
+
+        by_rows(count, body)
+        mixed_ref[...] = dot_nt(attention_ref[...], out_ref[...]).astype(bf16)
+
+
+def feed_back(grads, kept, small, whole, ratio):
+    norm, inverse, low, act, slope, norm_two, inverse_two = kept
+    count, width = grads.shape
+    blocks = relative_blocks()
+    half = len(blocks) // 2
+    shard = width // len(blocks)
+    rows = pl.BlockSpec((count, width), lambda j, index: (0, 0))
+    line = pl.BlockSpec((count, 1), lambda j, index: (0, 0))
+    part = pl.BlockSpec((count, width), lambda j, index: (0, j))
+    edge = pl.BlockSpec((8, width), lambda j, index: (0, 0))
+
+    def weight(shift, moves):
+        return pl.BlockSpec((width, width), lambda j, index: (0, shift + moves * j))
+
+    if shard % 8:
+        blocks = None
+        out = [jax.ShapeDtypeStruct((ratio, width, width), bf16)] * 2
+        specs = [pl.BlockSpec((1, width, width), lambda j, index: (j, 0, 0))] * 2
+    else:
+        block = (1, half, shard, width)
+        out = [jax.ShapeDtypeStruct((ratio, half, shard, width), bf16)] * 2
+        out += [jax.ShapeDtypeStruct((1, half, shard, ratio * width), bf16)] * 2
+        specs = [pl.BlockSpec(block, lambda j, index: (j, 0, 0, 0))] * 2
+        specs += [pl.BlockSpec(block, lambda j, index: (0, 0, 0, j))] * 2
+    results = pl.pallas_call(
+        functools.partial(feed_back_kernel, blocks),
+        grid_spec=pltpu.PrefetchScalarGridSpec(
+            num_scalar_prefetch=1,
+            grid=(ratio,),
+            in_specs=[
+                rows, rows, line, rows, line, edge, rows, part, part,
+                weight(0, 0), weight(1, 1), weight(1 + ratio, 1),
+            ],
+            out_specs=[
+                rows, rows, rows, edge, pl.BlockSpec((1, width), lambda j, index: (0, j)), *specs
+            ],
+            scratch_shapes=[
+                pltpu.VMEM((count, width), bf16), pltpu.VMEM((count, width), f32),
+                pltpu.VMEM((width, width), f32), pltpu.VMEM((count, width), bf16),
+                pltpu.VMEM((width, count), bf16),
+            ],
+        ),
+        out_shape=[
+            jax.ShapeDtypeStruct((count, width), f32), jax.ShapeDtypeStruct((count, width), bf16),
+            jax.ShapeDtypeStruct((count, width), bf16), jax.ShapeDtypeStruct((8, width), f32),
+            jax.ShapeDtypeStruct((1, ratio * width), f32), *out,
+        ],
+        compiler_params=pltpu.CompilerParams(vmem_limit_bytes=VMEM_LIMIT),
+        cost_estimate=pl.CostEstimate(
+            flops=2 * count * width * width * (1 + 4 * ratio), transcendentals=0,
+            bytes_accessed=4 * whole.size + 4 * count * width * ratio + 20 * count * width,
+        ),
+        name="feed_back",
+    )(small_index(), grads, norm, inverse, norm_two, inverse_two, small["vectors"], low, act, slope,
+      whole, whole, whole)
+    one, attention_low, grad_mixed, sums, up_sums, *out = results
+    if blocks is None:
+        down = [turned(out[0][i]) for i in range(ratio)]
+        down = [jnp.concatenate([d[:, side] for d in down]) for side in range(2)]
+        up = [turned(out[1][i]) for i in range(ratio)]
+        up = [jnp.concatenate([u[:, side] for u in up], axis=2) for side in range(2)]
+    else:
+        down = [side.reshape(ratio, half * shard, width) for side in out[:2]]
+        up = [side.reshape(1, half * shard, ratio * width) for side in out[2:]]
+    return one, attention_low, grad_mixed, sums, up_sums, down, up
+
+
 def units_back_kernel(spread_ref, *refs):
     parts, out_ref = refs[:-1], refs[-1]
     total = None
@@ -732,10 +974,11 @@
     each = len(sources) // layers
     at = 0
     for layer in range(layers):
-        *vectors, up_ref, taps_ref = sources[layer * each : (layer + 1) * each]
-        for vector in vectors:
-            lines_ref[at : at + 1, :] = vector[...]
-            at += 1
+        query_ref, value_ref, sums_ref, up_ref, taps_ref = sources[layer * each : (layer + 1) * each]
+        lines_ref[at : at + 1, :] = query_ref[...]
+        lines_ref[at + 1 : at + 2, :] = value_ref[...]
+        lines_ref[at + 2 : at + 2 + len(EDGES), :] = sums_ref[: len(EDGES), :]
+        at += 2 + len(EDGES)
         for kind in range(2):
             lines_ref[at : at + TAPS, :] = taps_ref[kind, :TAPS]
             at += TAPS
@@ -752,8 +995,9 @@
     rows = width // len(blocks)
     if rows % 8:
         lines = []
-        for *vectors, up, taps in per_layer:
-            lines += vectors + [taps[0, :TAPS], taps[1, :TAPS], up.reshape(-1, width)]
+        for query, value, sums, up, taps in per_layer:
+            lines += [query, value, sums[: len(EDGES)], taps[0, :TAPS], taps[1, :TAPS]]
+            lines.append(up.reshape(-1, width))
         lines = jnp.concatenate(lines, axis=0)
         lines = jnp.pad(lines, ((0, SMALL_COLUMNS - lines.shape[0]), (0, 0))).T.astype(bf16)
         lines = turned(lines)
@@ -774,7 +1018,7 @@
 
 
 def layer_forward(x, weights, masks, select, count, at):
-    qkv_weight, late_weights, small = weights
+    qkv_weight, feed_weights, small = weights
     width = x.shape[1]
     length = x.shape[0] // count
     x_low = x.astype(bf16)
@@ -783,66 +1027,56 @@
     qkv = at("projected", (qkv + bias).astype(bf16).reshape(count, length, -1))
     rows_low = passed_along(qkv[:, length - WIN :, width:], 1)
     rows_up = passed_along(qkv[:, :WIN, width:], -1)
+    rows_low, rows_up = tied([rows_low, rows_up])
     pooled = at("pooled", pool(select, small["taps"], qkv, rows_low, width))
     pooled_low, pooled_up = pooled_rims(pooled)
     pooled_up = at("attending", pooled_up)
     operands = attend_operands(qkv, rows_low, rows_up, pooled, pooled_low, pooled_up)
     mixed, stats = attend(masks, operands, width)
     mixed = at("attended", mixed.reshape(count * length, width))
-    out_weight, up_weight, down_weight = late_weights()
-    norm, inverse = normalised(x + matmul(mixed, out_weight) + small["output_bias"])
-    hidden = norm * small["mixer_gain"] + small["mixer_shift"]
-    hidden = at("mixed", hidden)
-    hidden_low = hidden.astype(bf16)
-    act, slope = gelu_both(matmul(hidden_low, up_weight) + small["up_bias"])
-    act_low, slope = act.astype(bf16), slope.astype(bf16)
-    norm_two, inverse_two = normalised(hidden + matmul(act_low, down_weight) + small["down_bias"])
-    y = at("fed", norm_two * small["feed_gain"] + small["feed_shift"])
-    kept = (x_low, operands, stats, mixed, norm, inverse, hidden_low, act_low, slope,
-            norm_two, inverse_two)
-    return y, kept, (qkv_weight, out_weight, up_weight, down_weight, small)
+    ratio = small["up_bias"].shape[1] // width
+    norm, inverse, hidden_low, act_low, slope, norm_two, inverse_two, y = feed_forward(
+        x, mixed, small, feed_weights, ratio
+    )
+    y = at("fed", y)
+    kept = (x_low, operands, stats, mixed, (norm, inverse, hidden_low, act_low, slope, norm_two, inverse_two))
+    return y, kept
 
 
 def layer_backward(grads, kept, weights, masks, select, count, at):
-    qkv_weight, out_weight, up_weight, down_weight, small = weights
-    (x_low, operands, stats, mixed, norm, inverse, hidden_low, act_low, slope,
-     norm_two, inverse_two) = kept
+    qkv_weight, feed_weights, small = weights
+    x_low, operands, stats, mixed, feed_kept = kept
     rows, width = grads.shape
     length = rows // count
-    ratio = act_low.shape[1] // width
+    ratio = small["up_bias"].shape[1] // width
 
     def total(value):
         return jnp.sum(value.astype(f32), axis=0, keepdims=True)
 
-    feed_gain, feed_shift = total(grads * norm_two), total(grads)
-    grad_two = normalised_back(grads, small["feed_gain"], norm_two, inverse_two)
-    feed_low = grad_two.astype(bf16)
-    feed_low = at("down", feed_low, (act_low, feed_low))
-    grad_pre = (slope.astype(f32) * matmul_t(feed_low, down_weight)).astype(bf16)
-    grad_pre = at("up", grad_pre, (hidden_low, grad_pre))
-    grad_hidden = grad_two + matmul_t(grad_pre, up_weight)
-    mixer_gain, mixer_shift = total(grad_hidden * norm), total(grad_hidden)
-    grad_one = normalised_back(grad_hidden, small["mixer_gain"], norm, inverse)
-    attention_low = grad_one.astype(bf16)
-    grad_mixed = matmul_t(attention_low, out_weight).astype(bf16).reshape(count, length, width)
-    grad_mixed = at("attending", grad_mixed)
-    grad_query, own, pooled_own, rim_low, rim_up = attend_back(masks, stats, grad_mixed, operands)
+    grad_one, attention_low, grad_mixed, sums, up_sums, down_halves, up_halves = feed_back(
+        grads, feed_kept, small, feed_weights, ratio
+    )
+    grad_mixed = at("attending", grad_mixed, (down_halves, up_halves))
+    grad_mixed = grad_mixed.reshape(count, length, width)
+    part = max(count // 2, 1)
+    pieces = list(attend_back(masks, stats, grad_mixed, operands, 0, part))
+    if part < count:
+        pieces[0] = at("halfway", pieces[0])
+        pieces = attend_back(masks, stats, grad_mixed, operands, part, count - part, pieces)
+    grad_query, own, pooled_own, rim_low, rim_up = pieces
+    rim_up = at("rims", rim_up)
     grad_query = grad_query.reshape(rows, width)
     from_low, from_up, pooled_own = rims_return(rim_low, rim_up, pooled_own)
-    pooled_own = at("attended", pooled_own, (x_low, grad_query, mixed, attention_low))
     own, tail, taps = pool_back(
         select, small["taps"], operands[0], operands[3], own, pooled_own, from_low, from_up
     )
     tail = passed_along(tail, -1).astype(f32)
-    own = at("pooled", own)
+    own = at("pooled", own, (x_low, grad_query, mixed, attention_low))
     own = own + jnp.pad(tail, ((0, 0), (0, 0), (length - 16, 0), (0, 0)))
     own = own.astype(bf16).reshape(2, rows, width)
     grad_qkv = (grad_query, own[0], own[1])
     grad_x = grad_one + matmul_t(jnp.concatenate(grad_qkv, axis=1), qkv_weight)
-    small_sums = [
-        total(grad_query), total(own[1]), total(attention_low), total(feed_low),
-        mixer_gain, mixer_shift, feed_gain, feed_shift, total(grad_pre), taps,
-    ]
+    small_sums = [total(grad_query), total(own[1]), sums, up_sums, taps]
     return grad_x, (x_low, *grad_qkv, mixed, attention_low), small_sums
 
 
@@ -869,16 +1103,11 @@
         result.append({
             "query_bias": piece[0],
             "value_bias": piece[1],
-            "output_bias": piece[2],
-            "down_bias": piece[3],
-            "mixer_gain": piece[4],
-            "mixer_shift": piece[5],
-            "feed_gain": piece[6],
-            "feed_shift": piece[7],
+            "vectors": piece[2:10],
             "taps": jnp.stack([
                 jnp.pad(piece[8 : 8 + TAPS], pad), jnp.pad(piece[8 + TAPS : 8 + 2 * TAPS], pad),
             ]),
-            "up_bias": piece[8 + 2 * TAPS :].reshape(ratio * width),
+            "up_bias": piece[8 + 2 * TAPS :].reshape(1, ratio * width),
         })
     return result
 
@@ -905,8 +1134,6 @@
         split = rows.reshape(rows.shape[0], devices, ratio, shard_rows)
         return split.transpose(0, 2, 1, 3).reshape(rows.shape)
 
-    up_shards = [units_apart(up_weight[layer]) for layer in range(layers)]
-    down_shards = [down_weight[layer].reshape(ratio, shard_rows, width) for layer in range(layers)]
     shard = jnp.concatenate(
         [query_weight[0], key_weight[0], value_weight[0], small_shard], axis=1
     )
@@ -915,30 +1142,31 @@
     later = [
         Gather(jnp.concatenate(
             [query_weight[layer], key_weight[layer], value_weight[layer]], axis=1
-        )[None], path("z"))
+        )[None], path("x"))
         for layer in range(1, layers)
     ]
     x = tokens.reshape(count * length, width).astype(f32)
     feeds = []
-    for layer in range(layers):
-        shard = jnp.concatenate(
-            [output_weight[layer], up_shards[layer], *down_shards[layer]], axis=1
+
+    def gather_feed(layer, after):
+        out, up, down, after = tied(
+            [output_weight[layer], up_weight[layer], down_weight[layer], after]
         )
+        parts = down.reshape(ratio, shard_rows, width)
+        shard = jnp.concatenate([out, units_apart(up), *parts], axis=1)
         feeds.append(lax.all_gather(shard, ("seq", "batch"), axis=0, tiled=True))
+        return after
+
     x = checkpoint(x, [], [first])
-    while first.left > 1:
+    x = gather_feed(0, checkpoint(x, [first]))
+    while first.left > 2:
         x = checkpoint(x, [first])
+    for layer in range(1, layers):
+        x = gather_feed(layer, x)
+    x = checkpoint(x, [first])
     x = checkpoint(x, [first], later)
     first_whole = in_place(first.halves, first.cols)
     smalls = unpack_small(first_whole[:, 3 * width :], layers, ratio)
-
-    def late_weights(layer):
-        whole = feeds[layer]
-        down_whole = whole[:, (1 + ratio) * width :].reshape(width, ratio, width)
-        return (
-            whole[:, :width], whole[:, width : (1 + ratio) * width],
-            down_whole.transpose(1, 0, 2).reshape(-1, width),
-        )
 
     def landed(value, flows, left):
         while True:
@@ -965,10 +1193,8 @@
             qkv_weight = first_whole[:, : 3 * width]
         else:
             qkv_weight = in_place(later[layer - 1].halves, width)
-        late = functools.partial(late_weights, layer)
-        x, kept, whole = layer_forward(
-            x, (qkv_weight, late, smalls[layer]), masks, select, count, forward_at(layer)
-        )
+        whole = (qkv_weight, feeds[layer], smalls[layer])
+        x, kept = layer_forward(x, whole, masks, select, count, forward_at(layer))
         states.append(kept)
         weights.append(whole)
     layer_output = x.astype(bf16).reshape(tokens.shape)
@@ -976,41 +1202,42 @@
     grads = grads.reshape(count * length, width)
     flows = {}
     plans = {
-        "down": ["up", "attended", "pooled", "end", "next down", "never"],
-        "up": ["attending", "pooled", "end", "next up", "next attending", "never"],
-        "in": ["next down", "next attended", "next pooled", "never"],
-        "query": ["pooled", "never"],
+        "down": ["rims", "next attending", "next halfway", "next rims", "never"],
+        "up": ["rims", "next attending", "next halfway", "next rims", "never"],
+        "in": ["next attending", "next rims", "never"],
+        "query": ["never"],
     }
+    last_plans = {
+        "down": ["halfway", "rims", "never"],
+        "up": ["halfway", "rims", "never"],
+    }
+    waiting = []
 
     def due(layer, name):
         result = []
         for (kind, owner), flow in flows.items():
-            when = plans[kind][min(flow.stage, len(plans[kind]) - 1)]
-            if not flow.done and when == ("next " if owner > layer else "") + name:
-                result.append(flow)
-            elif not flow.done and owner > layer + 1:
+            plan = last_plans[kind] if owner == 0 and kind in last_plans else plans[kind]
+            when = plan[min(flow.stage, len(plan) - 1)]
+            if flow.done or flow in waiting:
+                continue
+            if when == ("next " if owner > layer else "") + name or owner > layer + 1:
                 result.append(flow)
         return result
 
     def backward_at(layer):
         def at(name, value, given=None):
             landing, begin = due(layer, name), []
-            if name == "down":
-                plan = [(0, part, 1, 0) for part in range(ratio)]
-                flow = Scatter(weight_grads(given, plan, width, stacked=True), path("y")[::-1])
-                flows[name, layer] = flow
-                begin.append(flow)
-            if name == "up":
-                plan = [(0, 0, 1, part) for part in range(ratio)]
-                flow = Scatter(weight_grads(given, plan, width), path("x")[::-1])
-                flows[name, layer] = flow
-                begin.append(flow)
-            if name == "attended" and layer == 0:
+            if name == "attending":
+                for kind, halves, last in zip(("down", "up"), given, "yx"):
+                    flows[kind, layer] = Scatter(halves, path(last)[::-1])
+                    begin.append(flows[kind, layer])
+            if name == "pooled" and layer == 0:
                 plan = [(0, 0, 1, 0), (2, 0, 3, 0)]
                 flow = Scatter(weight_grads(given, plan, width), path("z")[::-1])
                 flows["query", layer] = flow
-                begin.append(flow)
-            return checkpoint(value, landing, begin)
+            if name in ("rims", "pooled"):
+                waiting.extend(flow for flow in landing if len(flow.order) - flow.stage > 2)
+            return checkpoint(value, landing, [] if name == "pooled" else begin, waiting)
 
         return at
 
@@ -1023,18 +1250,25 @@
             plan = [(0, 0, 1 + i, 0) for i in range(3)] + [(4, 0, 5, 0)]
             flow = Scatter(weight_grads(given, plan, width), path("z")[::-1])
             flows["in", layer] = flow
-            grads = checkpoint(grads, due(layer, "end"), [flow])
+            grads = checkpoint(grads, due(layer, "end"), [flow] + waiting)
+            waiting.clear()
     halves = weight_grads((given[0], *given[2:4]), [(0, 0, 1, 0), (0, 0, 2, 0)], width)
     sides = small_grads(small_sums, width)
     joined = [jnp.concatenate(parts, axis=2) for parts in zip(halves, sides)]
-    last = Scatter(joined, path("y")[::-1])
+    last = Scatter(joined, path("x")[::-1])
     flows["last", 0] = last
-    marker = checkpoint(last.keep[:1, :1, :1], [], [last])
+    ends = [last, flows["query", 0]]
+    marker = checkpoint(last.keep[:1, :1, :1], [], ends)
+    marker = checkpoint(marker, ends, waiting)
     while True:
-        flying = [flow for flow in flows.values() if not flow.done]
-        if not flying:
+        ends = [flow for flow in ends if not flow.done]
+        others = [flow for flow in flows.values() if not flow.done and flow not in ends]
+        if not ends + others:
             break
-        marker = checkpoint(marker, flying)
+        if ends:
+            marker = checkpoint(marker, ends)
+        if others:
+            marker = checkpoint(marker, others)
     totals = []
     for layer in range(layers):
         if layer > 0:

time: 639 us -> 597 us (0.934)
  matrix products: 69 us -> 13.1 us
  Pallas kernels: 126 us -> 176 us
  local copies, waits for them, and re-layouts: 61.3 us -> 37.1 us
  waiting for transfers between devices: 197 us -> 177 us
  starting transfers between devices: 100 us -> 115 us
  other arithmetic: 60.1 us -> 53.7 us
    pallas_call x2 -> x8, Pallas kernels: 38.6 us -> 113 us  [the longest x4 42.2 us: attend_back(): pl.pallas_call(kernel, grid=(count, groups), in_specs=mask_specs + [moved...]
    dot_general x8 -> x2, matrix products: 40.3 us -> 4.97 us  [matmul_t(): lax.dot_general(a, b, (((1,), (1,)), ((), ())), preferred_element_type=f32)]
    ppermute x45, waiting for transfers between devices: 183 us -> 155 us  [exchange(): return lax.ppermute(value, axis, pairs)]
    pallas_call x7 -> x3, Pallas kernels: 33.9 us -> 9.75 us  [weight_grads(): pl.pallas_call(functools.partial(weight_grads_kernel, blocks, plan), grid...]
    dot_general x8 -> x2, matrix products: 28.6 us -> 8.12 us  [matmul(): return jnp.dot(a, b, preferred_element_type=f32)]
    ppermute x45, starting transfers between devices: 66.1 us -> 83.4 us  [exchange(): return lax.ppermute(value, axis, pairs)]
    ppermute x14, waiting for transfers between devices: 7.44 us -> 22 us  [passed_along(): return lax.ppermute(value, 'seq', pairs)]
    slice x18 -> x2, local copies, waits for them, and re-layouts: 15.6 us -> 1.47 us  [the longest x1 1.43 us: unpack_small(): piece[2:10]]
  transfers between devices with their start and end apart: 61 -> 61, of which waited for: 28 -> 30; matrix products, arithmetic and copies ran while one was open for 19% -> 10% of each run, Pallas kernels for 16% -> 21%
where the time goes in v2:
time: 597 us; the launch traced here: 588 us
  waiting for transfers between devices  177 us (30%)
  Pallas kernels  176 us (29%)
  starting transfers between devices  115 us (19%)
  other arithmetic  53.7 us (9%)
  local copies, waits for them, and re-layouts  37.1 us (6%)
  between operations  16.6 us (3%)
  matrix products  13.1 us (2%)
    ppermute x45, waiting for transfers between devices, exchange(): return lax.ppermute(value, axis, pairs)  155 us
    ppermute x45, starting transfers between devices, exchange(): return lax.ppermute(value, axis, pairs)  83.4 us
    pallas_call x4, Pallas kernels, attend_back(): pl.pallas_call(kernel, grid=(count, groups), in_specs=mask_specs + [moved...  42.2 us
    pallas_call x2, Pallas kernels, feed_back(): pl.pallas_call(functools.partial(feed_back_kernel, blocks), grid_spec=plt...  41.3 us
    ppermute x14, starting transfers between devices, passed_along(): return lax.ppermute(value, 'seq', pairs)  31.2 us
    convert_element_type x30, other arithmetic, land(): (keep[:, side].astype(f32) + got[:, side].astype(f32)).astype(bf16)  31.2 us
    pallas_call x2, Pallas kernels, feed_forward(): pl.pallas_call(feed_kernel, grid=(ratio,), in_specs=[rows, rows, pl.Block...  29.1 us
    ppermute x14, waiting for transfers between devices, passed_along(): return lax.ppermute(value, 'seq', pairs)  22 us
  transfers between devices with their start and end apart: 61, of which 30 were waited for; matrix products, arithmetic and copies ran while one was open for 10% of the time, Pallas kernels for 21%

profile of v2, /device:TPU:0, one launch (start us, length us, event | category | flops | bytes accessed | tf_op | source)
XLA Modules:
  0.0 587.5 jit_solution(17213658371316817435)
XLA Ops:
  15.0 5.6 collective-permute-done
  25.0 6.2 %collective-permute-done.1 = bf16[1,48,2432]{2,1,0:T(8,128)(2,1)S(1)} collective-permute-done((bf16[1,48,2432]{2,1,0:T(8,128)(2,1)S(1)}, bf16[1,48,2432]{2,1,0:T(8,128)(2,1)S(1)}, u32[]{:S(2)}, u32[]{:S(2)}) %collective-permute-start.1) | collective-permute-done | bytes 233504 | tf_op jit(solution)/shard_map/ppermute | solution.py:50
  32.5 12.1 %collective-permute-done.2 = bf16[1,96,2432]{2,1,0:T(8,128)(2,1)S(1)} collective-permute-done((bf16[1,96,2432]{2,1,0:T(8,128)(2,1)S(1)}, bf16[1,96,2432]{2,1,0:T(8,128)(2,1)S(1)}, u32[]{:S(2)}, u32[]{:S(2)}) %collective-permute-start.2) | collective-permute-done | bytes 466976 | tf_op jit(solution)/shard_map/ppermute | solution.py:50
  49.5 23.6 %collective-permute-done.3 = bf16[1,192,2432]{2,1,0:T(8,128)(2,1)S(1)} collective-permute-done((bf16[1,192,2432]{2,1,0:T(8,128)(2,1)S(1)}, bf16[1,192,2432]{2,1,0:T(8,128)(2,1)S(1)}, u32[]{:S(2)}, u32[]{:S(2)}) %collective-permute-start.3) | collective-permute-done | bytes 933920 | tf_op jit(solution)/shard_map/ppermute | solution.py:50
  84.4 5.4 collective-permute-start.5
  94.0 8.8 %collective-permute-done.5 = bf16[1,24,2304]{2,1,0:T(8,128)(2,1)S(1)} collective-permute-done((bf16[1,24,2304]{2,1,0:T(8,128)(2,1)S(1)}, bf16[1,24,2304]{2,1,0:T(8,128)(2,1)S(1)}, u32[]{:S(2)}, u32[]{:S(2)}) %collective-permute-start.5) | collective-permute-done | bytes 110624 | tf_op jit(solution)/shard_map/ppermute | solution.py:50
  112.8 11.8 %collective-permute-done.8 = bf16[1,48,2304]{2,1,0:T(8,128)(2,1)S(1)} collective-permute-done((bf16[1,48,2304]{2,1,0:T(8,128)(2,1)S(1)}, bf16[1,48,2304]{2,1,0:T(8,128)(2,1)S(1)}, u32[]{:S(2)}, u32[]{:S(2)}) %collective-permute-start.8) | collective-permute-done | bytes 221216 | tf_op jit(solution)/shard_map/ppermute | solution.py:50
  133.6 11.1 %attend.2 = (bf16[2,256,768]{2,1,0:T(8,128)(2,1)S(1)}, f32[2,3,8,256]{3,2,1,0:T(8,128)S(1)}) custom-call(f32[2,256,256]{2,1,0:T(8,128)S(1)} %pad_maximum_fusion.8.near_ref.refs_0_, f32[2,192,256]{2,1,0:T(8,128)S(1)} %copy-done.6, bf16[2,256,2304]{2,1,0:T(8,128)(2,1)S(1)} %bitcast.355, bf16[2,256,2304]{2,1,0:T(8,128)(2,1)S(1)} %bitcast.356, ...), custom_call_target="tpu_custom_call" | custom-call | flops 786432000 | bytes 8000000 | tf_op jit(solution)/shard_map/attend/pallas_call | solution.py:363
  154.6 14.5 %feed_forward.2 = (f32[512,768]{1,0:T(8,128)S(1)}, f32[512,1]{1,0:T(8,128)S(1)}, bf16[512,768]{1,0:T(8,128)(2,1)S(1)}, bf16[512,3072]{1,0:T(8,128)(2,1)}, bf16[5...) custom-call(f32[512,768]{1,0:T(8,128)} %bitcast_convert_fusion.x_ref, ...), custom_call_target="tpu_custom_call" | custom-call | flops 5435817984 | bytes 24772608 | tf_op jit(solution)/shard_map/feed_forward/pallas_call | solution.py:775
  170.3 7.5 %collective-permute-done.12 = bf16[1,192,2304]{2,1,0:T(8,128)(2,1)} collective-permute-done((bf16[1,192,2304]{2,1,0:T(8,128)(2,1)S(1)}, bf16[1,192,2304]{2,1,0:T(8,128)(2,1)}, u32[]{:S(2)}, u32[]{:S(2)}) %collective-permute-start.12) | collective-permute-done | bytes 884768 | tf_op jit(solution)/shard_map/ppermute | solution.py:50
  197.7 7.2 %collective-permute-done.15.ku_ref.vu_ref.refs_9_.refs_10_ = bf16[2,64,1536]{2,1,0:T(8,128)(2,1)S(1)} collective-permute-done((bf16[2,64,1536]{2,1,0:T(8,128)(2,1)S(1)}, bf16[2,64,1536]{2,1,0:T(8,128)(2,1)S(1)}, u32[]{:S(2)}, u32[]{:S(2)}) %collective-permute-start.15) | collective-permute-done | bytes 393248 | tf_op jit(solution)/shard_map/ppermute | solution.py:171
  206.7 10.0 %collective-permute-start.16 = (bf16[2,64,1536]{2,1,0:T(8,128)(2,1)S(1)}, bf16[2,64,1536]{2,1,0:T(8,128)(2,1)S(1)}, u32[]{:S(2)}, u32[]{:S(2)}) collective-permute-start(bf16[2,64,1536]{2,1,0:T(8,128)(2,1)S(1)} %pool.3.pk_ref.pv_ref.refs_11_.refs_12_), channel_id=1, source_target_pairs={{0,2},{2,4},{4,6},{6,8},{8,10},{10,12},{12,14},{14,16},{16,18},{18... | collective-permute-start | bytes 1179656 | tf_op jit(solution)/shard_map/ppermute | solution.py:171
  222.3 10.5 %attend.3 = (bf16[2,256,768]{2,1,0:T(8,128)(2,1)S(1)}, f32[2,3,8,256]{3,2,1,0:T(8,128)S(1)}) custom-call(f32[2,256,256]{2,1,0:T(8,128)S(1)} %pad_maximum_fusion.8.near_ref.refs_0_, f32[2,192,256]{2,1,0:T(8,128)S(1)} %copy-done.7, bf16[2,256,2304]{2,1,0:T(8,128)(2,1)S(1)} %bitcast.367, bf16[2,256,2304]{2,1,0:T(8,128)(2,1)S(1)} %bitcast.368, ...), custom_call_target="tpu_custom_call" | custom-call | flops 786432000 | bytes 8000000 | tf_op jit(solution)/shard_map/attend/pallas_call | solution.py:363
  236.3 14.6 %feed_forward.3 = (f32[512,768]{1,0:T(8,128)S(1)}, f32[512,1]{1,0:T(8,128)S(1)}, bf16[512,768]{1,0:T(8,128)(2,1)S(1)}, bf16[512,3072]{1,0:T(8,128)(2,1)}, bf16[5...) custom-call(f32[512,768]{1,0:T(8,128)} %get-tuple-element.269.x_ref, ...), custom_call_target="tpu_custom_call" | custom-call | flops 5435817984 | bytes 24772608 | tf_op jit(solution)/shard_map/feed_forward/pallas_call | solution.py:775
  253.2 20.7 %feed_back.2 = (f32[512,768]{1,0:T(8,128)S(1)}, bf16[512,768]{1,0:T(8,128)(2,1)S(1)}, bf16[512,768]{1,0:T(8,128)(2,1)S(1)}, f32[8,768]{1,0:T(8,128)S(1)}, f32[1,...) custom-call(s32[1]{0:T(128)} %bitcast.32.index_ref, ...), custom_call_target="tpu_custom_call" | custom-call | flops 10267656192 | bytes 35389440 | tf_op jit(solution)/shard_map/feed_back/pallas_call | solution.py:886
  274.8 6.0 %collective-permute-start.18 = (bf16[4,384,768]{2,1,0:T(8,128)(2,1)}, bf16[4,384,768]{2,1,0:T(8,128)(2,1)S(1)}, u32[]{:S(2)}, u32[]{:S(2)}) collective-permute-start(bf16[4,384,768]{2,1,0:T(8,128)(2,1)} %bitcast.513), channel_id=1, source_target_pairs={{0,2},{2,0},{4,6},{6,4},{8,10},{10,8},{12,14},{14,12},{16,18},{18,... | collective-permute-start | bytes 7077896 | tf_op jit(solution)/shard_map/ppermute | solution.py:50
  280.9 10.8 %attend_back.4 = (bf16[2,256,768]{2,1,0:T(8,128)(2,1)S(1)}, f32[2,2,256,768]{3,2,1,0:T(8,128)}, f32[2,2,64,768]{3,2,1,0:T(8,128)S(1)}, bf16[2,2,128,768]{3,2,1,0:T(8,128)(2,1)S(1)}, bf16[2,2,128,768]{3,2,1,0:T(8,128)(2,1)S(1)}) custom-call(f32[2,256,256]{2,1,0:T(8,128)S(1)} %pad_maximum_fusion.8.near_ref.refs_0_, f32[2,192,256]{2,1,0:T(8,128)S(1)} %copy-done.8, ...), custom_call_target="tpu_custom_call" | custom-call | flops 983040000 | bytes 6000000 | tf_op jit(solution)/shard_map/attend_back/pallas_call | solution.py:408
  291.7 10.4 %attend_back.5 = (bf16[2,256,768]{2,1,0:T(8,128)(2,1)S(1)}, f32[2,2,256,768]{3,2,1,0:T(8,128)}, f32[2,2,64,768]{3,2,1,0:T(8,128)S(1)}, bf16[2,2,128,768]{3,2,1,0:T(8,128)(2,1)S(1)}, bf16[2,2,128,768]{3,2,1,0:T(8,128)(2,1)S(1)}) custom-call(f32[2,256,256]{2,1,0:T(8,128)S(1)} %pad_maximum_fusion.8, ...), custom_call_target="tpu_custom_call", output_to_operand_aliasing={{0}: (17, {}), {1}: (18, {}), {2}: (19, {}), {3}: (20, {}),... | custom-call | flops 983040000 | bytes 6000000 | tf_op jit(solution)/shard_map/attend_back/pallas_call | solution.py:408
  311.0 7.0 %pool_back.2 = (f32[2,2,256,768]{3,2,1,0:T(8,128)}, bf16[2,2,16,768]{3,2,1,0:T(8,128)(2,1)S(1)}, f32[2,8,768]{2,1,0:T(8,128)S(1)}) custom-call(bf16[320,256]{1,0:T(8,128)(2,1)S(1)} %fusion.41.select_ref, bf16[256,320]{1,0:T(8,128)(2,1)S(1)} %fusion.38.spread_ref, f32[2,8,768]{2,1,0:T(8,128)S(1)} %pad_maximum_fusion.19.kernel_ref, ...), custom_call_target="tpu_custom_call" | custom-call | flops 1572864000 | bytes 9000000 | tf_op jit(solution)/shard_map/pool_back/pallas_call | solution.py:535
  323.0 11.9 %collective-permute-done.22 = bf16[2,2,16,768]{3,2,1,0:T(8,128)(2,1)S(1)} collective-permute-done((bf16[2,2,16,768]{3,2,1,0:T(8,128)(2,1)S(1)}, bf16[2,2,16,768]{3,2,1,0:T(8,128)(2,1)S(1)}, u32[]{:S(2)}, u32[]{:S(2)}) %collective-permute-start.22) | collective-permute-done | bytes 98336 | tf_op jit(solution)/shard_map/ppermute | solution.py:171
  340.1 5.3 weight_grads.3
  354.7 20.6 %feed_back.3 = (f32[512,768]{1,0:T(8,128)S(1)}, bf16[512,768]{1,0:T(8,128)(2,1)S(1)}, bf16[512,768]{1,0:T(8,128)(2,1)S(1)}, f32[8,768]{1,0:T(8,128)S(1)}, f32[1,...) custom-call(s32[1]{0:T(128)} %bitcast.32.index_ref, ...), custom_call_target="tpu_custom_call" | custom-call | flops 10267656192 | bytes 35389440 | tf_op jit(solution)/shard_map/feed_back/pallas_call | solution.py:886
  392.8 10.6 %attend_back.6 = (bf16[2,256,768]{2,1,0:T(8,128)(2,1)S(1)}, f32[2,2,256,768]{3,2,1,0:T(8,128)}, f32[2,2,64,768]{3,2,1,0:T(8,128)S(1)}, bf16[2,2,128,768]{3,2,1,0:T(8,128)(2,1)S(1)}, bf16[2,2,128,768]{3,2,1,0:T(8,128)(2,1)S(1)}) custom-call(f32[2,256,256]{2,1,0:T(8,128)S(1)} %pad_maximum_fusion.8.near_ref.refs_0_, f32[2,192,256]{2,1,0:T(8,128)S(1)} %copy-done.8, ...), custom_call_target="tpu_custom_call" | custom-call | flops 983040000 | bytes 6000000 | tf_op jit(solution)/shard_map/attend_back/pallas_call | solution.py:408
  419.1 10.5 %attend_back.7 = (bf16[2,256,768]{2,1,0:T(8,128)(2,1)S(1)}, f32[2,2,256,768]{3,2,1,0:T(8,128)}, f32[2,2,64,768]{3,2,1,0:T(8,128)S(1)}, bf16[2,2,128,768]{3,2,1,0:T(8,128)(2,1)S(1)}, bf16[2,2,128,768]{3,2,1,0:T(8,128)(2,1)S(1)}) custom-call(f32[2,256,256]{2,1,0:T(8,128)S(1)} %pad_maximum_fusion.8, ...), custom_call_target="tpu_custom_call", output_to_operand_aliasing={{0}: (17, {}), {1}: (18, {}), {2}: (19, {}), {3}: (20, {}),... | custom-call | flops 983040000 | bytes 6000000 | tf_op jit(solution)/shard_map/attend_back/pallas_call | solution.py:408
  431.3 15.8 %collective-permute-done.33 = bf16[4,192,768]{2,1,0:T(8,128)(2,1)S(1)} collective-permute-done((bf16[4,192,768]{2,1,0:T(8,128)(2,1)}, bf16[4,192,768]{2,1,0:T(8,128)(2,1)S(1)}, u32[]{:S(2)}, u32[]{:S(2)}) %collective-permute-start.33) | collective-permute-done | bytes 1179680 | tf_op jit(solution)/shard_map/ppermute | solution.py:50
  456.0 6.9 %pool_back.3 = (f32[2,2,256,768]{3,2,1,0:T(8,128)}, bf16[2,2,16,768]{3,2,1,0:T(8,128)(2,1)S(1)}, f32[2,8,768]{2,1,0:T(8,128)S(1)}) custom-call(bf16[320,256]{1,0:T(8,128)(2,1)S(1)} %fusion.41.select_ref, bf16[256,320]{1,0:T(8,128)(2,1)S(1)} %fusion.38.spread_ref, f32[2,8,768]{2,1,0:T(8,128)S(1)} %pad_maximum_fusion.18.kernel_ref, ...), custom_call_target="tpu_custom_call" | custom-call | flops 1572864000 | bytes 9000000 | tf_op jit(solution)/shard_map/pool_back/pallas_call | solution.py:535
  466.6 11.8 %collective-permute-start.48 = (bf16[4,24,768]{2,1,0:T(8,128)(2,1)}, bf16[4,24,768]{2,1,0:T(8,128)(2,1)S(1)}, u32[]{:S(2)}, u32[]{:S(2)}) collective-permute-start(bf16[4,24,768]{2,1,0:T(8,128)(2,1)} %fusion.58), channel_id=1, source_target_pairs={{0,16},{2,18},{4,20},{6,22},{8,24},{10,26},{12,28},{14,30},{16,0},... | collective-permute-start | bytes 442376 | tf_op jit(solution)/shard_map/ppermute | solution.py:50
  498.4 6.7 %collective-permute-done.50 = bf16[1,96,3072]{2,1,0:T(8,128)(2,1)S(1)} collective-permute-done((bf16[1,96,3072]{2,1,0:T(8,128)(2,1)S(1)}, bf16[1,96,3072]{2,1,0:T(8,128)(2,1)S(1)}, u32[]{:S(2)}, u32[]{:S(2)}) %collective-permute-start.50) | collective-permute-done | bytes 589856 | tf_op jit(solution)/shard_map/ppermute | solution.py:50
  507.0 10.0 %collective-permute-done.52 = bf16[1,96,3072]{2,1,0:T(8,128)(2,1)S(1)} collective-permute-done((bf16[1,96,3072]{2,1,0:T(8,128)(2,1)S(1)}, bf16[1,96,3072]{2,1,0:T(8,128)(2,1)S(1)}, u32[]{:S(2)}, u32[]{:S(2)}) %collective-permute-start.52) | collective-permute-done | bytes 589856 | tf_op jit(solution)/shard_map/ppermute | solution.py:50
  540.4 8.6 %collective-permute-done.56 = bf16[1,24,3072]{2,1,0:T(8,128)(2,1)S(1)} collective-permute-done((bf16[1,24,3072]{2,1,0:T(8,128)(2,1)S(1)}, bf16[1,24,3072]{2,1,0:T(8,128)(2,1)S(1)}, u32[]{:S(2)}, u32[]{:S(2)}) %collective-permute-start.56) | collective-permute-done | bytes 147488 | tf_op jit(solution)/shard_map/ppermute | solution.py:50
  554.9 5.9 %units_back.1 = f32[48,3072]{1,0:T(8,128)} custom-call(bf16[4,384,1536]{2,1,0:T(8,128)(2,1)S(1)} %add_convert_fusion.spread_ref, f32[48,3072]{1,0:T(8,128)S(1)} %pad_maximum_fusion.6.refs_0_.refs_1_.refs_2_.refs_3_, f32[48,3072]{1,0:T(8,128)S(1)} %pad_maximum_fusion.6.refs_0_.refs_1_.refs_2_.refs_3_, ...), custom_call_target="tpu_custom_call" | custom-call | tf_op jit(solution)/shard_map/units_back/pallas_call | solution.py:953
  564.8 4.9 collective-permute-done.47
  (506 shorter events, 237.7 us)
Async XLA Ops:
  7.4 147.3 %all-gather.3.cloned.1.call-start = ((), (), s32[]{:S(2)}) async-start(), calls=%async_computation | async-start | bytes 10948608 | tf_op jit(solution)/shard_map/all_gather | solution.py:1157
  24.1 210.3 %all-gather.5.cloned.1.call-start = ((), (), s32[]{:S(2)}) async-start(), calls=%async_computation.1 | async-start | bytes 10948608 | tf_op jit(solution)/shard_map/all_gather | solution.py:1157
  48.2 25.0 %collective-permute-start.3 = (bf16[1,192,2432]{2,1,0:T(8,128)(2,1)S(1)}, bf16[1,192,2432]{2,1,0:T(8,128)(2,1)S(1)}, u32[]{:S(2)}, u32[]{:S(2)}) collective-permute-start(bf16[1,192,2432]{2,1,0:T(8,128)(2,1)S(1)} %bitcast.417), channel_id=1, source_target_pairs={{0,4},{2,6},{4,0},{6,2},{8,12},{10,14},{12,8},{14,10},{16,20},{18,... | collective-permute-start | bytes 2801672 | tf_op jit(solution)/shard_map/ppermute | solution.py:50
  84.4 18.5 %collective-permute-start.5 = (bf16[1,24,2304]{2,1,0:T(8,128)(2,1)S(1)}, bf16[1,24,2304]{2,1,0:T(8,128)(2,1)S(1)}, u32[]{:S(2)}, u32[]{:S(2)}) collective-permute-start(bf16[1,24,2304]{2,1,0:T(8,128)(2,1)S(1)} %maximum_bitcast_fusion.1), channel_id=1, source_target_pairs={{0,16},{2,18},{4,20},{6,22},{8,24},{10,26},{12,28},{14,30},{16,0},... | collective-permute-start | bytes 331784 | tf_op jit(solution)/shard_map/ppermute | solution.py:50
  106.1 18.5 %collective-permute-start.8 = (bf16[1,48,2304]{2,1,0:T(8,128)(2,1)S(1)}, bf16[1,48,2304]{2,1,0:T(8,128)(2,1)S(1)}, u32[]{:S(2)}, u32[]{:S(2)}) collective-permute-start(bf16[1,48,2304]{2,1,0:T(8,128)(2,1)S(1)} %bitcast.462), channel_id=1, source_target_pairs={{0,8},{2,10},{4,12},{6,14},{8,0},{10,2},{12,4},{14,6},{16,24},{18,... | collective-permute-start | bytes 663560 | tf_op jit(solution)/shard_map/ppermute | solution.py:50
  128.8 20.2 %collective-permute-start.11 = (bf16[1,96,2304]{2,1,0:T(8,128)(2,1)}, bf16[1,96,2304]{2,1,0:T(8,128)(2,1)}, u32[]{:S(2)}, u32[]{:S(2)}) collective-permute-start(bf16[1,96,2304]{2,1,0:T(8,128)(2,1)} %bitcast.45), channel_id=1, source_target_pairs={{0,4},{2,6},{4,0},{6,2},{8,12},{10,14},{12,8},{14,10},{16,20},{18,... | collective-permute-start | bytes 1327112 | tf_op jit(solution)/shard_map/ppermute | solution.py:50
  150.3 27.5 %collective-permute-start.12 = (bf16[1,192,2304]{2,1,0:T(8,128)(2,1)S(1)}, bf16[1,192,2304]{2,1,0:T(8,128)(2,1)}, u32[]{:S(2)}, u32[]{:S(2)}) collective-permute-start(bf16[1,192,2304]{2,1,0:T(8,128)(2,1)S(1)} %bitcast.421), channel_id=1, source_target_pairs={{0,1},{1,0},{2,3},{3,2},{4,5},{5,4},{6,7},{7,6},{8,9},{9,8},{10,11... | collective-permute-start | bytes 2654216 | tf_op jit(solution)/shard_map/ppermute | solution.py:50
  274.8 28.5 %collective-permute-start.18 = (bf16[4,384,768]{2,1,0:T(8,128)(2,1)}, bf16[4,384,768]{2,1,0:T(8,128)(2,1)S(1)}, u32[]{:S(2)}, u32[]{:S(2)}) collective-permute-start(bf16[4,384,768]{2,1,0:T(8,128)(2,1)} %bitcast.513), channel_id=1, source_target_pairs={{0,2},{2,0},{4,6},{6,4},{8,10},{10,8},{12,14},{14,12},{16,18},{18,... | collective-permute-start | bytes 7077896 | tf_op jit(solution)/shard_map/ppermute | solution.py:50
  280.8 22.6 %collective-permute-start.19 = (bf16[1,384,3072]{2,1,0:T(8,128)(2,1)}, bf16[1,384,3072]{2,1,0:T(8,128)(2,1)}, u32[]{:S(2)}, u32[]{:S(2)}) collective-permute-start(bf16[1,384,3072]{2,1,0:T(8,128)(2,1)} %bitcast.512), channel_id=1, source_target_pairs={{0,2},{2,0},{4,6},{6,4},{8,10},{10,8},{12,14},{14,12},{16,18},{18,... | collective-permute-start | bytes 7077896 | tf_op jit(solution)/shard_map/ppermute | solution.py:50
  317.9 16.9 %collective-permute-start.22 = (bf16[2,2,16,768]{3,2,1,0:T(8,128)(2,1)S(1)}, bf16[2,2,16,768]{3,2,1,0:T(8,128)(2,1)S(1)}, u32[]{:S(2)}, u32[]{:S(2)}) collective-permute-start(bf16[2,2,16,768]{3,2,1,0:T(8,128)(2,1)S(1)} %get-tuple-element.305), channel_id=1, source_target_pairs={{2,0},{4,2},{6,4},{8,6},{10,8},{12,10},{14,12},{16,14},{18,16},{20... | collective-permute-start | bytes 294920 | tf_op jit(solution)/shard_map/ppermute | solution.py:171
  345.3 35.3 %collective-permute-start.25 = (bf16[1,384,3072]{2,1,0:T(8,128)(2,1)}, bf16[1,384,3072]{2,1,0:T(8,128)(2,1)S(1)}, u32[]{:S(2)}, u32[]{:S(2)}) collective-permute-start(bf16[1,384,3072]{2,1,0:T(8,128)(2,1)} %bitcast.514), channel_id=1, source_target_pairs={{0,2},{2,0},{4,6},{6,4},{8,10},{10,8},{12,14},{14,12},{16,18},{18,... | collective-permute-start | bytes 7077896 | tf_op jit(solution)/shard_map/ppermute | solution.py:50
  349.3 28.3 %collective-permute-start.23 = (bf16[4,192,768]{2,1,0:T(8,128)(2,1)}, bf16[4,192,768]{2,1,0:T(8,128)(2,1)}, u32[]{:S(2)}, u32[]{:S(2)}) collective-permute-start(bf16[4,192,768]{2,1,0:T(8,128)(2,1)} %get-tuple-element.323), channel_id=1, source_target_pairs={{0,4},{2,6},{4,0},{6,2},{8,12},{10,14},{12,8},{14,10},{16,20},{18,... | collective-permute-start | bytes 3538952 | tf_op jit(solution)/shard_map/ppermute | solution.py:50
  351.2 29.4 %collective-permute-start.24 = (bf16[1,192,3072]{2,1,0:T(8,128)(2,1)S(1)}, bf16[1,192,3072]{2,1,0:T(8,128)(2,1)}, u32[]{:S(2)}, u32[]{:S(2)}) collective-permute-start(bf16[1,192,3072]{2,1,0:T(8,128)(2,1)S(1)} %bitcast.448), channel_id=1, source_target_pairs={{0,1},{1,0},{2,3},{3,2},{4,5},{5,4},{6,7},{7,6},{8,9},{9,8},{10,11... | collective-permute-start | bytes 3538952 | tf_op jit(solution)/shard_map/ppermute | solution.py:50
  388.1 17.4 %collective-permute-start.28 = (bf16[4,384,768]{2,1,0:T(8,128)(2,1)}, bf16[4,384,768]{2,1,0:T(8,128)(2,1)}, u32[]{:S(2)}, u32[]{:S(2)}) collective-permute-start(bf16[4,384,768]{2,1,0:T(8,128)(2,1)} %bitcast.89), channel_id=1, source_target_pairs={{0,2},{2,0},{4,6},{6,4},{8,10},{10,8},{12,14},{14,12},{16,18},{18,... | collective-permute-start | bytes 7077896 | tf_op jit(solution)/shard_map/ppermute | solution.py:50
  388.1 17.4 %collective-permute-start.29 = (bf16[1,384,3072]{2,1,0:T(8,128)(2,1)}, bf16[1,384,3072]{2,1,0:T(8,128)(2,1)S(1)}, u32[]{:S(2)}, u32[]{:S(2)}) collective-permute-start(bf16[1,384,3072]{2,1,0:T(8,128)(2,1)} %bitcast.90), channel_id=1, source_target_pairs={{0,2},{2,0},{4,6},{6,4},{8,10},{10,8},{12,14},{14,12},{16,18},{18,... | collective-permute-start | bytes 7077896 | tf_op jit(solution)/shard_map/ppermute | solution.py:50
  388.6 15.4 %collective-permute-start.26 = (bf16[4,96,768]{2,1,0:T(8,128)(2,1)}, bf16[4,96,768]{2,1,0:T(8,128)(2,1)S(1)}, u32[]{:S(2)}, u32[]{:S(2)}) collective-permute-start(bf16[4,96,768]{2,1,0:T(8,128)(2,1)} %get-tuple-element.335), channel_id=1, source_target_pairs={{0,1},{1,0},{2,3},{3,2},{4,5},{5,4},{6,7},{7,6},{8,9},{9,8},{10,11... | collective-permute-start | bytes 1769480 | tf_op jit(solution)/shard_map/ppermute | solution.py:50
  391.0 38.6 %collective-permute-start.32 = (bf16[1,192,3072]{2,1,0:T(8,128)(2,1)}, bf16[1,192,3072]{2,1,0:T(8,128)(2,1)S(1)}, u32[]{:S(2)}, u32[]{:S(2)}) collective-permute-start(bf16[1,192,3072]{2,1,0:T(8,128)(2,1)} %bitcast.88), channel_id=1, source_target_pairs={{0,8},{2,10},{4,12},{6,14},{8,0},{10,2},{12,4},{14,6},{16,24},{18,... | collective-permute-start | bytes 3538952 | tf_op jit(solution)/shard_map/ppermute | solution.py:50
  413.6 33.5 %collective-permute-start.33 = (bf16[4,192,768]{2,1,0:T(8,128)(2,1)}, bf16[4,192,768]{2,1,0:T(8,128)(2,1)S(1)}, u32[]{:S(2)}, u32[]{:S(2)}) collective-permute-start(bf16[4,192,768]{2,1,0:T(8,128)(2,1)} %get-tuple-element.358), channel_id=1, source_target_pairs={{0,4},{2,6},{4,0},{6,2},{8,12},{10,14},{12,8},{14,10},{16,20},{18,... | collective-permute-start | bytes 3538952 | tf_op jit(solution)/shard_map/ppermute | solution.py:50
  414.1 33.0 %collective-permute-start.34 = (bf16[1,192,3072]{2,1,0:T(8,128)(2,1)}, bf16[1,192,3072]{2,1,0:T(8,128)(2,1)S(1)}, u32[]{:S(2)}, u32[]{:S(2)}) collective-permute-start(bf16[1,192,3072]{2,1,0:T(8,128)(2,1)} %bitcast.103), channel_id=1, source_target_pairs={{0,1},{1,0},{2,3},{3,2},{4,5},{5,4},{6,7},{7,6},{8,9},{9,8},{10,11... | collective-permute-start | bytes 3538952 | tf_op jit(solution)/shard_map/ppermute | solution.py:50
  429.6 25.7 %collective-permute-start.36 = (bf16[2,2,128,768]{3,2,1,0:T(8,128)(2,1)S(1)}, bf16[2,2,128,768]{3,2,1,0:T(8,128)(2,1)S(1)}, u32[]{:S(2)}, u32[]{:S(2)}) collective-permute-start(bf16[2,2,128,768]{3,2,1,0:T(8,128)(2,1)S(1)} %get-tuple-element.364), channel_id=1, source_target_pairs={{2,0},{4,2},{6,4},{8,6},{10,8},{12,10},{14,12},{16,14},{18,16},{20... | collective-permute-start | bytes 2359304 | tf_op jit(solution)/shard_map/ppermute | solution.py:171
  462.9 15.6 %collective-permute-start.37 = (bf16[2,2,16,768]{3,2,1,0:T(8,128)(2,1)S(1)}, bf16[2,2,16,768]{3,2,1,0:T(8,128)(2,1)S(1)}, u32[]{:S(2)}, u32[]{:S(2)}) collective-permute-start(bf16[2,2,16,768]{3,2,1,0:T(8,128)(2,1)S(1)} %get-tuple-element.366), channel_id=1, source_target_pairs={{2,0},{4,2},{6,4},{8,6},{10,8},{12,10},{14,12},{16,14},{18,16},{20... | collective-permute-start | bytes 294920 | tf_op jit(solution)/shard_map/ppermute | solution.py:171
  466.6 29.2 %collective-permute-start.48 = (bf16[4,24,768]{2,1,0:T(8,128)(2,1)}, bf16[4,24,768]{2,1,0:T(8,128)(2,1)S(1)}, u32[]{:S(2)}, u32[]{:S(2)}) collective-permute-start(bf16[4,24,768]{2,1,0:T(8,128)(2,1)} %fusion.58), channel_id=1, source_target_pairs={{0,16},{2,18},{4,20},{6,22},{8,24},{10,26},{12,28},{14,30},{16,0},... | collective-permute-start | bytes 442376 | tf_op jit(solution)/shard_map/ppermute | solution.py:50
  478.4 17.5 %collective-permute-start.49 = (bf16[1,24,3072]{2,1,0:T(8,128)(2,1)}, bf16[1,24,3072]{2,1,0:T(8,128)(2,1)S(1)}, u32[]{:S(2)}, u32[]{:S(2)}) collective-permute-start(bf16[1,24,3072]{2,1,0:T(8,128)(2,1)} %fusion.59), channel_id=1, source_target_pairs={{0,16},{2,18},{4,20},{6,22},{8,24},{10,26},{12,28},{14,30},{16,0},... | collective-permute-start | bytes 442376 | tf_op jit(solution)/shard_map/ppermute | solution.py:50
  488.8 16.2 %collective-permute-start.50 = (bf16[1,96,3072]{2,1,0:T(8,128)(2,1)S(1)}, bf16[1,96,3072]{2,1,0:T(8,128)(2,1)S(1)}, u32[]{:S(2)}, u32[]{:S(2)}) collective-permute-start(bf16[1,96,3072]{2,1,0:T(8,128)(2,1)S(1)} %get-tuple-element.404), channel_id=1, source_target_pairs={{0,4},{2,6},{4,0},{6,2},{8,12},{10,14},{12,8},{14,10},{16,20},{18,... | collective-permute-start | bytes 1769480 | tf_op jit(solution)/shard_map/ppermute | solution.py:50
  490.8 16.2 %collective-permute-start.51 = (bf16[4,96,768]{2,1,0:T(8,128)(2,1)S(1)}, bf16[4,96,768]{2,1,0:T(8,128)(2,1)S(1)}, u32[]{:S(2)}, u32[]{:S(2)}) collective-permute-start(bf16[4,96,768]{2,1,0:T(8,128)(2,1)S(1)} %get-tuple-element.405), channel_id=1, source_target_pairs={{0,1},{1,0},{2,3},{3,2},{4,5},{5,4},{6,7},{7,6},{8,9},{9,8},{10,11... | collective-permute-start | bytes 1769480 | tf_op jit(solution)/shard_map/ppermute | solution.py:50
  492.8 24.2 %collective-permute-start.52 = (bf16[1,96,3072]{2,1,0:T(8,128)(2,1)S(1)}, bf16[1,96,3072]{2,1,0:T(8,128)(2,1)S(1)}, u32[]{:S(2)}, u32[]{:S(2)}) collective-permute-start(bf16[1,96,3072]{2,1,0:T(8,128)(2,1)S(1)} %get-tuple-element.406), channel_id=1, source_target_pairs={{0,4},{2,6},{4,0},{6,2},{8,12},{10,14},{12,8},{14,10},{16,20},{18,... | collective-permute-start | bytes 1769480 | tf_op jit(solution)/shard_map/ppermute | solution.py:50
  495.8 27.6 %collective-permute-start.40 = (bf16[1,192,1664]{2,1,0:T(8,128)(2,1)S(1)}, bf16[1,192,1664]{2,1,0:T(8,128)(2,1)S(1)}, u32[]{:S(2)}, u32[]{:S(2)}) collective-permute-start(bf16[1,192,1664]{2,1,0:T(8,128)(2,1)S(1)} %bitcast.467), channel_id=1, source_target_pairs={{0,1},{1,0},{2,3},{3,2},{4,5},{5,4},{6,7},{7,6},{8,9},{9,8},{10,11... | collective-permute-start | bytes 1916936 | tf_op jit(solution)/shard_map/ppermute | solution.py:50
  495.9 27.5 %collective-permute-start.41 = (bf16[1,192,1536]{2,1,0:T(8,128)(2,1)S(1)}, bf16[1,192,1536]{2,1,0:T(8,128)(2,1)S(1)}, u32[]{:S(2)}, u32[]{:S(2)}) collective-permute-start(bf16[1,192,1536]{2,1,0:T(8,128)(2,1)S(1)} %bitcast.468), channel_id=1, source_target_pairs={{0,8},{2,10},{4,12},{6,14},{8,0},{10,2},{12,4},{14,6},{16,24},{18,... | collective-permute-start | bytes 1769480 | tf_op jit(solution)/shard_map/ppermute | solution.py:50
  535.8 16.4 %collective-permute-start.57 = (bf16[4,24,768]{2,1,0:T(8,128)(2,1)S(1)}, bf16[4,24,768]{2,1,0:T(8,128)(2,1)S(1)}, u32[]{:S(2)}, u32[]{:S(2)}) collective-permute-start(bf16[4,24,768]{2,1,0:T(8,128)(2,1)S(1)} %fusion.63), channel_id=1, source_target_pairs={{0,16},{2,18},{4,20},{6,22},{8,24},{10,26},{12,28},{14,30},{16,0},... | collective-permute-start | bytes 442376 | tf_op jit(solution)/shard_map/ppermute | solution.py:50
  536.9 17.7 %collective-permute-start.58 = (bf16[1,24,3072]{2,1,0:T(8,128)(2,1)S(1)}, bf16[1,24,3072]{2,1,0:T(8,128)(2,1)S(1)}, u32[]{:S(2)}, u32[]{:S(2)}) collective-permute-start(bf16[1,24,3072]{2,1,0:T(8,128)(2,1)S(1)} %fusion.64), channel_id=1, source_target_pairs={{0,16},{2,18},{4,20},{6,22},{8,24},{10,26},{12,28},{14,30},{16,0},... | collective-permute-start | bytes 442376 | tf_op jit(solution)/shard_map/ppermute | solution.py:50
  538.9 21.9 %collective-permute-start.44 = (bf16[1,48,1664]{2,1,0:T(8,128)(2,1)S(1)}, bf16[1,48,1664]{2,1,0:T(8,128)(2,1)S(1)}, u32[]{:S(2)}, u32[]{:S(2)}) collective-permute-start(bf16[1,48,1664]{2,1,0:T(8,128)(2,1)S(1)} %bitcast.497), channel_id=1, source_target_pairs={{0,8},{2,10},{4,12},{6,14},{8,0},{10,2},{12,4},{14,6},{16,24},{18,... | collective-permute-start | bytes 479240 | tf_op jit(solution)/shard_map/ppermute | solution.py:50
  539.8 21.0 %collective-permute-start.45 = (bf16[1,48,1536]{2,1,0:T(8,128)(2,1)S(1)}, bf16[1,48,1536]{2,1,0:T(8,128)(2,1)S(1)}, u32[]{:S(2)}, u32[]{:S(2)}) collective-permute-start(bf16[1,48,1536]{2,1,0:T(8,128)(2,1)S(1)} %get-tuple-element.396), channel_id=1, source_target_pairs={{0,1},{1,0},{2,3},{3,2},{4,5},{5,4},{6,7},{7,6},{8,9},{9,8},{10,11... | collective-permute-start | bytes 442376 | tf_op jit(solution)/shard_map/ppermute | solution.py:50
  (141 other events, 1297.4 us)
Sparse Core Ops, SparseCore 0:
  24.3 96.0 all-gather.2
  123.2 100.9 all-gather.4

commit v3 on v2

--- a/solution.py
+++ b/solution.py
@@ -188,17 +188,19 @@
 def rims_return(rim_low, rim_up, pooled_own):
     size = pooled_own.shape[2]
     hops = pooled_hops(size)
-    far_low, far_up = rim_low[:, :, WIN:], rim_up[:, :, WIN:]
+    if hops == 1:
+        second = passed_along(rim_low[:, :, WIN : WIN + 16], -2)
+        return tied([passed_along(rim_up, 1), passed_along(rim_low, -1), second]) + [pooled_own]
+    far_low, far_up = rim_low[:, :, WIN : WIN + REACH], rim_up[:, :, WIN:]
     for hop in range(2, hops + 1):
         start = REACH - hop * size
         pooled_own = pooled_own + passed_along(far_low[:, :, start : start + size], -hop).astype(f32)
         start = (hop - 1) * size
         pooled_own = pooled_own + passed_along(far_up[:, :, start : start + size], hop).astype(f32)
-    if hops > 1:
-        near_low, near_up = rim_low[:, :, :WIN], rim_up[:, :, :WIN]
-        rim_low = jnp.concatenate([near_low, far_low[:, :, REACH - size :]], axis=2)
-        rim_up = jnp.concatenate([near_up, far_up[:, :, :size]], axis=2)
-    return passed_along(rim_up, 1), passed_along(rim_low, -1), pooled_own
+    near_low, near_up = rim_low[:, :, :WIN], rim_up[:, :, :WIN]
+    rim_low = jnp.concatenate([near_low, far_low[:, :, REACH - size :]], axis=2)
+    rim_up = jnp.concatenate([near_up, far_up[:, :, :size]], axis=2)
+    return passed_along(rim_up, 1), passed_along(rim_low, -1), None, pooled_own
 
 
 def dot_nt(a, b):
@@ -321,7 +323,8 @@
             up_ref[kind, 0, :WIN, at] = rows[WIN + length :].astype(bf16)
             far = far_totals[kind]
             pool_ref[kind, 0, :, at] = far[REACH : far.shape[0] - REACH]
-            low_ref[kind, 0, WIN:, at] = far[:REACH].astype(bf16)
+            low_ref[kind, 0, WIN : WIN + REACH, at] = far[:REACH].astype(bf16)
+            low_ref[kind, 0, WIN + REACH :, at] = far[REACH : REACH + 16].astype(bf16)
             up_ref[kind, 0, WIN:, at] = far[far.shape[0] - REACH :].astype(bf16)
 
 
@@ -392,7 +395,7 @@
     in_specs = [stat, spec(length, 0)] + specs
     out_specs = [
         spec(length, 0), pair_spec(length), pair_spec(pooled),
-        pair_spec(WIN + REACH), pair_spec(WIN + REACH),
+        pair_spec(WIN + REACH + 16), pair_spec(WIN + REACH),
     ]
     out_specs = [moved(block) for block in out_specs[:1]] + [
         pl.BlockSpec(
@@ -415,7 +418,7 @@
             jax.ShapeDtypeStruct((every, length, width), bf16),
             jax.ShapeDtypeStruct((2, every, length, width), f32),
             jax.ShapeDtypeStruct((2, every, pooled, width), f32),
-            jax.ShapeDtypeStruct((2, every, WIN + REACH, width), bf16),
+            jax.ShapeDtypeStruct((2, every, WIN + REACH + 16, width), bf16),
             jax.ShapeDtypeStruct((2, every, WIN + REACH, width), bf16),
         ],
         input_output_aliases={kernel_inputs + i: i for i in range(len(before))},
@@ -492,15 +495,16 @@
 
 
 def pool_back_kernel(select_ref, spread_ref, kernel_ref, rows_ref, low_rows_ref, own_ref, pool_ref,
-                     low_ref, up_ref, grad_ref, tail_ref, taps_ref):
+                     low_ref, up_ref, *rest):
+    *rims, grad_ref, tail_ref, taps_ref = rest if len(rest) == 3 else (*rest[:3], None, rest[3])
     pooled = pool_ref.shape[2]
     length = rows_ref.shape[1]
     tap_row = lax.broadcasted_iota(jnp.int32, (8, LANES), 0)
     tail_row = lax.broadcasted_iota(jnp.int32, (16, LANES), 0)
     taps_total = jnp.zeros((8, LANES), f32)
     for group in range(rows_ref.shape[0]):
-        grads = pool_ref[0, group] + low_ref[0, group, WIN:].astype(f32)
-        grads = (grads + up_ref[0, group, WIN:].astype(f32)).astype(bf16).astype(f32)
+        grads = pool_ref[0, group] + low_ref[0, group, WIN : WIN + pooled].astype(f32)
+        grads = (grads + up_ref[0, group, WIN : WIN + pooled].astype(f32)).astype(bf16).astype(f32)
         taps = dot_nn(select_ref[...], rows_ref[group])
         low_rows = low_rows_ref[group].astype(f32)
         edge = grads[0:1]
@@ -515,16 +519,29 @@
         high = spread.astype(bf16)
         rest = (spread - high.astype(f32)).astype(bf16)
         total = own_ref[0, group] + dot_nn(spread_ref[...], high) + dot_nn(spread_ref[...], rest)
-        grad_ref[0, group] = total
-        grad_ref[0, group, :WIN] = total[:WIN] + low_ref[0, group, :WIN].astype(f32)
-        grad_ref[0, group, length - WIN :] = total[length - WIN :] + up_ref[0, group, :WIN].astype(f32)
-        tail = jnp.where(tail_row == 14, edge * kernel_ref[0, 0:1, :], 0.0)
-        tail = tail + jnp.where(tail_row == 15, edge * kernel_ref[0, 1:2, :], 0.0)
-        tail_ref[0, group] = tail.astype(bf16)
+        first, last = kernel_ref[0, 0:1, :], kernel_ref[0, 1:2, :]
+        if rims:
+            mine_ref, second_ref = rims
+            edge = up_ref[0, group, WIN + pooled : WIN + pooled + 1].astype(f32)
+            edge = edge + mine_ref[0, group, 0:1].astype(f32) + second_ref[0, group, 0:1].astype(f32)
+            edge = edge.astype(bf16).astype(f32)
+        tail = jnp.where(tail_row == 14, edge * first, 0.0)
+        tail = tail + jnp.where(tail_row == 15, edge * last, 0.0)
+        kind = grad_ref.dtype
+        upper = total[length - WIN :] + up_ref[0, group, :WIN].astype(f32)
+        if length > 2 * WIN:
+            grad_ref[0, group, WIN : length - WIN] = total[WIN : length - WIN].astype(kind)
+        grad_ref[0, group, :WIN] = (total[:WIN] + low_ref[0, group, :WIN].astype(f32)).astype(kind)
+        if rims:
+            grad_ref[0, group, length - WIN : length - 16] = upper[: WIN - 16].astype(kind)
+            grad_ref[0, group, length - 16 :] = (upper[WIN - 16 :] + tail).astype(kind)
+        else:
+            grad_ref[0, group, length - WIN :] = upper.astype(kind)
+            tail_ref[0, group] = tail.astype(bf16)
     taps_ref[0] = taps_total
 
 
-def pool_back(select, kernel, qkv, rows_low, own, pooled_own, from_low, from_up):
+def pool_back(select, kernel, qkv, rows_low, own, pooled_own, from_low, from_up, rim_up, second):
     count, length, width = own.shape[1:]
     groups = width // LANES
     pooled = length // 4
@@ -532,6 +549,13 @@
     def pair_spec(rows):
         return pl.BlockSpec((1, count, rows, LANES), lambda j: (j // groups, 0, 0, j % groups))
 
+    joined = second is not None
+    tail_shape = jax.ShapeDtypeStruct((2, count, 16, width), bf16)
+    tail_specs, tail_shapes = ([], []) if joined else ([pair_spec(16)], [tail_shape])
+    rim_spec = pl.BlockSpec(
+        (1, count, 16, LANES), lambda j: (j // groups, 0, WIN // 16, j % groups)
+    )
+    extra_specs, extra = ([rim_spec, pair_spec(16)], [rim_up, second]) if joined else ([], [])
     return pl.pallas_call(
         pool_back_kernel,
         grid=(2 * groups,),
@@ -543,14 +567,13 @@
             pl.BlockSpec((count, 16, LANES), lambda j: (0, WIN // 16 - 1, j)),
             pair_spec(length), pair_spec(pooled),
             pair_spec(from_low.shape[2]), pair_spec(from_up.shape[2]),
-        ],
-        out_specs=[
-            pair_spec(length), pair_spec(16),
+        ] + extra_specs,
+        out_specs=[pair_spec(length)] + tail_specs + [
             pl.BlockSpec((1, 8, LANES), lambda j: (j // groups, 0, j % groups)),
         ],
         out_shape=[
-            jax.ShapeDtypeStruct((2, count, length, width), f32),
-            jax.ShapeDtypeStruct((2, count, 16, width), bf16),
+            jax.ShapeDtypeStruct((2, count, length, width), bf16 if joined else f32),
+            *tail_shapes,
             jax.ShapeDtypeStruct((2, 8, width), f32),
         ],
         compiler_params=pltpu.CompilerParams(vmem_limit_bytes=VMEM_LIMIT),
@@ -558,7 +581,7 @@
             flops=count * length * width * 4000, bytes_accessed=9000000, transcendentals=0
         ),
         name="pool_back",
-    )(select, select.T, kernel, qkv, rows_low, own, pooled_own, from_low, from_up)
+    )(select, select.T, kernel, qkv, rows_low, own, pooled_own, from_low, from_up, *extra)
 
 
 def matmul(a, b):
@@ -1066,13 +1089,15 @@
     grad_query, own, pooled_own, rim_low, rim_up = pieces
     rim_up = at("rims", rim_up)
     grad_query = grad_query.reshape(rows, width)
-    from_low, from_up, pooled_own = rims_return(rim_low, rim_up, pooled_own)
-    own, tail, taps = pool_back(
-        select, small["taps"], operands[0], operands[3], own, pooled_own, from_low, from_up
+    from_low, from_up, second, pooled_own = rims_return(rim_low, rim_up, pooled_own)
+    own, *tail, taps = pool_back(
+        select, small["taps"], operands[0], operands[3], own, pooled_own, from_low, from_up,
+        rim_up, second,
     )
-    tail = passed_along(tail, -1).astype(f32)
+    if tail:
+        tail = passed_along(tail[0], -1).astype(f32)
+        own = own + jnp.pad(tail, ((0, 0), (0, 0), (length - 16, 0), (0, 0)))
     own = at("pooled", own, (x_low, grad_query, mixed, attention_low))
-    own = own + jnp.pad(tail, ((0, 0), (0, 0), (length - 16, 0), (0, 0)))
     own = own.astype(bf16).reshape(2, rows, width)
     grad_qkv = (grad_query, own[0], own[1])
     grad_x = grad_one + matmul_t(jnp.concatenate(grad_qkv, axis=1), qkv_weight)

time: 597 us -> 587 us (0.983)
  waiting for transfers between devices: 177 us -> 166 us
    ppermute x14, waiting for transfers between devices: 22 us -> 12.8 us  [passed_along(): return lax.ppermute(value, 'seq', pairs)]
    unnamed x241 -> x237, local copies, waits for them, and re-layouts: 21.8 us -> 20.2 us
  transfers between devices with their start and end apart: 61 -> 61, of which waited for: 30 -> 28; matrix products, arithmetic and copies ran while one was open for 10% -> 10% of each run, Pallas kernels for 21% -> 22%
where the time goes in v3:
time: 587 us; the launch traced here: 578 us
  Pallas kernels  174 us (30%)
  waiting for transfers between devices  166 us (28%)
  starting transfers between devices  116 us (20%)
  other arithmetic  53.4 us (9%)
  local copies, waits for them, and re-layouts  37.4 us (6%)
  between operations  16.7 us (3%)
  matrix products  15.2 us (3%)
    ppermute x45, waiting for transfers between devices, exchange(): return lax.ppermute(value, axis, pairs)  153 us
    ppermute x45, starting transfers between devices, exchange(): return lax.ppermute(value, axis, pairs)  84.4 us
    pallas_call x4, Pallas kernels, attend_back(): pl.pallas_call(kernel, grid=(count, groups), in_specs=mask_specs + [moved...  42 us
    pallas_call x2, Pallas kernels, feed_back(): pl.pallas_call(functools.partial(feed_back_kernel, blocks), grid_spec=plt...  41.5 us
    convert_element_type x30, other arithmetic, land(): (keep[:, side].astype(f32) + got[:, side].astype(f32)).astype(bf16)  31.9 us
    ppermute x14, starting transfers between devices, passed_along(): return lax.ppermute(value, 'seq', pairs)  31.3 us
    pallas_call x2, Pallas kernels, feed_forward(): pl.pallas_call(feed_kernel, grid=(ratio,), in_specs=[rows, rows, pl.Block...  29.4 us
    pallas_call x2, Pallas kernels, attend(): pl.pallas_call(attend_kernel, grid=(count, groups), in_specs=mask_specs +...  21.6 us
  transfers between devices with their start and end apart: 61, of which 28 were waited for; matrix products, arithmetic and copies ran while one was open for 10% of the time, Pallas kernels for 22%

profile of v3, /device:TPU:0, one launch (start us, length us, event | category | flops | bytes accessed | tf_op | source)
XLA Modules:
  0.0 578.3 jit_solution(6075423216515838216)
XLA Ops:
  15.0 5.6 collective-permute-done
  25.0 6.2 %collective-permute-done.1 = bf16[1,48,2432]{2,1,0:T(8,128)(2,1)S(1)} collective-permute-done((bf16[1,48,2432]{2,1,0:T(8,128)(2,1)S(1)}, bf16[1,48,2432]{2,1,0:T(8,128)(2,1)S(1)}, u32[]{:S(2)}, u32[]{:S(2)}) %collective-permute-start.1) | collective-permute-done | bytes 233504 | tf_op jit(solution)/shard_map/ppermute | solution.py:50
  32.5 12.1 %collective-permute-done.2 = bf16[1,96,2432]{2,1,0:T(8,128)(2,1)S(1)} collective-permute-done((bf16[1,96,2432]{2,1,0:T(8,128)(2,1)S(1)}, bf16[1,96,2432]{2,1,0:T(8,128)(2,1)S(1)}, u32[]{:S(2)}, u32[]{:S(2)}) %collective-permute-start.2) | collective-permute-done | bytes 466976 | tf_op jit(solution)/shard_map/ppermute | solution.py:50
  49.6 23.6 %collective-permute-done.3 = bf16[1,192,2432]{2,1,0:T(8,128)(2,1)S(1)} collective-permute-done((bf16[1,192,2432]{2,1,0:T(8,128)(2,1)S(1)}, bf16[1,192,2432]{2,1,0:T(8,128)(2,1)S(1)}, u32[]{:S(2)}, u32[]{:S(2)}) %collective-permute-start.3) | collective-permute-done | bytes 933920 | tf_op jit(solution)/shard_map/ppermute | solution.py:50
  84.4 5.4 collective-permute-start.5
  94.1 8.8 %collective-permute-done.5 = bf16[1,24,2304]{2,1,0:T(8,128)(2,1)S(1)} collective-permute-done((bf16[1,24,2304]{2,1,0:T(8,128)(2,1)S(1)}, bf16[1,24,2304]{2,1,0:T(8,128)(2,1)S(1)}, u32[]{:S(2)}, u32[]{:S(2)}) %collective-permute-start.5) | collective-permute-done | bytes 110624 | tf_op jit(solution)/shard_map/ppermute | solution.py:50
  112.8 11.7 %collective-permute-done.8 = bf16[1,48,2304]{2,1,0:T(8,128)(2,1)S(1)} collective-permute-done((bf16[1,48,2304]{2,1,0:T(8,128)(2,1)S(1)}, bf16[1,48,2304]{2,1,0:T(8,128)(2,1)S(1)}, u32[]{:S(2)}, u32[]{:S(2)}) %collective-permute-start.8) | collective-permute-done | bytes 221216 | tf_op jit(solution)/shard_map/ppermute | solution.py:50
  133.7 11.1 %attend.2 = (bf16[2,256,768]{2,1,0:T(8,128)(2,1)S(1)}, f32[2,3,8,256]{3,2,1,0:T(8,128)S(1)}) custom-call(f32[2,256,256]{2,1,0:T(8,128)S(1)} %pad_maximum_fusion.8.near_ref.refs_0_, f32[2,192,256]{2,1,0:T(8,128)S(1)} %copy-done.4, bf16[2,256,2304]{2,1,0:T(8,128)(2,1)S(1)} %bitcast.355, bf16[2,256,2304]{2,1,0:T(8,128)(2,1)S(1)} %bitcast.356, ...), custom_call_target="tpu_custom_call" | custom-call | flops 786432000 | bytes 8000000 | tf_op jit(solution)/shard_map/attend/pallas_call | solution.py:366
  154.7 14.7 %feed_forward.2 = (f32[512,768]{1,0:T(8,128)S(1)}, f32[512,1]{1,0:T(8,128)S(1)}, bf16[512,768]{1,0:T(8,128)(2,1)S(1)}, bf16[512,3072]{1,0:T(8,128)(2,1)}, bf16[5...) custom-call(f32[512,768]{1,0:T(8,128)} %bitcast_convert_fusion.x_ref, ...), custom_call_target="tpu_custom_call" | custom-call | flops 5435817984 | bytes 24772608 | tf_op jit(solution)/shard_map/feed_forward/pallas_call | solution.py:798
  170.5 7.4 %collective-permute-done.12 = bf16[1,192,2304]{2,1,0:T(8,128)(2,1)} collective-permute-done((bf16[1,192,2304]{2,1,0:T(8,128)(2,1)S(1)}, bf16[1,192,2304]{2,1,0:T(8,128)(2,1)}, u32[]{:S(2)}, u32[]{:S(2)}) %collective-permute-start.12) | collective-permute-done | bytes 884768 | tf_op jit(solution)/shard_map/ppermute | solution.py:50
  197.7 7.1 %collective-permute-done.15.ku_ref.vu_ref.refs_9_.refs_10_ = bf16[2,64,1536]{2,1,0:T(8,128)(2,1)S(1)} collective-permute-done((bf16[2,64,1536]{2,1,0:T(8,128)(2,1)S(1)}, bf16[2,64,1536]{2,1,0:T(8,128)(2,1)S(1)}, u32[]{:S(2)}, u32[]{:S(2)}) %collective-permute-start.15) | collective-permute-done | bytes 393248 | tf_op jit(solution)/shard_map/ppermute | solution.py:171
  206.6 10.1 %collective-permute-start.16 = (bf16[2,64,1536]{2,1,0:T(8,128)(2,1)S(1)}, bf16[2,64,1536]{2,1,0:T(8,128)(2,1)S(1)}, u32[]{:S(2)}, u32[]{:S(2)}) collective-permute-start(bf16[2,64,1536]{2,1,0:T(8,128)(2,1)S(1)} %pool.3.pk_ref.pv_ref.refs_11_.refs_12_), channel_id=1, source_target_pairs={{0,2},{2,4},{4,6},{6,8},{8,10},{10,12},{12,14},{14,16},{16,18},{18... | collective-permute-start | bytes 1179656 | tf_op jit(solution)/shard_map/ppermute | solution.py:171
  222.3 10.5 %attend.3 = (bf16[2,256,768]{2,1,0:T(8,128)(2,1)S(1)}, f32[2,3,8,256]{3,2,1,0:T(8,128)S(1)}) custom-call(f32[2,256,256]{2,1,0:T(8,128)S(1)} %pad_maximum_fusion.8.near_ref.refs_0_, f32[2,192,256]{2,1,0:T(8,128)S(1)} %copy-done.5, bf16[2,256,2304]{2,1,0:T(8,128)(2,1)S(1)} %bitcast.367, bf16[2,256,2304]{2,1,0:T(8,128)(2,1)S(1)} %bitcast.368, ...), custom_call_target="tpu_custom_call" | custom-call | flops 786432000 | bytes 8000000 | tf_op jit(solution)/shard_map/attend/pallas_call | solution.py:366
  236.2 14.8 %feed_forward.3 = (f32[512,768]{1,0:T(8,128)S(1)}, f32[512,1]{1,0:T(8,128)S(1)}, bf16[512,768]{1,0:T(8,128)(2,1)S(1)}, bf16[512,3072]{1,0:T(8,128)(2,1)}, bf16[5...) custom-call(f32[512,768]{1,0:T(8,128)} %get-tuple-element.273.x_ref, ...), custom_call_target="tpu_custom_call" | custom-call | flops 5435817984 | bytes 24772608 | tf_op jit(solution)/shard_map/feed_forward/pallas_call | solution.py:798
  253.4 20.7 %feed_back.2 = (f32[512,768]{1,0:T(8,128)S(1)}, bf16[512,768]{1,0:T(8,128)(2,1)S(1)}, bf16[512,768]{1,0:T(8,128)(2,1)S(1)}, f32[8,768]{1,0:T(8,128)S(1)}, f32[1,...) custom-call(s32[1]{0:T(128)} %bitcast.32.index_ref, ...), custom_call_target="tpu_custom_call" | custom-call | flops 10267656192 | bytes 35389440 | tf_op jit(solution)/shard_map/feed_back/pallas_call | solution.py:909
  274.0 6.0 %collective-permute-start.18 = (bf16[4,384,768]{2,1,0:T(8,128)(2,1)}, bf16[4,384,768]{2,1,0:T(8,128)(2,1)}, u32[]{:S(2)}, u32[]{:S(2)}) collective-permute-start(bf16[4,384,768]{2,1,0:T(8,128)(2,1)} %bitcast.515), channel_id=1, source_target_pairs={{0,2},{2,0},{4,6},{6,4},{8,10},{10,8},{12,14},{14,12},{16,18},{18,... | collective-permute-start | bytes 7077896 | tf_op jit(solution)/shard_map/ppermute | solution.py:50
  280.3 10.9 %attend_back.4 = (bf16[2,256,768]{2,1,0:T(8,128)(2,1)S(1)}, f32[2,2,256,768]{3,2,1,0:T(8,128)}, f32[2,2,64,768]{3,2,1,0:T(8,128)S(1)}, bf16[2,2,144,768]{3,2,1,0:T(8,128)(2,1)}, bf16[2,2,128,768]{3,2,1,0:T(8,128)(2,1)S(1)}) custom-call(f32[2,256,256]{2,1,0:T(8,128)S(1)} %pad_maximum_fusion.8.near_ref.refs_0_, f32[2,192,256]{2,1,0:T(8,128)S(1)} %copy-done.6, ...), custom_call_target="tpu_custom_call" | custom-call | flops 983040000 | bytes 6000000 | tf_op jit(solution)/shard_map/attend_back/pallas_call | solution.py:411
  291.1 10.3 %attend_back.5 = (bf16[2,256,768]{2,1,0:T(8,128)(2,1)S(1)}, f32[2,2,256,768]{3,2,1,0:T(8,128)}, f32[2,2,64,768]{3,2,1,0:T(8,128)S(1)}, bf16[2,2,144,768]{3,2,1,0:T(8,128)(2,1)}, bf16[2,2,128,768]{3,2,1,0:T(8,128)(2,1)S(1)}) custom-call(f32[2,256,256]{2,1,0:T(8,128)S(1)} %pad_maximum_fusion.8, ...), custom_call_target="tpu_custom_call", output_to_operand_aliasing={{0}: (17, {}), {1}: (18, {}), {2}: (19, {}), {3}: (20, {}),... | custom-call | flops 983040000 | bytes 6000000 | tf_op jit(solution)/shard_map/attend_back/pallas_call | solution.py:411
  319.3 6.1 %pool_back.2 = (bf16[2,2,256,768]{3,2,1,0:T(8,128)(2,1)S(1)}, f32[2,8,768]{2,1,0:T(8,128)S(1)}) custom-call(bf16[320,256]{1,0:T(8,128)(2,1)S(1)} %fusion.41.select_ref, bf16[256,320]{1,0:T(8,128)(2,1)S(1)} %fusion.38.spread_ref, f32[2,8,768]{2,1,0:T(8,128)S(1)} %pad_maximum_fusion.19.kernel_ref, bf16[2,256,2304]{2,1,0:T(8,128)(2,1)} %bitcast.376, ...), custom_call_target="tpu_custom_call" | custom-call | flops 1572864000 | bytes 9000000 | tf_op jit(solution)/shard_map/pool_back/pallas_call | solution.py:559
  330.3 5.1 weight_grads.3
  335.4 8.6 %collective-permute-start.25 = (bf16[1,384,3072]{2,1,0:T(8,128)(2,1)}, bf16[1,384,3072]{2,1,0:T(8,128)(2,1)S(1)}, u32[]{:S(2)}, u32[]{:S(2)}) collective-permute-start(bf16[1,384,3072]{2,1,0:T(8,128)(2,1)} %bitcast.516), channel_id=1, source_target_pairs={{0,2},{2,0},{4,6},{6,4},{8,10},{10,8},{12,14},{14,12},{16,18},{18,... | collective-permute-start | bytes 7077896 | tf_op jit(solution)/shard_map/ppermute | solution.py:50
  347.7 20.8 %feed_back.3 = (f32[512,768]{1,0:T(8,128)S(1)}, bf16[512,768]{1,0:T(8,128)(2,1)S(1)}, bf16[512,768]{1,0:T(8,128)(2,1)S(1)}, f32[8,768]{1,0:T(8,128)S(1)}, f32[1,...) custom-call(s32[1]{0:T(128)} %bitcast.32.index_ref, ...), custom_call_target="tpu_custom_call" | custom-call | flops 10267656192 | bytes 35389440 | tf_op jit(solution)/shard_map/feed_back/pallas_call | solution.py:909
  388.8 10.4 %attend_back.6 = (bf16[2,256,768]{2,1,0:T(8,128)(2,1)S(1)}, f32[2,2,256,768]{3,2,1,0:T(8,128)}, f32[2,2,64,768]{3,2,1,0:T(8,128)S(1)}, bf16[2,2,144,768]{3,2,1,0:T(8,128)(2,1)}, bf16[2,2,128,768]{3,2,1,0:T(8,128)(2,1)S(1)}) custom-call(f32[2,256,256]{2,1,0:T(8,128)S(1)} %pad_maximum_fusion.8.near_ref.refs_0_, f32[2,192,256]{2,1,0:T(8,128)S(1)} %copy-done.6, ...), custom_call_target="tpu_custom_call" | custom-call | flops 983040000 | bytes 6000000 | tf_op jit(solution)/shard_map/attend_back/pallas_call | solution.py:411
  418.5 10.4 %attend_back.7 = (bf16[2,256,768]{2,1,0:T(8,128)(2,1)S(1)}, f32[2,2,256,768]{3,2,1,0:T(8,128)}, f32[2,2,64,768]{3,2,1,0:T(8,128)S(1)}, bf16[2,2,144,768]{3,2,1,0:T(8,128)(2,1)}, bf16[2,2,128,768]{3,2,1,0:T(8,128)(2,1)S(1)}) custom-call(f32[2,256,256]{2,1,0:T(8,128)S(1)} %pad_maximum_fusion.8, ...), custom_call_target="tpu_custom_call", output_to_operand_aliasing={{0}: (17, {}), {1}: (18, {}), {2}: (19, {}), {3}: (20, {}),... | custom-call | flops 983040000 | bytes 6000000 | tf_op jit(solution)/shard_map/attend_back/pallas_call | solution.py:411
  430.3 14.7 %collective-permute-done.33 = bf16[4,192,768]{2,1,0:T(8,128)(2,1)S(1)} collective-permute-done((bf16[4,192,768]{2,1,0:T(8,128)(2,1)}, bf16[4,192,768]{2,1,0:T(8,128)(2,1)S(1)}, u32[]{:S(2)}, u32[]{:S(2)}) %collective-permute-start.33) | collective-permute-done | bytes 1179680 | tf_op jit(solution)/shard_map/ppermute | solution.py:50
  455.1 7.4 %collective-permute-start.48 = (bf16[4,24,768]{2,1,0:T(8,128)(2,1)S(1)}, bf16[4,24,768]{2,1,0:T(8,128)(2,1)S(1)}, u32[]{:S(2)}, u32[]{:S(2)}) collective-permute-start(bf16[4,24,768]{2,1,0:T(8,128)(2,1)S(1)} %fusion.58), channel_id=1, source_target_pairs={{0,16},{2,18},{4,20},{6,22},{8,24},{10,26},{12,28},{14,30},{16,0},... | collective-permute-start | bytes 442376 | tf_op jit(solution)/shard_map/ppermute | solution.py:50
  464.7 5.9 %pool_back.3 = (bf16[2,2,256,768]{3,2,1,0:T(8,128)(2,1)S(1)}, f32[2,8,768]{2,1,0:T(8,128)S(1)}) custom-call(bf16[320,256]{1,0:T(8,128)(2,1)S(1)} %fusion.41.select_ref, bf16[256,320]{1,0:T(8,128)(2,1)S(1)} %fusion.38.spread_ref, f32[2,8,768]{2,1,0:T(8,128)S(1)} %pad_maximum_fusion.18.kernel_ref, bf16[2,256,2304]{2,1,0:T(8,128)(2,1)} %bitcast.364, ...), custom_call_target="tpu_custom_call" | custom-call | flops 1572864000 | bytes 9000000 | tf_op jit(solution)/shard_map/pool_back/pallas_call | solution.py:559
  488.4 7.7 %collective-permute-done.50 = bf16[1,96,3072]{2,1,0:T(8,128)(2,1)S(1)} collective-permute-done((bf16[1,96,3072]{2,1,0:T(8,128)(2,1)S(1)}, bf16[1,96,3072]{2,1,0:T(8,128)(2,1)S(1)}, u32[]{:S(2)}, u32[]{:S(2)}) %collective-permute-start.50) | collective-permute-done | bytes 589856 | tf_op jit(solution)/shard_map/ppermute | solution.py:50
  496.6 11.1 %collective-permute-done.52 = bf16[1,96,3072]{2,1,0:T(8,128)(2,1)S(1)} collective-permute-done((bf16[1,96,3072]{2,1,0:T(8,128)(2,1)S(1)}, bf16[1,96,3072]{2,1,0:T(8,128)(2,1)S(1)}, u32[]{:S(2)}, u32[]{:S(2)}) %collective-permute-start.52) | collective-permute-done | bytes 589856 | tf_op jit(solution)/shard_map/ppermute | solution.py:50
  531.6 8.4 %collective-permute-done.56 = bf16[1,24,3072]{2,1,0:T(8,128)(2,1)S(1)} collective-permute-done((bf16[1,24,3072]{2,1,0:T(8,128)(2,1)S(1)}, bf16[1,24,3072]{2,1,0:T(8,128)(2,1)S(1)}, u32[]{:S(2)}, u32[]{:S(2)}) %collective-permute-start.56) | collective-permute-done | bytes 147488 | tf_op jit(solution)/shard_map/ppermute | solution.py:50
  545.3 5.9 %units_back.1 = f32[48,3072]{1,0:T(8,128)} custom-call(bf16[4,384,1536]{2,1,0:T(8,128)(2,1)S(1)} %add_convert_fusion.spread_ref, f32[48,3072]{1,0:T(8,128)S(1)} %pad_maximum_fusion.6.refs_0_.refs_1_.refs_2_.refs_3_, f32[48,3072]{1,0:T(8,128)S(1)} %pad_maximum_fusion.6.refs_0_.refs_1_.refs_2_.refs_3_, ...), custom_call_target="tpu_custom_call" | custom-call | tf_op jit(solution)/shard_map/units_back/pallas_call | solution.py:976
  555.2 5.2 collective-permute-done.47
  (502 shorter events, 236.9 us)
Async XLA Ops:
  7.4 147.3 %all-gather.3.cloned.1.call-start = ((), (), s32[]{:S(2)}) async-start(), calls=%async_computation | async-start | bytes 10948608 | tf_op jit(solution)/shard_map/all_gather | solution.py:1182
  24.2 210.2 %all-gather.5.cloned.1.call-start = ((), (), s32[]{:S(2)}) async-start(), calls=%async_computation.1 | async-start | bytes 10948608 | tf_op jit(solution)/shard_map/all_gather | solution.py:1182
  48.2 25.0 %collective-permute-start.3 = (bf16[1,192,2432]{2,1,0:T(8,128)(2,1)S(1)}, bf16[1,192,2432]{2,1,0:T(8,128)(2,1)S(1)}, u32[]{:S(2)}, u32[]{:S(2)}) collective-permute-start(bf16[1,192,2432]{2,1,0:T(8,128)(2,1)S(1)} %bitcast.417), channel_id=1, source_target_pairs={{0,4},{2,6},{4,0},{6,2},{8,12},{10,14},{12,8},{14,10},{16,20},{18,... | collective-permute-start | bytes 2801672 | tf_op jit(solution)/shard_map/ppermute | solution.py:50
  84.4 18.5 %collective-permute-start.5 = (bf16[1,24,2304]{2,1,0:T(8,128)(2,1)S(1)}, bf16[1,24,2304]{2,1,0:T(8,128)(2,1)S(1)}, u32[]{:S(2)}, u32[]{:S(2)}) collective-permute-start(bf16[1,24,2304]{2,1,0:T(8,128)(2,1)S(1)} %maximum_bitcast_fusion.1), channel_id=1, source_target_pairs={{0,16},{2,18},{4,20},{6,22},{8,24},{10,26},{12,28},{14,30},{16,0},... | collective-permute-start | bytes 331784 | tf_op jit(solution)/shard_map/ppermute | solution.py:50
  106.1 18.5 %collective-permute-start.8 = (bf16[1,48,2304]{2,1,0:T(8,128)(2,1)S(1)}, bf16[1,48,2304]{2,1,0:T(8,128)(2,1)S(1)}, u32[]{:S(2)}, u32[]{:S(2)}) collective-permute-start(bf16[1,48,2304]{2,1,0:T(8,128)(2,1)S(1)} %bitcast.462), channel_id=1, source_target_pairs={{0,8},{2,10},{4,12},{6,14},{8,0},{10,2},{12,4},{14,6},{16,24},{18,... | collective-permute-start | bytes 663560 | tf_op jit(solution)/shard_map/ppermute | solution.py:50
  128.9 20.2 %collective-permute-start.11 = (bf16[1,96,2304]{2,1,0:T(8,128)(2,1)}, bf16[1,96,2304]{2,1,0:T(8,128)(2,1)}, u32[]{:S(2)}, u32[]{:S(2)}) collective-permute-start(bf16[1,96,2304]{2,1,0:T(8,128)(2,1)} %bitcast.45), channel_id=1, source_target_pairs={{0,4},{2,6},{4,0},{6,2},{8,12},{10,14},{12,8},{14,10},{16,20},{18,... | collective-permute-start | bytes 1327112 | tf_op jit(solution)/shard_map/ppermute | solution.py:50
  150.4 27.6 %collective-permute-start.12 = (bf16[1,192,2304]{2,1,0:T(8,128)(2,1)S(1)}, bf16[1,192,2304]{2,1,0:T(8,128)(2,1)}, u32[]{:S(2)}, u32[]{:S(2)}) collective-permute-start(bf16[1,192,2304]{2,1,0:T(8,128)(2,1)S(1)} %bitcast.421), channel_id=1, source_target_pairs={{0,1},{1,0},{2,3},{3,2},{4,5},{5,4},{6,7},{7,6},{8,9},{9,8},{10,11... | collective-permute-start | bytes 2654216 | tf_op jit(solution)/shard_map/ppermute | solution.py:50
  274.0 30.9 %collective-permute-start.18 = (bf16[4,384,768]{2,1,0:T(8,128)(2,1)}, bf16[4,384,768]{2,1,0:T(8,128)(2,1)}, u32[]{:S(2)}, u32[]{:S(2)}) collective-permute-start(bf16[4,384,768]{2,1,0:T(8,128)(2,1)} %bitcast.515), channel_id=1, source_target_pairs={{0,2},{2,0},{4,6},{6,4},{8,10},{10,8},{12,14},{14,12},{16,18},{18,... | collective-permute-start | bytes 7077896 | tf_op jit(solution)/shard_map/ppermute | solution.py:50
  280.1 24.8 %collective-permute-start.19 = (bf16[1,384,3072]{2,1,0:T(8,128)(2,1)}, bf16[1,384,3072]{2,1,0:T(8,128)(2,1)}, u32[]{:S(2)}, u32[]{:S(2)}) collective-permute-start(bf16[1,384,3072]{2,1,0:T(8,128)(2,1)} %bitcast.514), channel_id=1, source_target_pairs={{0,2},{2,0},{4,6},{6,4},{8,10},{10,8},{12,14},{14,12},{16,18},{18,... | collective-permute-start | bytes 7077896 | tf_op jit(solution)/shard_map/ppermute | solution.py:50
  301.4 17.9 %collective-permute-start.21 = (bf16[2,2,144,768]{3,2,1,0:T(8,128)(2,1)}, bf16[2,2,144,768]{3,2,1,0:T(8,128)(2,1)S(1)}, u32[]{:S(2)}, u32[]{:S(2)}) collective-permute-start(bf16[2,2,144,768]{3,2,1,0:T(8,128)(2,1)} %get-tuple-element.307), channel_id=1, source_target_pairs={{2,0},{4,2},{6,4},{8,6},{10,8},{12,10},{14,12},{16,14},{18,16},{20... | collective-permute-start | bytes 2654216 | tf_op jit(solution)/shard_map/ppermute | solution.py:171
  335.4 39.1 %collective-permute-start.25 = (bf16[1,384,3072]{2,1,0:T(8,128)(2,1)}, bf16[1,384,3072]{2,1,0:T(8,128)(2,1)S(1)}, u32[]{:S(2)}, u32[]{:S(2)}) collective-permute-start(bf16[1,384,3072]{2,1,0:T(8,128)(2,1)} %bitcast.516), channel_id=1, source_target_pairs={{0,2},{2,0},{4,6},{6,4},{8,10},{10,8},{12,14},{14,12},{16,18},{18,... | collective-permute-start | bytes 7077896 | tf_op jit(solution)/shard_map/ppermute | solution.py:50
  344.0 29.3 %collective-permute-start.23 = (bf16[4,192,768]{2,1,0:T(8,128)(2,1)}, bf16[4,192,768]{2,1,0:T(8,128)(2,1)}, u32[]{:S(2)}, u32[]{:S(2)}) collective-permute-start(bf16[4,192,768]{2,1,0:T(8,128)(2,1)} %get-tuple-element.329), channel_id=1, source_target_pairs={{0,4},{2,6},{4,0},{6,2},{8,12},{10,14},{12,8},{14,10},{16,20},{18,... | collective-permute-start | bytes 3538952 | tf_op jit(solution)/shard_map/ppermute | solution.py:50
  346.4 28.1 %collective-permute-start.24 = (bf16[1,192,3072]{2,1,0:T(8,128)(2,1)S(1)}, bf16[1,192,3072]{2,1,0:T(8,128)(2,1)S(1)}, u32[]{:S(2)}, u32[]{:S(2)}) collective-permute-start(bf16[1,192,3072]{2,1,0:T(8,128)(2,1)S(1)} %bitcast.447), channel_id=1, source_target_pairs={{0,1},{1,0},{2,3},{3,2},{4,5},{5,4},{6,7},{7,6},{8,9},{9,8},{10,11... | collective-permute-start | bytes 3538952 | tf_op jit(solution)/shard_map/ppermute | solution.py:50
  382.5 17.1 %collective-permute-start.28 = (bf16[4,384,768]{2,1,0:T(8,128)(2,1)}, bf16[4,384,768]{2,1,0:T(8,128)(2,1)S(1)}, u32[]{:S(2)}, u32[]{:S(2)}) collective-permute-start(bf16[4,384,768]{2,1,0:T(8,128)(2,1)} %bitcast.89), channel_id=1, source_target_pairs={{0,2},{2,0},{4,6},{6,4},{8,10},{10,8},{12,14},{14,12},{16,18},{18,... | collective-permute-start | bytes 7077896 | tf_op jit(solution)/shard_map/ppermute | solution.py:50
  382.5 17.1 %collective-permute-start.29 = (bf16[1,384,3072]{2,1,0:T(8,128)(2,1)}, bf16[1,384,3072]{2,1,0:T(8,128)(2,1)S(1)}, u32[]{:S(2)}, u32[]{:S(2)}) collective-permute-start(bf16[1,384,3072]{2,1,0:T(8,128)(2,1)} %bitcast.90), channel_id=1, source_target_pairs={{0,2},{2,0},{4,6},{6,4},{8,10},{10,8},{12,14},{14,12},{16,18},{18,... | collective-permute-start | bytes 7077896 | tf_op jit(solution)/shard_map/ppermute | solution.py:50
  383.0 16.2 %collective-permute-start.26 = (bf16[4,96,768]{2,1,0:T(8,128)(2,1)}, bf16[4,96,768]{2,1,0:T(8,128)(2,1)}, u32[]{:S(2)}, u32[]{:S(2)}) collective-permute-start(bf16[4,96,768]{2,1,0:T(8,128)(2,1)} %get-tuple-element.341), channel_id=1, source_target_pairs={{0,1},{1,0},{2,3},{3,2},{4,5},{5,4},{6,7},{7,6},{8,9},{9,8},{10,11... | collective-permute-start | bytes 1769480 | tf_op jit(solution)/shard_map/ppermute | solution.py:50
  384.9 44.0 %collective-permute-start.32 = (bf16[1,192,3072]{2,1,0:T(8,128)(2,1)}, bf16[1,192,3072]{2,1,0:T(8,128)(2,1)}, u32[]{:S(2)}, u32[]{:S(2)}) collective-permute-start(bf16[1,192,3072]{2,1,0:T(8,128)(2,1)} %bitcast.88), channel_id=1, source_target_pairs={{0,8},{2,10},{4,12},{6,14},{8,0},{10,2},{12,4},{14,6},{16,24},{18,... | collective-permute-start | bytes 3538952 | tf_op jit(solution)/shard_map/ppermute | solution.py:50
  409.9 35.1 %collective-permute-start.33 = (bf16[4,192,768]{2,1,0:T(8,128)(2,1)}, bf16[4,192,768]{2,1,0:T(8,128)(2,1)S(1)}, u32[]{:S(2)}, u32[]{:S(2)}) collective-permute-start(bf16[4,192,768]{2,1,0:T(8,128)(2,1)} %get-tuple-element.364), channel_id=1, source_target_pairs={{0,4},{2,6},{4,0},{6,2},{8,12},{10,14},{12,8},{14,10},{16,20},{18,... | collective-permute-start | bytes 3538952 | tf_op jit(solution)/shard_map/ppermute | solution.py:50
  410.6 34.4 %collective-permute-start.34 = (bf16[1,192,3072]{2,1,0:T(8,128)(2,1)}, bf16[1,192,3072]{2,1,0:T(8,128)(2,1)S(1)}, u32[]{:S(2)}, u32[]{:S(2)}) collective-permute-start(bf16[1,192,3072]{2,1,0:T(8,128)(2,1)} %bitcast.103), channel_id=1, source_target_pairs={{0,1},{1,0},{2,3},{3,2},{4,5},{5,4},{6,7},{7,6},{8,9},{9,8},{10,11... | collective-permute-start | bytes 3538952 | tf_op jit(solution)/shard_map/ppermute | solution.py:50
  428.9 33.7 %collective-permute-start.36 = (bf16[2,2,144,768]{3,2,1,0:T(8,128)(2,1)}, bf16[2,2,144,768]{3,2,1,0:T(8,128)(2,1)S(1)}, u32[]{:S(2)}, u32[]{:S(2)}) collective-permute-start(bf16[2,2,144,768]{3,2,1,0:T(8,128)(2,1)} %get-tuple-element.370), channel_id=1, source_target_pairs={{2,0},{4,2},{6,4},{8,6},{10,8},{12,10},{14,12},{16,14},{18,16},{20... | collective-permute-start | bytes 2654216 | tf_op jit(solution)/shard_map/ppermute | solution.py:171
  445.1 18.5 %collective-permute-start.35 = (bf16[2,2,128,768]{3,2,1,0:T(8,128)(2,1)S(1)}, bf16[2,2,128,768]{3,2,1,0:T(8,128)(2,1)S(1)}, u32[]{:S(2)}, u32[]{:S(2)}) collective-permute-start(bf16[2,2,128,768]{3,2,1,0:T(8,128)(2,1)S(1)} %get-tuple-element.369.rest_0_), channel_id=1, source_target_pairs={{0,2},{2,4},{4,6},{6,8},{8,10},{10,12},{12,14},{14,16},{16,18},{18... | collective-permute-start | bytes 2359304 | tf_op jit(solution)/shard_map/ppermute | solution.py:171
  455.1 31.1 %collective-permute-start.48 = (bf16[4,24,768]{2,1,0:T(8,128)(2,1)S(1)}, bf16[4,24,768]{2,1,0:T(8,128)(2,1)S(1)}, u32[]{:S(2)}, u32[]{:S(2)}) collective-permute-start(bf16[4,24,768]{2,1,0:T(8,128)(2,1)S(1)} %fusion.58), channel_id=1, source_target_pairs={{0,16},{2,18},{4,20},{6,22},{8,24},{10,26},{12,28},{14,30},{16,0},... | collective-permute-start | bytes 442376 | tf_op jit(solution)/shard_map/ppermute | solution.py:50
  462.6 24.3 %collective-permute-start.49 = (bf16[1,24,3072]{2,1,0:T(8,128)(2,1)S(1)}, bf16[1,24,3072]{2,1,0:T(8,128)(2,1)}, u32[]{:S(2)}, u32[]{:S(2)}) collective-permute-start(bf16[1,24,3072]{2,1,0:T(8,128)(2,1)S(1)} %fusion.59), channel_id=1, source_target_pairs={{0,16},{2,18},{4,20},{6,22},{8,24},{10,26},{12,28},{14,30},{16,0},... | collective-permute-start | bytes 442376 | tf_op jit(solution)/shard_map/ppermute | solution.py:50
  479.8 16.3 %collective-permute-start.50 = (bf16[1,96,3072]{2,1,0:T(8,128)(2,1)S(1)}, bf16[1,96,3072]{2,1,0:T(8,128)(2,1)S(1)}, u32[]{:S(2)}, u32[]{:S(2)}) collective-permute-start(bf16[1,96,3072]{2,1,0:T(8,128)(2,1)S(1)} %get-tuple-element.412), channel_id=1, source_target_pairs={{0,4},{2,6},{4,0},{6,2},{8,12},{10,14},{12,8},{14,10},{16,20},{18,... | collective-permute-start | bytes 1769480 | tf_op jit(solution)/shard_map/ppermute | solution.py:50
  481.9 25.8 %collective-permute-start.52 = (bf16[1,96,3072]{2,1,0:T(8,128)(2,1)S(1)}, bf16[1,96,3072]{2,1,0:T(8,128)(2,1)S(1)}, u32[]{:S(2)}, u32[]{:S(2)}) collective-permute-start(bf16[1,96,3072]{2,1,0:T(8,128)(2,1)S(1)} %get-tuple-element.414), channel_id=1, source_target_pairs={{0,4},{2,6},{4,0},{6,2},{8,12},{10,14},{12,8},{14,10},{16,20},{18,... | collective-permute-start | bytes 1769480 | tf_op jit(solution)/shard_map/ppermute | solution.py:50
  486.3 26.5 %collective-permute-start.40 = (bf16[1,192,1664]{2,1,0:T(8,128)(2,1)S(1)}, bf16[1,192,1664]{2,1,0:T(8,128)(2,1)S(1)}, u32[]{:S(2)}, u32[]{:S(2)}) collective-permute-start(bf16[1,192,1664]{2,1,0:T(8,128)(2,1)S(1)} %bitcast.467), channel_id=1, source_target_pairs={{0,1},{1,0},{2,3},{3,2},{4,5},{5,4},{6,7},{7,6},{8,9},{9,8},{10,11... | collective-permute-start | bytes 1916936 | tf_op jit(solution)/shard_map/ppermute | solution.py:50
  486.9 25.9 %collective-permute-start.41 = (bf16[1,192,1536]{2,1,0:T(8,128)(2,1)S(1)}, bf16[1,192,1536]{2,1,0:T(8,128)(2,1)S(1)}, u32[]{:S(2)}, u32[]{:S(2)}) collective-permute-start(bf16[1,192,1536]{2,1,0:T(8,128)(2,1)S(1)} %bitcast.468), channel_id=1, source_target_pairs={{0,8},{2,10},{4,12},{6,14},{8,0},{10,2},{12,4},{14,6},{16,24},{18,... | collective-permute-start | bytes 1769480 | tf_op jit(solution)/shard_map/ppermute | solution.py:50
  513.1 16.6 %collective-permute-start.42 = (bf16[1,96,1664]{2,1,0:T(8,128)(2,1)S(1)}, bf16[1,96,1664]{2,1,0:T(8,128)(2,1)S(1)}, u32[]{:S(2)}, u32[]{:S(2)}) collective-permute-start(bf16[1,96,1664]{2,1,0:T(8,128)(2,1)S(1)} %get-tuple-element.399), channel_id=1, source_target_pairs={{0,4},{2,6},{4,0},{6,2},{8,12},{10,14},{12,8},{14,10},{16,20},{18,... | collective-permute-start | bytes 958472 | tf_op jit(solution)/shard_map/ppermute | solution.py:50
  526.7 16.4 %collective-permute-start.57 = (bf16[4,24,768]{2,1,0:T(8,128)(2,1)S(1)}, bf16[4,24,768]{2,1,0:T(8,128)(2,1)S(1)}, u32[]{:S(2)}, u32[]{:S(2)}) collective-permute-start(bf16[4,24,768]{2,1,0:T(8,128)(2,1)S(1)} %fusion.63), channel_id=1, source_target_pairs={{0,16},{2,18},{4,20},{6,22},{8,24},{10,26},{12,28},{14,30},{16,0},... | collective-permute-start | bytes 442376 | tf_op jit(solution)/shard_map/ppermute | solution.py:50
  527.2 17.8 %collective-permute-start.58 = (bf16[1,24,3072]{2,1,0:T(8,128)(2,1)S(1)}, bf16[1,24,3072]{2,1,0:T(8,128)(2,1)S(1)}, u32[]{:S(2)}, u32[]{:S(2)}) collective-permute-start(bf16[1,24,3072]{2,1,0:T(8,128)(2,1)S(1)} %fusion.64), channel_id=1, source_target_pairs={{0,16},{2,18},{4,20},{6,22},{8,24},{10,26},{12,28},{14,30},{16,0},... | collective-permute-start | bytes 442376 | tf_op jit(solution)/shard_map/ppermute | solution.py:50
  529.8 21.4 %collective-permute-start.44 = (bf16[1,48,1664]{2,1,0:T(8,128)(2,1)S(1)}, bf16[1,48,1664]{2,1,0:T(8,128)(2,1)S(1)}, u32[]{:S(2)}, u32[]{:S(2)}) collective-permute-start(bf16[1,48,1664]{2,1,0:T(8,128)(2,1)S(1)} %bitcast.499), channel_id=1, source_target_pairs={{0,8},{2,10},{4,12},{6,14},{8,0},{10,2},{12,4},{14,6},{16,24},{18,... | collective-permute-start | bytes 479240 | tf_op jit(solution)/shard_map/ppermute | solution.py:50
  531.0 20.3 %collective-permute-start.45 = (bf16[1,48,1536]{2,1,0:T(8,128)(2,1)S(1)}, bf16[1,48,1536]{2,1,0:T(8,128)(2,1)S(1)}, u32[]{:S(2)}, u32[]{:S(2)}) collective-permute-start(bf16[1,48,1536]{2,1,0:T(8,128)(2,1)S(1)} %get-tuple-element.404), channel_id=1, source_target_pairs={{0,1},{1,0},{2,3},{3,2},{4,5},{5,4},{6,7},{7,6},{8,9},{9,8},{10,11... | collective-permute-start | bytes 442376 | tf_op jit(solution)/shard_map/ppermute | solution.py:50
  (139 other events, 1292.2 us)
Sparse Core Ops, SparseCore 0:
  24.3 96.0 all-gather.2
  123.2 100.4 all-gather.4

commit v4 on v3

--- a/solution.py
+++ b/solution.py
@@ -494,6 +494,96 @@
     )(select, kernel, qkv, rows_low)
 
 
+def pool_messages_kernel(select_ref, kernel_ref, rows_ref, up_ref, down_ref, head_ref):
+    pooled = up_ref.shape[1] - WIN
+    length = rows_ref.shape[1]
+    for group in range(rows_ref.shape[0]):
+        taps = dot_nn(select_ref[...], rows_ref[group])
+        total = kernel_ref[0, 0:1, :] * taps[:pooled]
+        for tap in range(1, TAPS):
+            total = total + kernel_ref[0, tap : tap + 1, :] * taps[tap * pooled : (tap + 1) * pooled]
+        head_ref[group] = total[:16]
+        total = total.astype(bf16)
+        up_ref[group, :WIN] = rows_ref[group, length - WIN :]
+        up_ref[group, WIN:] = total
+        down_ref[group, :WIN] = rows_ref[group, :WIN]
+        down_ref[group, WIN:] = total
+
+
+def pool_messages(select, kernel, qkv, width):
+    count, length = qkv.shape[:2]
+    groups = width // LANES
+
+    def spec(rows):
+        return pl.BlockSpec((count, rows, LANES), lambda j: (0, 0, j))
+
+    message = jax.ShapeDtypeStruct((count, WIN + length // 4, 2 * width), bf16)
+    return pl.pallas_call(
+        pool_messages_kernel,
+        grid=(2 * groups,),
+        in_specs=[
+            pl.BlockSpec(select.shape, lambda j: (0, 0)),
+            pl.BlockSpec((1, 8, LANES), lambda j: (j // groups, 0, j % groups)),
+            pl.BlockSpec((count, length, LANES), lambda j: (0, 0, j + groups)),
+        ],
+        out_specs=[spec(WIN + length // 4), spec(WIN + length // 4), spec(16)],
+        out_shape=[message, message, jax.ShapeDtypeStruct((count, 16, 2 * width), f32)],
+        compiler_params=pltpu.CompilerParams(vmem_limit_bytes=VMEM_LIMIT),
+        cost_estimate=pl.CostEstimate(
+            flops=count * length * width * 1300, bytes_accessed=2500000, transcendentals=0
+        ),
+        name="pool_messages",
+    )(select, kernel, qkv)
+
+
+def pool_join_kernel(kernel_ref, head_ref, mine_ref, tail_ref, low_ref, second_ref, up_ref,
+                     out_low_ref, out_ref, out_up_ref):
+    first, last = kernel_ref[0, 0:1, :], kernel_ref[0, 1:2, :]
+    row = lax.broadcasted_iota(jnp.int32, (16, LANES), 0)
+
+    def completed(block, before):
+        before = before.astype(f32)
+        edge = first * before[14:15] + last * before[15:16]
+        return (block + jnp.where(row == 0, edge, 0.0)).astype(bf16)
+
+    for group in range(mine_ref.shape[0]):
+        out_low_ref[group] = low_ref[group, WIN:]
+        out_ref[group] = mine_ref[group]
+        out_up_ref[group] = up_ref[group, WIN:]
+        out_low_ref[group, :16] = completed(
+            low_ref[group, WIN : WIN + 16].astype(f32), second_ref[group]
+        )
+        out_ref[group, :16] = completed(head_ref[group], low_ref[group, WIN - 16 : WIN])
+        out_up_ref[group, :16] = completed(
+            up_ref[group, WIN : WIN + 16].astype(f32), tail_ref[group]
+        )
+
+
+def pool_join(kernel, head, own_message, qkv, from_low, second, from_up, width):
+    count, length = qkv.shape[:2]
+    groups = width // LANES
+    pooled = length // 4
+
+    def spec(rows, at=0, shift=0):
+        return pl.BlockSpec((count, rows, LANES), lambda j: (0, at, j + shift))
+
+    out = jax.ShapeDtypeStruct((count, pooled, 2 * width), bf16)
+    return pl.pallas_call(
+        pool_join_kernel,
+        grid=(2 * groups,),
+        in_specs=[
+            pl.BlockSpec((1, 8, LANES), lambda j: (j // groups, 0, j % groups)),
+            spec(16), spec(pooled, WIN // pooled), spec(16, length // 16 - 1, groups),
+            spec(WIN + pooled), spec(16), spec(WIN + pooled),
+        ],
+        out_specs=[spec(pooled)] * 3,
+        out_shape=[out] * 3,
+        compiler_params=pltpu.CompilerParams(vmem_limit_bytes=VMEM_LIMIT),
+        cost_estimate=pl.CostEstimate(flops=0, bytes_accessed=5000000, transcendentals=0),
+        name="pool_join",
+    )(kernel, head, own_message, qkv, from_low, second, from_up)
+
+
 def pool_back_kernel(select_ref, spread_ref, kernel_ref, rows_ref, low_rows_ref, own_ref, pool_ref,
                      low_ref, up_ref, *rest):
     *rims, grad_ref, tail_ref, taps_ref = rest if len(rest) == 3 else (*rest[:3], None, rest[3])
@@ -783,7 +873,8 @@
         by_rows(count, body)
 
 
-def feed_forward(x, mixed, small, whole, ratio):
+def feed_forward(x, mixed, small, feed, ratio):
+    out_weight, out_at, whole, up_at = feed
     count, width = x.shape
     rows = pl.BlockSpec((count, width), lambda j: (0, 0))
     line = pl.BlockSpec((count, 1), lambda j: (0, 0))
@@ -801,7 +892,7 @@
         in_specs=[
             rows, rows, pl.BlockSpec((8, width), lambda j: (0, 0)),
             pl.BlockSpec((1, width), lambda j: (0, j)),
-            weight(0, 0), weight(1, 1), weight(1 + ratio, 1),
+            weight(out_at, 0), weight(up_at, 1), weight(up_at + ratio, 1),
         ],
         out_specs=[rows, line, rows, part, part, rows, line, rows],
         out_shape=[
@@ -815,7 +906,7 @@
             bytes_accessed=2 * whole.size + 4 * count * width * ratio + 20 * count * width,
         ),
         name="feed_forward",
-    )(x, mixed, small["vectors"], small["up_bias"], whole, whole, whole)
+    )(x, mixed, small["vectors"], small["up_bias"], out_weight, whole, whole)
 
 
 def feed_back_kernel(blocks, index_ref, grads_ref, norm_ref, inverse_ref, norm_two_ref,
@@ -882,8 +973,9 @@
         mixed_ref[...] = dot_nt(attention_ref[...], out_ref[...]).astype(bf16)
 
 
-def feed_back(grads, kept, small, whole, ratio):
+def feed_back(grads, kept, small, feed, ratio):
     norm, inverse, low, act, slope, norm_two, inverse_two = kept
+    out_weight, out_at, whole, up_at = feed
     count, width = grads.shape
     blocks = relative_blocks()
     half = len(blocks) // 2
@@ -913,7 +1005,7 @@
             grid=(ratio,),
             in_specs=[
                 rows, rows, line, rows, line, edge, rows, part, part,
-                weight(0, 0), weight(1, 1), weight(1 + ratio, 1),
+                weight(out_at, 0), weight(up_at, 1), weight(up_at + ratio, 1),
             ],
             out_specs=[
                 rows, rows, rows, edge, pl.BlockSpec((1, width), lambda j, index: (0, j)), *specs
@@ -936,7 +1028,7 @@
         ),
         name="feed_back",
     )(small_index(), grads, norm, inverse, norm_two, inverse_two, small["vectors"], low, act, slope,
-      whole, whole, whole)
+      out_weight, whole, whole)
     one, attention_low, grad_mixed, sums, up_sums, *out = results
     if blocks is None:
         down = [turned(out[0][i]) for i in range(ratio)]
@@ -1048,11 +1140,21 @@
     bias = jnp.concatenate([small["query_bias"], jnp.zeros((width,), f32), small["value_bias"]])
     qkv = matmul(x_low, qkv_weight)
     qkv = at("projected", (qkv + bias).astype(bf16).reshape(count, length, -1))
-    rows_low = passed_along(qkv[:, length - WIN :, width:], 1)
-    rows_up = passed_along(qkv[:, :WIN, width:], -1)
-    rows_low, rows_up = tied([rows_low, rows_up])
-    pooled = at("pooled", pool(select, small["taps"], qkv, rows_low, width))
-    pooled_low, pooled_up = pooled_rims(pooled)
+    if pooled_hops(length // 4) == 1 and length // 4 == WIN:
+        up_message, down_message, head = pool_messages(select, small["taps"], qkv, width)
+        rows_low, rows_up, second = tied([
+            passed_along(up_message, 1), passed_along(down_message, -1),
+            passed_along(qkv[:, length - 16 :, width:], 2),
+        ])
+        rows_low = at("pooled", rows_low)
+        pooled_low, pooled, pooled_up = pool_join(
+            small["taps"], head, up_message, qkv, rows_low, second, rows_up, width
+        )
+    else:
+        rows_low = passed_along(qkv[:, length - WIN :, width:], 1)
+        rows_up = passed_along(qkv[:, :WIN, width:], -1)
+        pooled = at("pooled", pool(select, small["taps"], qkv, rows_low, width))
+        pooled_low, pooled_up = pooled_rims(pooled)
     pooled_up = at("attending", pooled_up)
     operands = attend_operands(qkv, rows_low, rows_up, pooled, pooled_low, pooled_up)
     mixed, stats = attend(masks, operands, width)
@@ -1166,7 +1268,8 @@
 
     later = [
         Gather(jnp.concatenate(
-            [query_weight[layer], key_weight[layer], value_weight[layer]], axis=1
+            [query_weight[layer], key_weight[layer], value_weight[layer], output_weight[layer]],
+            axis=1,
         )[None], path("x"))
         for layer in range(1, layers)
     ]
@@ -1177,8 +1280,8 @@
         out, up, down, after = tied(
             [output_weight[layer], up_weight[layer], down_weight[layer], after]
         )
-        parts = down.reshape(ratio, shard_rows, width)
-        shard = jnp.concatenate([out, units_apart(up), *parts], axis=1)
+        parts = [units_apart(up), *down.reshape(ratio, shard_rows, width)]
+        shard = jnp.concatenate([out] * (layer == 0) + parts, axis=1)
         feeds.append(lax.all_gather(shard, ("seq", "batch"), axis=0, tiled=True))
         return after
 
@@ -1186,10 +1289,14 @@
     x = gather_feed(0, checkpoint(x, [first]))
     while first.left > 2:
         x = checkpoint(x, [first])
+    x = checkpoint(x, [], later)
     for layer in range(1, layers):
         x = gather_feed(layer, x)
+    if later:
+        x = checkpoint(x, later)
+        x = checkpoint(x, later, [], later)
     x = checkpoint(x, [first])
-    x = checkpoint(x, [first], later)
+    x = checkpoint(x, [first])
     first_whole = in_place(first.halves, first.cols)
     smalls = unpack_small(first_whole[:, 3 * width :], layers, ratio)
 
@@ -1204,7 +1311,9 @@
         following = later[layer : layer + 1]
 
         def at(name, value):
-            if name in ("projected", "pooled", "attended"):
+            if name == "pooled":
+                return checkpoint(value, [], following)
+            if name == "attended":
                 return checkpoint(value, following)
             if name == "fed":
                 return landed(value, following, 0)
@@ -1218,7 +1327,8 @@
             qkv_weight = first_whole[:, : 3 * width]
         else:
             qkv_weight = in_place(later[layer - 1].halves, width)
-        whole = (qkv_weight, feeds[layer], smalls[layer])
+        feed = (feeds[0], 0, feeds[0], 1) if layer == 0 else (qkv_weight, 3, feeds[layer], 0)
+        whole = (qkv_weight[:, : 3 * width], feed, smalls[layer])
         x, kept = layer_forward(x, whole, masks, select, count, forward_at(layer))
         states.append(kept)
         weights.append(whole)

time: 587 us -> 582 us (level)
  other arithmetic: 53.4 us -> 44.9 us
  Pallas kernels: 174 us -> 180 us
  waiting for transfers between devices: 166 us -> 160 us
    ppermute x45, waiting for transfers between devices: 153 us -> 142 us  [exchange(): return lax.ppermute(value, axis, pairs)]
    convert_element_type x30, other arithmetic: 31.9 us -> 25.3 us  [land(): (keep[:, side].astype(f32) + got[:, side].astype(f32)).astype(bf16)]
    ppermute x14 -> x12, starting transfers between devices: 31.3 us -> 26.7 us  [passed_along(): return lax.ppermute(value, 'seq', pairs)]
    unnamed x237 -> x286, local copies, waits for them, and re-layouts: 20.2 us -> 23 us
    ppermute x14 -> x12, waiting for transfers between devices: 12.8 us -> 12.3 us  [passed_along(): return lax.ppermute(value, 'seq', pairs)]
  transfers between devices with their start and end apart: 61 -> 59, of which waited for: 28 -> 28; matrix products, arithmetic and copies ran while one was open for 10% -> 9% of each run, Pallas kernels for 22% -> 23%
where the time goes in v4:
time: 582 us; the launch traced here: 573 us
  Pallas kernels  180 us (31%)
  waiting for transfers between devices  160 us (27%)
  starting transfers between devices  115 us (20%)
  other arithmetic  44.9 us (8%)
  local copies, waits for them, and re-layouts  40.8 us (7%)
  between operations  16.8 us (3%)
  matrix products  15.7 us (3%)
    ppermute x45, waiting for transfers between devices, exchange(): return lax.ppermute(value, axis, pairs)  142 us
    ppermute x45, starting transfers between devices, exchange(): return lax.ppermute(value, axis, pairs)  88.4 us
    pallas_call x4, Pallas kernels, attend_back(): pl.pallas_call(kernel, grid=(count, groups), in_specs=mask_specs + [moved...  41.9 us
    pallas_call x2, Pallas kernels, feed_back(): pl.pallas_call(functools.partial(feed_back_kernel, blocks), grid_spec=plt...  41.6 us
    pallas_call x2, Pallas kernels, feed_forward(): pl.pallas_call(feed_kernel, grid=(ratio,), in_specs=[rows, rows, pl.Block...  29.3 us
    ppermute x12, starting transfers between devices, passed_along(): return lax.ppermute(value, 'seq', pairs)  26.7 us
    convert_element_type x30, other arithmetic, land(): (keep[:, side].astype(f32) + got[:, side].astype(f32)).astype(bf16)  25.3 us
    pallas_call x2, Pallas kernels, attend(): pl.pallas_call(attend_kernel, grid=(count, groups), in_specs=mask_specs +...  23 us
  transfers between devices with their start and end apart: 59, of which 28 were waited for; matrix products, arithmetic and copies ran while one was open for 9% of the time, Pallas kernels for 23%

profile of v4, /device:TPU:0, one launch (start us, length us, event | category | flops | bytes accessed | tf_op | source)
XLA Modules:
  0.0 573.3 jit_solution(8628838020727789614)
XLA Ops:
  15.1 5.6 collective-permute-done
  25.0 6.2 %collective-permute-done.1 = bf16[1,48,2432]{2,1,0:T(8,128)(2,1)S(1)} collective-permute-done((bf16[1,48,2432]{2,1,0:T(8,128)(2,1)S(1)}, bf16[1,48,2432]{2,1,0:T(8,128)(2,1)S(1)}, u32[]{:S(2)}, u32[]{:S(2)}) %collective-permute-start.1) | collective-permute-done | bytes 233504 | tf_op jit(solution)/shard_map/ppermute | solution.py:50
  32.6 12.1 %collective-permute-done.2 = bf16[1,96,2432]{2,1,0:T(8,128)(2,1)S(1)} collective-permute-done((bf16[1,96,2432]{2,1,0:T(8,128)(2,1)S(1)}, bf16[1,96,2432]{2,1,0:T(8,128)(2,1)S(1)}, u32[]{:S(2)}, u32[]{:S(2)}) %collective-permute-start.2) | collective-permute-done | bytes 466976 | tf_op jit(solution)/shard_map/ppermute | solution.py:50
  54.0 10.5 %collective-permute-done.3 = bf16[1,24,3072]{2,1,0:T(8,128)(2,1)S(1)} collective-permute-done((bf16[1,24,3072]{2,1,0:T(8,128)(2,1)S(1)}, bf16[1,24,3072]{2,1,0:T(8,128)(2,1)S(1)}, u32[]{:S(2)}, u32[]{:S(2)}) %collective-permute-start.3) | collective-permute-done | bytes 147488 | tf_op jit(solution)/shard_map/ppermute | solution.py:50
  66.5 13.4 %collective-permute-done.4 = bf16[1,48,3072]{2,1,0:T(8,128)(2,1)S(1)} collective-permute-done((bf16[1,48,3072]{2,1,0:T(8,128)(2,1)S(1)}, bf16[1,48,3072]{2,1,0:T(8,128)(2,1)S(1)}, u32[]{:S(2)}, u32[]{:S(2)}) %collective-permute-start.4) | collective-permute-done | bytes 294944 | tf_op jit(solution)/shard_map/ppermute | solution.py:50
  101.8 5.0 collective-permute-start.9
  112.2 7.0 %collective-permute-start.10 = (bf16[1,96,3072]{2,1,0:T(8,128)(2,1)S(1)}, bf16[1,96,3072]{2,1,0:T(8,128)(2,1)}, u32[]{:S(2)}, u32[]{:S(2)}) collective-permute-start(bf16[1,96,3072]{2,1,0:T(8,128)(2,1)S(1)} %bitcast.443), channel_id=1, source_target_pairs={{0,4},{2,6},{4,0},{6,2},{8,12},{10,14},{12,8},{14,10},{16,20},{18,... | collective-permute-start | bytes 1769480 | tf_op jit(solution)/shard_map/ppermute | solution.py:50
  126.0 11.6 %attend.2 = (bf16[2,256,768]{2,1,0:T(8,128)(2,1)S(1)}, f32[2,3,8,256]{3,2,1,0:T(8,128)S(1)}) custom-call(f32[2,256,256]{2,1,0:T(8,128)S(1)} %pad_maximum_fusion.9.near_ref.refs_0_, f32[2,192,256]{2,1,0:T(8,128)S(1)} %pad_maximum_fusion.11.far_ref.refs_1_, bf16[2,256,2304]{2,1,0:T(8,128)(2,1)} %bitcast.354, bf16[2,256,2304]{2,1,0:T(8,128)(2,1)} %bitcast.355, ...), custom_call_target="tpu_custom_call" | custom-call | flops 786432000 | bytes 8000000 | tf_op jit(solution)/shard_map/attend/pallas_call | solution.py:366
  145.2 14.5 %feed_forward.2 = (f32[512,768]{1,0:T(8,128)S(1)}, f32[512,1]{1,0:T(8,128)S(1)}, bf16[512,768]{1,0:T(8,128)(2,1)S(1)}, bf16[512,3072]{1,0:T(8,128)(2,1)}, bf16[5...) custom-call(f32[512,768]{1,0:T(8,128)} %bitcast_convert_fusion.x_ref, ...), custom_call_target="tpu_custom_call" | custom-call | flops 5435817984 | bytes 24772608 | tf_op jit(solution)/shard_map/feed_forward/pallas_call | solution.py:889
  161.0 13.2 %collective-permute-done.11 = bf16[1,192,3072]{2,1,0:T(8,128)(2,1)} collective-permute-done((bf16[1,192,3072]{2,1,0:T(8,128)(2,1)S(1)}, bf16[1,192,3072]{2,1,0:T(8,128)(2,1)}, u32[]{:S(2)}, u32[]{:S(2)}) %collective-permute-start.11) | collective-permute-done | bytes 1179680 | tf_op jit(solution)/shard_map/ppermute | solution.py:50
  209.3 11.4 %attend.3 = (bf16[2,256,768]{2,1,0:T(8,128)(2,1)S(1)}, f32[2,3,8,256]{3,2,1,0:T(8,128)S(1)}) custom-call(f32[2,256,256]{2,1,0:T(8,128)S(1)} %copy-done.8, f32[2,192,256]{2,1,0:T(8,128)S(1)} %pad_maximum_fusion.11.far_ref.refs_1_, bf16[2,256,2304]{2,1,0:T(8,128)(2,1)} %bitcast.367, bf16[2,256,2304]{2,1,0:T(8,128)(2,1)} %bitcast.368, ...), custom_call_target="tpu_custom_call" | custom-call | flops 786432000 | bytes 8000000 | tf_op jit(solution)/shard_map/attend/pallas_call | solution.py:366
  221.5 5.3 all-gather.5.cloned.1.call-done.up_ref.down_ref
  228.0 14.8 %feed_forward.3 = (f32[512,768]{1,0:T(8,128)S(1)}, f32[512,1]{1,0:T(8,128)S(1)}, bf16[512,768]{1,0:T(8,128)(2,1)S(1)}, bf16[512,3072]{1,0:T(8,128)(2,1)}, bf16[5...) custom-call(f32[512,768]{1,0:T(8,128)} %get-tuple-element.293.x_ref, ...), custom_call_target="tpu_custom_call" | custom-call | flops 5435817984 | bytes 23592960 | tf_op jit(solution)/shard_map/feed_forward/pallas_call | solution.py:889
  245.1 20.7 %feed_back.2 = (f32[512,768]{1,0:T(8,128)S(1)}, bf16[512,768]{1,0:T(8,128)(2,1)S(1)}, bf16[512,768]{1,0:T(8,128)(2,1)S(1)}, f32[8,768]{1,0:T(8,128)S(1)}, f32[1,...) custom-call(s32[1]{0:T(128)} %bitcast.35.index_ref, ...), custom_call_target="tpu_custom_call" | custom-call | flops 10267656192 | bytes 33030144 | tf_op jit(solution)/shard_map/feed_back/pallas_call | solution.py:1001
  265.8 11.1 %collective-permute-start.16 = (bf16[4,384,768]{2,1,0:T(8,128)(2,1)}, bf16[4,384,768]{2,1,0:T(8,128)(2,1)S(1)}, u32[]{:S(2)}, u32[]{:S(2)}) collective-permute-start(bf16[4,384,768]{2,1,0:T(8,128)(2,1)} %bitcast.519), channel_id=1, source_target_pairs={{0,2},{2,0},{4,6},{6,4},{8,10},{10,8},{12,14},{14,12},{16,18},{18,... | collective-permute-start | bytes 7077896 | tf_op jit(solution)/shard_map/ppermute | solution.py:50
  277.0 10.7 %attend_back.4 = (bf16[2,256,768]{2,1,0:T(8,128)(2,1)S(1)}, f32[2,2,256,768]{3,2,1,0:T(8,128)}, f32[2,2,64,768]{3,2,1,0:T(8,128)S(1)}, bf16[2,2,144,768]{3,2,1,0:T(8,128)(2,1)}, bf16[2,2,128,768]{3,2,1,0:T(8,128)(2,1)S(1)}) custom-call(f32[2,256,256]{2,1,0:T(8,128)S(1)} %copy-done.8, f32[2,192,256]{2,1,0:T(8,128)S(1)} %pad_maximum_fusion.11.far_ref.refs_1_, ...), custom_call_target="tpu_custom_call" | custom-call | flops 983040000 | bytes 6000000 | tf_op jit(solution)/shard_map/attend_back/pallas_call | solution.py:411
  287.8 10.3 %attend_back.5 = (bf16[2,256,768]{2,1,0:T(8,128)(2,1)S(1)}, f32[2,2,256,768]{3,2,1,0:T(8,128)}, f32[2,2,64,768]{3,2,1,0:T(8,128)S(1)}, bf16[2,2,144,768]{3,2,1,0:T(8,128)(2,1)}, bf16[2,2,128,768]{3,2,1,0:T(8,128)(2,1)S(1)}) custom-call(f32[2,256,256]{2,1,0:T(8,128)S(1)} %copy-done.8, ...), custom_call_target="tpu_custom_call", output_to_operand_aliasing={{0}: (17, {}), {1}: (18, {}), {2}: (19, {}), {3}: (20, {}),... | custom-call | flops 983040000 | bytes 6000000 | tf_op jit(solution)/shard_map/attend_back/pallas_call | solution.py:411
  310.1 5.4 collective-permute-done.20.rest_1_
  315.5 6.2 %pool_back.2 = (bf16[2,2,256,768]{3,2,1,0:T(8,128)(2,1)S(1)}, f32[2,8,768]{2,1,0:T(8,128)S(1)}) custom-call(bf16[320,256]{1,0:T(8,128)(2,1)S(1)} %copy-done.17, bf16[256,320]{1,0:T(8,128)(2,1)S(1)} %fusion.42.spread_ref, f32[2,8,768]{2,1,0:T(8,128)S(1)} %copy-done.34, bf16[2,256,2304]{2,1,0:T(8,128)(2,1)} %bitcast.376, bf16[2,128,1536]{2,1,0:T(8,128)(2,1)S(1)} %copy-done.3, ...), custom_call_target="tpu_custom_call" | custom-call | flops 1572864000 | bytes 9000000 | tf_op jit(solution)/shard_map/pool_back/pallas_call | solution.py:649
  326.1 5.2 weight_grads.3
  331.3 9.0 %collective-permute-start.23 = (bf16[1,384,3072]{2,1,0:T(8,128)(2,1)}, bf16[1,384,3072]{2,1,0:T(8,128)(2,1)S(1)}, u32[]{:S(2)}, u32[]{:S(2)}) collective-permute-start(bf16[1,384,3072]{2,1,0:T(8,128)(2,1)} %bitcast.520), channel_id=1, source_target_pairs={{0,2},{2,0},{4,6},{6,4},{8,10},{10,8},{12,14},{14,12},{16,18},{18,... | collective-permute-start | bytes 7077896 | tf_op jit(solution)/shard_map/ppermute | solution.py:50
  344.4 20.9 %feed_back.3 = (f32[512,768]{1,0:T(8,128)S(1)}, bf16[512,768]{1,0:T(8,128)(2,1)S(1)}, bf16[512,768]{1,0:T(8,128)(2,1)S(1)}, f32[8,768]{1,0:T(8,128)S(1)}, f32[1,...) custom-call(s32[1]{0:T(128)} %bitcast.35.index_ref, ...), custom_call_target="tpu_custom_call" | custom-call | flops 10267656192 | bytes 35389440 | tf_op jit(solution)/shard_map/feed_back/pallas_call | solution.py:1001
  381.7 10.4 %attend_back.6 = (bf16[2,256,768]{2,1,0:T(8,128)(2,1)S(1)}, f32[2,2,256,768]{3,2,1,0:T(8,128)}, f32[2,2,64,768]{3,2,1,0:T(8,128)S(1)}, bf16[2,2,144,768]{3,2,1,0:T(8,128)(2,1)}, bf16[2,2,128,768]{3,2,1,0:T(8,128)(2,1)S(1)}) custom-call(f32[2,256,256]{2,1,0:T(8,128)S(1)} %copy-done.8, f32[2,192,256]{2,1,0:T(8,128)S(1)} %pad_maximum_fusion.11.far_ref.refs_1_, ...), custom_call_target="tpu_custom_call" | custom-call | flops 983040000 | bytes 6000000 | tf_op jit(solution)/shard_map/attend_back/pallas_call | solution.py:411
  408.6 10.5 %attend_back.7 = (bf16[2,256,768]{2,1,0:T(8,128)(2,1)S(1)}, f32[2,2,256,768]{3,2,1,0:T(8,128)}, f32[2,2,64,768]{3,2,1,0:T(8,128)S(1)}, bf16[2,2,144,768]{3,2,1,0:T(8,128)(2,1)}, bf16[2,2,128,768]{3,2,1,0:T(8,128)(2,1)S(1)}) custom-call(f32[2,256,256]{2,1,0:T(8,128)S(1)} %copy-done.8, ...), custom_call_target="tpu_custom_call", output_to_operand_aliasing={{0}: (17, {}), {1}: (18, {}), {2}: (19, {}), {3}: (20, {}),... | custom-call | flops 983040000 | bytes 6000000 | tf_op jit(solution)/shard_map/attend_back/pallas_call | solution.py:411
  420.6 17.6 %collective-permute-done.31 = bf16[4,192,768]{2,1,0:T(8,128)(2,1)S(1)} collective-permute-done((bf16[4,192,768]{2,1,0:T(8,128)(2,1)}, bf16[4,192,768]{2,1,0:T(8,128)(2,1)S(1)}, u32[]{:S(2)}, u32[]{:S(2)}) %collective-permute-start.31) | collective-permute-done | bytes 1179680 | tf_op jit(solution)/shard_map/ppermute | solution.py:50
  451.1 5.6 collective-permute-start.46
  458.8 6.0 %pool_back.3 = (bf16[2,2,256,768]{3,2,1,0:T(8,128)(2,1)S(1)}, f32[2,8,768]{2,1,0:T(8,128)S(1)}) custom-call(bf16[320,256]{1,0:T(8,128)(2,1)S(1)} %copy-done.17, bf16[256,320]{1,0:T(8,128)(2,1)S(1)} %copy-done.24, f32[2,8,768]{2,1,0:T(8,128)S(1)} %copy-done.32, bf16[2,256,2304]{2,1,0:T(8,128)(2,1)} %bitcast.363, ...), custom_call_target="tpu_custom_call" | custom-call | flops 1572864000 | bytes 9000000 | tf_op jit(solution)/shard_map/pool_back/pallas_call | solution.py:649
  482.9 7.3 %collective-permute-done.48 = bf16[1,96,3072]{2,1,0:T(8,128)(2,1)S(1)} collective-permute-done((bf16[1,96,3072]{2,1,0:T(8,128)(2,1)S(1)}, bf16[1,96,3072]{2,1,0:T(8,128)(2,1)S(1)}, u32[]{:S(2)}, u32[]{:S(2)}) %collective-permute-start.48) | collective-permute-done | bytes 589856 | tf_op jit(solution)/shard_map/ppermute | solution.py:50
  491.7 10.8 %collective-permute-done.50 = bf16[1,96,3072]{2,1,0:T(8,128)(2,1)S(1)} collective-permute-done((bf16[1,96,3072]{2,1,0:T(8,128)(2,1)S(1)}, bf16[1,96,3072]{2,1,0:T(8,128)(2,1)S(1)}, u32[]{:S(2)}, u32[]{:S(2)}) %collective-permute-start.50) | collective-permute-done | bytes 589856 | tf_op jit(solution)/shard_map/ppermute | solution.py:50
  527.1 7.3 %collective-permute-done.54 = bf16[1,24,3072]{2,1,0:T(8,128)(2,1)S(1)} collective-permute-done((bf16[1,24,3072]{2,1,0:T(8,128)(2,1)S(1)}, bf16[1,24,3072]{2,1,0:T(8,128)(2,1)S(1)}, u32[]{:S(2)}, u32[]{:S(2)}) %collective-permute-start.54) | collective-permute-done | bytes 147488 | tf_op jit(solution)/shard_map/ppermute | solution.py:50
  540.0 5.9 %units_back.1 = f32[48,3072]{1,0:T(8,128)} custom-call(bf16[4,384,1536]{2,1,0:T(8,128)(2,1)S(1)} %add_convert_fusion.spread_ref, f32[48,3072]{1,0:T(8,128)S(1)} %pad_maximum_fusion.7.refs_0_.refs_1_.refs_2_.refs_3_, f32[48,3072]{1,0:T(8,128)S(1)} %pad_maximum_fusion.7.refs_0_.refs_1_.refs_2_.refs_3_, ...), custom_call_target="tpu_custom_call" | custom-call | tf_op jit(solution)/shard_map/units_back/pallas_call | solution.py:1068
  549.8 5.5 collective-permute-done.45
  (548 shorter events, 239.2 us)
Async XLA Ops:
  7.4 137.9 %all-gather.3.cloned.1.call-start = ((), (), s32[]{:S(2)}) async-start(), calls=%async_computation | async-start | bytes 10948608 | tf_op jit(solution)/shard_map/all_gather | solution.py:1285
  24.2 202.6 %all-gather.5.cloned.1.call-start = ((), (), s32[]{:S(2)}) async-start(), calls=%async_computation.1 | async-start | bytes 9732096 | tf_op jit(solution)/shard_map/all_gather | solution.py:1285
  48.2 31.7 %collective-permute-start.5 = (bf16[1,192,2432]{2,1,0:T(8,128)(2,1)S(1)}, bf16[1,192,2432]{2,1,0:T(8,128)(2,1)S(1)}, u32[]{:S(2)}, u32[]{:S(2)}) collective-permute-start(bf16[1,192,2432]{2,1,0:T(8,128)(2,1)S(1)} %bitcast.423), channel_id=1, source_target_pairs={{0,4},{2,6},{4,0},{6,2},{8,12},{10,14},{12,8},{14,10},{16,20},{18,... | collective-permute-start | bytes 2801672 | tf_op jit(solution)/shard_map/ppermute | solution.py:50
  112.2 25.5 %collective-permute-start.10 = (bf16[1,96,3072]{2,1,0:T(8,128)(2,1)S(1)}, bf16[1,96,3072]{2,1,0:T(8,128)(2,1)}, u32[]{:S(2)}, u32[]{:S(2)}) collective-permute-start(bf16[1,96,3072]{2,1,0:T(8,128)(2,1)S(1)} %bitcast.443), channel_id=1, source_target_pairs={{0,4},{2,6},{4,0},{6,2},{8,12},{10,14},{12,8},{14,10},{16,20},{18,... | collective-permute-start | bytes 1769480 | tf_op jit(solution)/shard_map/ppermute | solution.py:50
  139.4 34.9 %collective-permute-start.11 = (bf16[1,192,3072]{2,1,0:T(8,128)(2,1)S(1)}, bf16[1,192,3072]{2,1,0:T(8,128)(2,1)}, u32[]{:S(2)}, u32[]{:S(2)}) collective-permute-start(bf16[1,192,3072]{2,1,0:T(8,128)(2,1)S(1)} %bitcast.418), channel_id=1, source_target_pairs={{0,1},{1,0},{2,3},{3,2},{4,5},{5,4},{6,7},{7,6},{8,9},{9,8},{10,11... | collective-permute-start | bytes 3538952 | tf_op jit(solution)/shard_map/ppermute | solution.py:50
  265.8 35.8 %collective-permute-start.16 = (bf16[4,384,768]{2,1,0:T(8,128)(2,1)}, bf16[4,384,768]{2,1,0:T(8,128)(2,1)S(1)}, u32[]{:S(2)}, u32[]{:S(2)}) collective-permute-start(bf16[4,384,768]{2,1,0:T(8,128)(2,1)} %bitcast.519), channel_id=1, source_target_pairs={{0,2},{2,0},{4,6},{6,4},{8,10},{10,8},{12,14},{14,12},{16,18},{18,... | collective-permute-start | bytes 7077896 | tf_op jit(solution)/shard_map/ppermute | solution.py:50
  276.9 24.7 %collective-permute-start.17 = (bf16[1,384,3072]{2,1,0:T(8,128)(2,1)}, bf16[1,384,3072]{2,1,0:T(8,128)(2,1)}, u32[]{:S(2)}, u32[]{:S(2)}) collective-permute-start(bf16[1,384,3072]{2,1,0:T(8,128)(2,1)} %bitcast.518), channel_id=1, source_target_pairs={{0,2},{2,0},{4,6},{6,4},{8,10},{10,8},{12,14},{14,12},{16,18},{18,... | collective-permute-start | bytes 7077896 | tf_op jit(solution)/shard_map/ppermute | solution.py:50
  298.1 17.4 %collective-permute-start.19 = (bf16[2,2,144,768]{3,2,1,0:T(8,128)(2,1)}, bf16[2,2,144,768]{3,2,1,0:T(8,128)(2,1)S(1)}, u32[]{:S(2)}, u32[]{:S(2)}) collective-permute-start(bf16[2,2,144,768]{3,2,1,0:T(8,128)(2,1)} %get-tuple-element.333), channel_id=1, source_target_pairs={{2,0},{4,2},{6,4},{8,6},{10,8},{12,10},{14,12},{16,14},{18,16},{20... | collective-permute-start | bytes 2654216 | tf_op jit(solution)/shard_map/ppermute | solution.py:171
  331.3 39.6 %collective-permute-start.23 = (bf16[1,384,3072]{2,1,0:T(8,128)(2,1)}, bf16[1,384,3072]{2,1,0:T(8,128)(2,1)S(1)}, u32[]{:S(2)}, u32[]{:S(2)}) collective-permute-start(bf16[1,384,3072]{2,1,0:T(8,128)(2,1)} %bitcast.520), channel_id=1, source_target_pairs={{0,2},{2,0},{4,6},{6,4},{8,10},{10,8},{12,14},{14,12},{16,18},{18,... | collective-permute-start | bytes 7077896 | tf_op jit(solution)/shard_map/ppermute | solution.py:50
  340.3 29.3 %collective-permute-start.21 = (bf16[4,192,768]{2,1,0:T(8,128)(2,1)}, bf16[4,192,768]{2,1,0:T(8,128)(2,1)}, u32[]{:S(2)}, u32[]{:S(2)}) collective-permute-start(bf16[4,192,768]{2,1,0:T(8,128)(2,1)} %get-tuple-element.355), channel_id=1, source_target_pairs={{0,4},{2,6},{4,0},{6,2},{8,12},{10,14},{12,8},{14,10},{16,20},{18,... | collective-permute-start | bytes 3538952 | tf_op jit(solution)/shard_map/ppermute | solution.py:50
  342.6 28.2 %collective-permute-start.22 = (bf16[1,192,3072]{2,1,0:T(8,128)(2,1)S(1)}, bf16[1,192,3072]{2,1,0:T(8,128)(2,1)}, u32[]{:S(2)}, u32[]{:S(2)}) collective-permute-start(bf16[1,192,3072]{2,1,0:T(8,128)(2,1)S(1)} %bitcast.451), channel_id=1, source_target_pairs={{0,1},{1,0},{2,3},{3,2},{4,5},{5,4},{6,7},{7,6},{8,9},{9,8},{10,11... | collective-permute-start | bytes 3538952 | tf_op jit(solution)/shard_map/ppermute | solution.py:50
  376.9 17.4 %collective-permute-start.26 = (bf16[4,384,768]{2,1,0:T(8,128)(2,1)}, bf16[4,384,768]{2,1,0:T(8,128)(2,1)}, u32[]{:S(2)}, u32[]{:S(2)}) collective-permute-start(bf16[4,384,768]{2,1,0:T(8,128)(2,1)} %bitcast.89), channel_id=1, source_target_pairs={{0,2},{2,0},{4,6},{6,4},{8,10},{10,8},{12,14},{14,12},{16,18},{18,... | collective-permute-start | bytes 7077896 | tf_op jit(solution)/shard_map/ppermute | solution.py:50
  376.9 17.4 %collective-permute-start.27 = (bf16[1,384,3072]{2,1,0:T(8,128)(2,1)}, bf16[1,384,3072]{2,1,0:T(8,128)(2,1)S(1)}, u32[]{:S(2)}, u32[]{:S(2)}) collective-permute-start(bf16[1,384,3072]{2,1,0:T(8,128)(2,1)} %bitcast.90), channel_id=1, source_target_pairs={{0,2},{2,0},{4,6},{6,4},{8,10},{10,8},{12,14},{14,12},{16,18},{18,... | collective-permute-start | bytes 7077896 | tf_op jit(solution)/shard_map/ppermute | solution.py:50
  379.7 39.4 %collective-permute-start.30 = (bf16[1,192,3072]{2,1,0:T(8,128)(2,1)}, bf16[1,192,3072]{2,1,0:T(8,128)(2,1)}, u32[]{:S(2)}, u32[]{:S(2)}) collective-permute-start(bf16[1,192,3072]{2,1,0:T(8,128)(2,1)} %bitcast.88), channel_id=1, source_target_pairs={{0,8},{2,10},{4,12},{6,14},{8,0},{10,2},{12,4},{14,6},{16,24},{18,... | collective-permute-start | bytes 3538952 | tf_op jit(solution)/shard_map/ppermute | solution.py:50
  403.7 34.6 %collective-permute-start.31 = (bf16[4,192,768]{2,1,0:T(8,128)(2,1)}, bf16[4,192,768]{2,1,0:T(8,128)(2,1)S(1)}, u32[]{:S(2)}, u32[]{:S(2)}) collective-permute-start(bf16[4,192,768]{2,1,0:T(8,128)(2,1)} %get-tuple-element.390), channel_id=1, source_target_pairs={{0,4},{2,6},{4,0},{6,2},{8,12},{10,14},{12,8},{14,10},{16,20},{18,... | collective-permute-start | bytes 3538952 | tf_op jit(solution)/shard_map/ppermute | solution.py:50
  404.2 34.1 %collective-permute-start.32 = (bf16[1,192,3072]{2,1,0:T(8,128)(2,1)}, bf16[1,192,3072]{2,1,0:T(8,128)(2,1)S(1)}, u32[]{:S(2)}, u32[]{:S(2)}) collective-permute-start(bf16[1,192,3072]{2,1,0:T(8,128)(2,1)} %bitcast.103), channel_id=1, source_target_pairs={{0,1},{1,0},{2,3},{3,2},{4,5},{5,4},{6,7},{7,6},{8,9},{9,8},{10,11... | collective-permute-start | bytes 3538952 | tf_op jit(solution)/shard_map/ppermute | solution.py:50
  419.1 37.7 %collective-permute-start.34 = (bf16[2,2,144,768]{3,2,1,0:T(8,128)(2,1)}, bf16[2,2,144,768]{3,2,1,0:T(8,128)(2,1)S(1)}, u32[]{:S(2)}, u32[]{:S(2)}) collective-permute-start(bf16[2,2,144,768]{3,2,1,0:T(8,128)(2,1)} %get-tuple-element.396), channel_id=1, source_target_pairs={{2,0},{4,2},{6,4},{8,6},{10,8},{12,10},{14,12},{16,14},{18,16},{20... | collective-permute-start | bytes 2654216 | tf_op jit(solution)/shard_map/ppermute | solution.py:171
  439.1 18.5 %collective-permute-start.33 = (bf16[2,2,128,768]{3,2,1,0:T(8,128)(2,1)S(1)}, bf16[2,2,128,768]{3,2,1,0:T(8,128)(2,1)}, u32[]{:S(2)}, u32[]{:S(2)}) collective-permute-start(bf16[2,2,128,768]{3,2,1,0:T(8,128)(2,1)S(1)} %get-tuple-element.395.rest_0_), channel_id=1, source_target_pairs={{0,2},{2,4},{4,6},{6,8},{8,10},{10,12},{12,14},{14,16},{16,18},{18... | collective-permute-start | bytes 2359304 | tf_op jit(solution)/shard_map/ppermute | solution.py:171
  451.1 28.6 %collective-permute-start.46 = (bf16[4,24,768]{2,1,0:T(8,128)(2,1)S(1)}, bf16[4,24,768]{2,1,0:T(8,128)(2,1)S(1)}, u32[]{:S(2)}, u32[]{:S(2)}) collective-permute-start(bf16[4,24,768]{2,1,0:T(8,128)(2,1)S(1)} %copy-done.115), channel_id=1, source_target_pairs={{0,16},{2,18},{4,20},{6,22},{8,24},{10,26},{12,28},{14,30},{16,0},... | collective-permute-start | bytes 442376 | tf_op jit(solution)/shard_map/ppermute | solution.py:50
  456.7 24.4 %collective-permute-start.47 = (bf16[1,24,3072]{2,1,0:T(8,128)(2,1)S(1)}, bf16[1,24,3072]{2,1,0:T(8,128)(2,1)S(1)}, u32[]{:S(2)}, u32[]{:S(2)}) collective-permute-start(bf16[1,24,3072]{2,1,0:T(8,128)(2,1)S(1)} %fusion.63), channel_id=1, source_target_pairs={{0,16},{2,18},{4,20},{6,22},{8,24},{10,26},{12,28},{14,30},{16,0},... | collective-permute-start | bytes 442376 | tf_op jit(solution)/shard_map/ppermute | solution.py:50
  474.1 16.2 %collective-permute-start.48 = (bf16[1,96,3072]{2,1,0:T(8,128)(2,1)S(1)}, bf16[1,96,3072]{2,1,0:T(8,128)(2,1)S(1)}, u32[]{:S(2)}, u32[]{:S(2)}) collective-permute-start(bf16[1,96,3072]{2,1,0:T(8,128)(2,1)S(1)} %get-tuple-element.438), channel_id=1, source_target_pairs={{0,4},{2,6},{4,0},{6,2},{8,12},{10,14},{12,8},{14,10},{16,20},{18,... | collective-permute-start | bytes 1769480 | tf_op jit(solution)/shard_map/ppermute | solution.py:50
  475.5 16.2 %collective-permute-start.49 = (bf16[4,96,768]{2,1,0:T(8,128)(2,1)S(1)}, bf16[4,96,768]{2,1,0:T(8,128)(2,1)S(1)}, u32[]{:S(2)}, u32[]{:S(2)}) collective-permute-start(bf16[4,96,768]{2,1,0:T(8,128)(2,1)S(1)} %get-tuple-element.439), channel_id=1, source_target_pairs={{0,1},{1,0},{2,3},{3,2},{4,5},{5,4},{6,7},{7,6},{8,9},{9,8},{10,11... | collective-permute-start | bytes 1769480 | tf_op jit(solution)/shard_map/ppermute | solution.py:50
  476.2 26.3 %collective-permute-start.50 = (bf16[1,96,3072]{2,1,0:T(8,128)(2,1)S(1)}, bf16[1,96,3072]{2,1,0:T(8,128)(2,1)S(1)}, u32[]{:S(2)}, u32[]{:S(2)}) collective-permute-start(bf16[1,96,3072]{2,1,0:T(8,128)(2,1)S(1)} %get-tuple-element.440), channel_id=1, source_target_pairs={{0,4},{2,6},{4,0},{6,2},{8,12},{10,14},{12,8},{14,10},{16,20},{18,... | collective-permute-start | bytes 1769480 | tf_op jit(solution)/shard_map/ppermute | solution.py:50
  479.7 26.1 %collective-permute-start.38 = (bf16[1,192,1664]{2,1,0:T(8,128)(2,1)S(1)}, bf16[1,192,1664]{2,1,0:T(8,128)(2,1)S(1)}, u32[]{:S(2)}, u32[]{:S(2)}) collective-permute-start(bf16[1,192,1664]{2,1,0:T(8,128)(2,1)S(1)} %bitcast.470), channel_id=1, source_target_pairs={{0,1},{1,0},{2,3},{3,2},{4,5},{5,4},{6,7},{7,6},{8,9},{9,8},{10,11... | collective-permute-start | bytes 1916936 | tf_op jit(solution)/shard_map/ppermute | solution.py:50
  481.1 24.7 %collective-permute-start.39 = (bf16[1,192,1536]{2,1,0:T(8,128)(2,1)S(1)}, bf16[1,192,1536]{2,1,0:T(8,128)(2,1)S(1)}, u32[]{:S(2)}, u32[]{:S(2)}) collective-permute-start(bf16[1,192,1536]{2,1,0:T(8,128)(2,1)S(1)} %bitcast.471), channel_id=1, source_target_pairs={{0,8},{2,10},{4,12},{6,14},{8,0},{10,2},{12,4},{14,6},{16,24},{18,... | collective-permute-start | bytes 1769480 | tf_op jit(solution)/shard_map/ppermute | solution.py:50
  506.1 18.2 %collective-permute-start.40 = (bf16[1,96,1664]{2,1,0:T(8,128)(2,1)S(1)}, bf16[1,96,1664]{2,1,0:T(8,128)(2,1)S(1)}, u32[]{:S(2)}, u32[]{:S(2)}) collective-permute-start(bf16[1,96,1664]{2,1,0:T(8,128)(2,1)S(1)} %get-tuple-element.425), channel_id=1, source_target_pairs={{0,4},{2,6},{4,0},{6,2},{8,12},{10,14},{12,8},{14,10},{16,20},{18,... | collective-permute-start | bytes 958472 | tf_op jit(solution)/shard_map/ppermute | solution.py:50
  507.2 17.1 %collective-permute-start.41 = (bf16[1,96,1536]{2,1,0:T(8,128)(2,1)S(1)}, bf16[1,96,1536]{2,1,0:T(8,128)(2,1)S(1)}, u32[]{:S(2)}, u32[]{:S(2)}) collective-permute-start(bf16[1,96,1536]{2,1,0:T(8,128)(2,1)S(1)} %get-tuple-element.426), channel_id=1, source_target_pairs={{0,4},{2,6},{4,0},{6,2},{8,12},{10,14},{12,8},{14,10},{16,20},{18,... | collective-permute-start | bytes 884744 | tf_op jit(solution)/shard_map/ppermute | solution.py:50
  518.4 16.1 %collective-permute-start.54 = (bf16[1,24,3072]{2,1,0:T(8,128)(2,1)S(1)}, bf16[1,24,3072]{2,1,0:T(8,128)(2,1)S(1)}, u32[]{:S(2)}, u32[]{:S(2)}) collective-permute-start(bf16[1,24,3072]{2,1,0:T(8,128)(2,1)S(1)} %fusion.66), channel_id=1, source_target_pairs={{0,16},{2,18},{4,20},{6,22},{8,24},{10,26},{12,28},{14,30},{16,0},... | collective-permute-start | bytes 442376 | tf_op jit(solution)/shard_map/ppermute | solution.py:50
  521.4 16.2 %collective-permute-start.55 = (bf16[4,24,768]{2,1,0:T(8,128)(2,1)S(1)}, bf16[4,24,768]{2,1,0:T(8,128)(2,1)S(1)}, u32[]{:S(2)}, u32[]{:S(2)}) collective-permute-start(bf16[4,24,768]{2,1,0:T(8,128)(2,1)S(1)} %fusion.67), channel_id=1, source_target_pairs={{0,16},{2,18},{4,20},{6,22},{8,24},{10,26},{12,28},{14,30},{16,0},... | collective-permute-start | bytes 442376 | tf_op jit(solution)/shard_map/ppermute | solution.py:50
  521.5 18.3 %collective-permute-start.56 = (bf16[1,24,3072]{2,1,0:T(8,128)(2,1)S(1)}, bf16[1,24,3072]{2,1,0:T(8,128)(2,1)S(1)}, u32[]{:S(2)}, u32[]{:S(2)}) collective-permute-start(bf16[1,24,3072]{2,1,0:T(8,128)(2,1)S(1)} %fusion.68), channel_id=1, source_target_pairs={{0,16},{2,18},{4,20},{6,22},{8,24},{10,26},{12,28},{14,30},{16,0},... | collective-permute-start | bytes 442376 | tf_op jit(solution)/shard_map/ppermute | solution.py:50
  524.5 21.4 %collective-permute-start.42 = (bf16[1,48,1664]{2,1,0:T(8,128)(2,1)S(1)}, bf16[1,48,1664]{2,1,0:T(8,128)(2,1)S(1)}, u32[]{:S(2)}, u32[]{:S(2)}) collective-permute-start(bf16[1,48,1664]{2,1,0:T(8,128)(2,1)S(1)} %bitcast.503), channel_id=1, source_target_pairs={{0,8},{2,10},{4,12},{6,14},{8,0},{10,2},{12,4},{14,6},{16,24},{18,... | collective-permute-start | bytes 479240 | tf_op jit(solution)/shard_map/ppermute | solution.py:50
  526.0 19.9 %collective-permute-start.43 = (bf16[1,48,1536]{2,1,0:T(8,128)(2,1)S(1)}, bf16[1,48,1536]{2,1,0:T(8,128)(2,1)S(1)}, u32[]{:S(2)}, u32[]{:S(2)}) collective-permute-start(bf16[1,48,1536]{2,1,0:T(8,128)(2,1)S(1)} %get-tuple-element.430), channel_id=1, source_target_pairs={{0,1},{1,0},{2,3},{3,2},{4,5},{5,4},{6,7},{7,6},{8,9},{9,8},{10,11... | collective-permute-start | bytes 442376 | tf_op jit(solution)/shard_map/ppermute | solution.py:50
  (162 other events, 1373.9 us)
Sparse Core Ops, SparseCore 0:
  24.3 99.4 all-gather.2
  126.7 100.1 all-gather.4

commit v5 on v4

--- a/solution.py
+++ b/solution.py
@@ -1416,9 +1416,8 @@
         parts.append(flows["up", layer].total[0])
         parts.append(flows["down", layer].total.reshape(ratio * shard_rows, width))
         totals.append(parts)
-    up_totals = units_back(
-        jnp.concatenate([parts[4] for parts in totals]), ratio, shard_rows
-    ).reshape(layers, shard_rows, ratio * width)
+    up_totals, _ = tied([jnp.concatenate([parts[4] for parts in totals]), last.keep])
+    up_totals = units_back(up_totals, ratio, shard_rows).reshape(layers, shard_rows, ratio * width)
     input_grad = grads.astype(bf16).reshape(tokens.shape)
     lines = last.total[0, :, 2 * width :].T
     per_layer = 8 + 2 * TAPS + ratio

time: 582 us -> 582 us (level)
  no operation moved by 1% of the time
where the time goes in v5:
time: 582 us; the launch traced here: 573 us
  Pallas kernels  180 us (31%)
  waiting for transfers between devices  160 us (27%)
  starting transfers between devices  115 us (20%)
  other arithmetic  44.9 us (8%)
  local copies, waits for them, and re-layouts  40.8 us (7%)
  between operations  16.8 us (3%)
  matrix products  15.7 us (3%)
    ppermute x45, waiting for transfers between devices, exchange(): return lax.ppermute(value, axis, pairs)  142 us
    ppermute x45, starting transfers between devices, exchange(): return lax.ppermute(value, axis, pairs)  88.4 us
    pallas_call x4, Pallas kernels, attend_back(): pl.pallas_call(kernel, grid=(count, groups), in_specs=mask_specs + [moved...  41.9 us
    pallas_call x2, Pallas kernels, feed_back(): pl.pallas_call(functools.partial(feed_back_kernel, blocks), grid_spec=plt...  41.6 us
    pallas_call x2, Pallas kernels, feed_forward(): pl.pallas_call(feed_kernel, grid=(ratio,), in_specs=[rows, rows, pl.Block...  29.3 us
    ppermute x12, starting transfers between devices, passed_along(): return lax.ppermute(value, 'seq', pairs)  26.7 us
    convert_element_type x30, other arithmetic, land(): (keep[:, side].astype(f32) + got[:, side].astype(f32)).astype(bf16)  25.3 us
    pallas_call x2, Pallas kernels, attend(): pl.pallas_call(attend_kernel, grid=(count, groups), in_specs=mask_specs +...  23 us
  transfers between devices with their start and end apart: 59, of which 28 were waited for; matrix products, arithmetic and copies ran while one was open for 9% of the time, Pallas kernels for 23%

profile of v5, /device:TPU:0, one launch (start us, length us, event | category | flops | bytes accessed | tf_op | source)
XLA Modules:
  0.0 573.3 jit_solution(7708884308653197409)
XLA Ops:
  15.1 5.6 collective-permute-done
  25.0 6.2 %collective-permute-done.1 = bf16[1,48,2432]{2,1,0:T(8,128)(2,1)S(1)} collective-permute-done((bf16[1,48,2432]{2,1,0:T(8,128)(2,1)S(1)}, bf16[1,48,2432]{2,1,0:T(8,128)(2,1)S(1)}, u32[]{:S(2)}, u32[]{:S(2)}) %collective-permute-start.1) | collective-permute-done | bytes 233504 | tf_op jit(solution)/shard_map/ppermute | solution.py:50
  32.6 12.1 %collective-permute-done.2 = bf16[1,96,2432]{2,1,0:T(8,128)(2,1)S(1)} collective-permute-done((bf16[1,96,2432]{2,1,0:T(8,128)(2,1)S(1)}, bf16[1,96,2432]{2,1,0:T(8,128)(2,1)S(1)}, u32[]{:S(2)}, u32[]{:S(2)}) %collective-permute-start.2) | collective-permute-done | bytes 466976 | tf_op jit(solution)/shard_map/ppermute | solution.py:50
  54.0 10.5 %collective-permute-done.3 = bf16[1,24,3072]{2,1,0:T(8,128)(2,1)S(1)} collective-permute-done((bf16[1,24,3072]{2,1,0:T(8,128)(2,1)S(1)}, bf16[1,24,3072]{2,1,0:T(8,128)(2,1)S(1)}, u32[]{:S(2)}, u32[]{:S(2)}) %collective-permute-start.3) | collective-permute-done | bytes 147488 | tf_op jit(solution)/shard_map/ppermute | solution.py:50
  66.5 13.4 %collective-permute-done.4 = bf16[1,48,3072]{2,1,0:T(8,128)(2,1)S(1)} collective-permute-done((bf16[1,48,3072]{2,1,0:T(8,128)(2,1)S(1)}, bf16[1,48,3072]{2,1,0:T(8,128)(2,1)S(1)}, u32[]{:S(2)}, u32[]{:S(2)}) %collective-permute-start.4) | collective-permute-done | bytes 294944 | tf_op jit(solution)/shard_map/ppermute | solution.py:50
  101.8 5.0 collective-permute-start.9
  112.2 7.0 %collective-permute-start.10 = (bf16[1,96,3072]{2,1,0:T(8,128)(2,1)S(1)}, bf16[1,96,3072]{2,1,0:T(8,128)(2,1)}, u32[]{:S(2)}, u32[]{:S(2)}) collective-permute-start(bf16[1,96,3072]{2,1,0:T(8,128)(2,1)S(1)} %bitcast.443), channel_id=1, source_target_pairs={{0,4},{2,6},{4,0},{6,2},{8,12},{10,14},{12,8},{14,10},{16,20},{18,... | collective-permute-start | bytes 1769480 | tf_op jit(solution)/shard_map/ppermute | solution.py:50
  126.0 11.6 %attend.2 = (bf16[2,256,768]{2,1,0:T(8,128)(2,1)S(1)}, f32[2,3,8,256]{3,2,1,0:T(8,128)S(1)}) custom-call(f32[2,256,256]{2,1,0:T(8,128)S(1)} %pad_maximum_fusion.9.near_ref.refs_0_, f32[2,192,256]{2,1,0:T(8,128)S(1)} %pad_maximum_fusion.11.far_ref.refs_1_, bf16[2,256,2304]{2,1,0:T(8,128)(2,1)} %bitcast.354, bf16[2,256,2304]{2,1,0:T(8,128)(2,1)} %bitcast.355, ...), custom_call_target="tpu_custom_call" | custom-call | flops 786432000 | bytes 8000000 | tf_op jit(solution)/shard_map/attend/pallas_call | solution.py:366
  145.2 14.5 %feed_forward.2 = (f32[512,768]{1,0:T(8,128)S(1)}, f32[512,1]{1,0:T(8,128)S(1)}, bf16[512,768]{1,0:T(8,128)(2,1)S(1)}, bf16[512,3072]{1,0:T(8,128)(2,1)}, bf16[5...) custom-call(f32[512,768]{1,0:T(8,128)} %bitcast_convert_fusion.x_ref, ...), custom_call_target="tpu_custom_call" | custom-call | flops 5435817984 | bytes 24772608 | tf_op jit(solution)/shard_map/feed_forward/pallas_call | solution.py:889
  161.0 13.2 %collective-permute-done.11 = bf16[1,192,3072]{2,1,0:T(8,128)(2,1)} collective-permute-done((bf16[1,192,3072]{2,1,0:T(8,128)(2,1)S(1)}, bf16[1,192,3072]{2,1,0:T(8,128)(2,1)}, u32[]{:S(2)}, u32[]{:S(2)}) %collective-permute-start.11) | collective-permute-done | bytes 1179680 | tf_op jit(solution)/shard_map/ppermute | solution.py:50
  209.3 11.4 %attend.3 = (bf16[2,256,768]{2,1,0:T(8,128)(2,1)S(1)}, f32[2,3,8,256]{3,2,1,0:T(8,128)S(1)}) custom-call(f32[2,256,256]{2,1,0:T(8,128)S(1)} %copy-done.8, f32[2,192,256]{2,1,0:T(8,128)S(1)} %pad_maximum_fusion.11.far_ref.refs_1_, bf16[2,256,2304]{2,1,0:T(8,128)(2,1)} %bitcast.367, bf16[2,256,2304]{2,1,0:T(8,128)(2,1)} %bitcast.368, ...), custom_call_target="tpu_custom_call" | custom-call | flops 786432000 | bytes 8000000 | tf_op jit(solution)/shard_map/attend/pallas_call | solution.py:366
  221.5 5.3 all-gather.5.cloned.1.call-done.up_ref.down_ref
  228.0 14.8 %feed_forward.3 = (f32[512,768]{1,0:T(8,128)S(1)}, f32[512,1]{1,0:T(8,128)S(1)}, bf16[512,768]{1,0:T(8,128)(2,1)S(1)}, bf16[512,3072]{1,0:T(8,128)(2,1)}, bf16[5...) custom-call(f32[512,768]{1,0:T(8,128)} %get-tuple-element.293.x_ref, ...), custom_call_target="tpu_custom_call" | custom-call | flops 5435817984 | bytes 23592960 | tf_op jit(solution)/shard_map/feed_forward/pallas_call | solution.py:889
  245.1 20.7 %feed_back.2 = (f32[512,768]{1,0:T(8,128)S(1)}, bf16[512,768]{1,0:T(8,128)(2,1)S(1)}, bf16[512,768]{1,0:T(8,128)(2,1)S(1)}, f32[8,768]{1,0:T(8,128)S(1)}, f32[1,...) custom-call(s32[1]{0:T(128)} %bitcast.35.index_ref, ...), custom_call_target="tpu_custom_call" | custom-call | flops 10267656192 | bytes 33030144 | tf_op jit(solution)/shard_map/feed_back/pallas_call | solution.py:1001
  265.8 11.1 %collective-permute-start.16 = (bf16[4,384,768]{2,1,0:T(8,128)(2,1)}, bf16[4,384,768]{2,1,0:T(8,128)(2,1)S(1)}, u32[]{:S(2)}, u32[]{:S(2)}) collective-permute-start(bf16[4,384,768]{2,1,0:T(8,128)(2,1)} %bitcast.519), channel_id=1, source_target_pairs={{0,2},{2,0},{4,6},{6,4},{8,10},{10,8},{12,14},{14,12},{16,18},{18,... | collective-permute-start | bytes 7077896 | tf_op jit(solution)/shard_map/ppermute | solution.py:50
  277.0 10.7 %attend_back.4 = (bf16[2,256,768]{2,1,0:T(8,128)(2,1)S(1)}, f32[2,2,256,768]{3,2,1,0:T(8,128)}, f32[2,2,64,768]{3,2,1,0:T(8,128)S(1)}, bf16[2,2,144,768]{3,2,1,0:T(8,128)(2,1)}, bf16[2,2,128,768]{3,2,1,0:T(8,128)(2,1)S(1)}) custom-call(f32[2,256,256]{2,1,0:T(8,128)S(1)} %copy-done.8, f32[2,192,256]{2,1,0:T(8,128)S(1)} %pad_maximum_fusion.11.far_ref.refs_1_, ...), custom_call_target="tpu_custom_call" | custom-call | flops 983040000 | bytes 6000000 | tf_op jit(solution)/shard_map/attend_back/pallas_call | solution.py:411
  287.8 10.3 %attend_back.5 = (bf16[2,256,768]{2,1,0:T(8,128)(2,1)S(1)}, f32[2,2,256,768]{3,2,1,0:T(8,128)}, f32[2,2,64,768]{3,2,1,0:T(8,128)S(1)}, bf16[2,2,144,768]{3,2,1,0:T(8,128)(2,1)}, bf16[2,2,128,768]{3,2,1,0:T(8,128)(2,1)S(1)}) custom-call(f32[2,256,256]{2,1,0:T(8,128)S(1)} %copy-done.8, ...), custom_call_target="tpu_custom_call", output_to_operand_aliasing={{0}: (17, {}), {1}: (18, {}), {2}: (19, {}), {3}: (20, {}),... | custom-call | flops 983040000 | bytes 6000000 | tf_op jit(solution)/shard_map/attend_back/pallas_call | solution.py:411
  310.1 5.4 collective-permute-done.20.rest_1_
  315.5 6.2 %pool_back.2 = (bf16[2,2,256,768]{3,2,1,0:T(8,128)(2,1)S(1)}, f32[2,8,768]{2,1,0:T(8,128)S(1)}) custom-call(bf16[320,256]{1,0:T(8,128)(2,1)S(1)} %copy-done.17, bf16[256,320]{1,0:T(8,128)(2,1)S(1)} %fusion.42.spread_ref, f32[2,8,768]{2,1,0:T(8,128)S(1)} %copy-done.34, bf16[2,256,2304]{2,1,0:T(8,128)(2,1)} %bitcast.376, bf16[2,128,1536]{2,1,0:T(8,128)(2,1)S(1)} %copy-done.3, ...), custom_call_target="tpu_custom_call" | custom-call | flops 1572864000 | bytes 9000000 | tf_op jit(solution)/shard_map/pool_back/pallas_call | solution.py:649
  326.1 5.2 weight_grads.3
  331.3 9.0 %collective-permute-start.23 = (bf16[1,384,3072]{2,1,0:T(8,128)(2,1)}, bf16[1,384,3072]{2,1,0:T(8,128)(2,1)S(1)}, u32[]{:S(2)}, u32[]{:S(2)}) collective-permute-start(bf16[1,384,3072]{2,1,0:T(8,128)(2,1)} %bitcast.520), channel_id=1, source_target_pairs={{0,2},{2,0},{4,6},{6,4},{8,10},{10,8},{12,14},{14,12},{16,18},{18,... | collective-permute-start | bytes 7077896 | tf_op jit(solution)/shard_map/ppermute | solution.py:50
  344.4 20.9 %feed_back.3 = (f32[512,768]{1,0:T(8,128)S(1)}, bf16[512,768]{1,0:T(8,128)(2,1)S(1)}, bf16[512,768]{1,0:T(8,128)(2,1)S(1)}, f32[8,768]{1,0:T(8,128)S(1)}, f32[1,...) custom-call(s32[1]{0:T(128)} %bitcast.35.index_ref, ...), custom_call_target="tpu_custom_call" | custom-call | flops 10267656192 | bytes 35389440 | tf_op jit(solution)/shard_map/feed_back/pallas_call | solution.py:1001
  381.7 10.4 %attend_back.6 = (bf16[2,256,768]{2,1,0:T(8,128)(2,1)S(1)}, f32[2,2,256,768]{3,2,1,0:T(8,128)}, f32[2,2,64,768]{3,2,1,0:T(8,128)S(1)}, bf16[2,2,144,768]{3,2,1,0:T(8,128)(2,1)}, bf16[2,2,128,768]{3,2,1,0:T(8,128)(2,1)S(1)}) custom-call(f32[2,256,256]{2,1,0:T(8,128)S(1)} %copy-done.8, f32[2,192,256]{2,1,0:T(8,128)S(1)} %pad_maximum_fusion.11.far_ref.refs_1_, ...), custom_call_target="tpu_custom_call" | custom-call | flops 983040000 | bytes 6000000 | tf_op jit(solution)/shard_map/attend_back/pallas_call | solution.py:411
  408.6 10.5 %attend_back.7 = (bf16[2,256,768]{2,1,0:T(8,128)(2,1)S(1)}, f32[2,2,256,768]{3,2,1,0:T(8,128)}, f32[2,2,64,768]{3,2,1,0:T(8,128)S(1)}, bf16[2,2,144,768]{3,2,1,0:T(8,128)(2,1)}, bf16[2,2,128,768]{3,2,1,0:T(8,128)(2,1)S(1)}) custom-call(f32[2,256,256]{2,1,0:T(8,128)S(1)} %copy-done.8, ...), custom_call_target="tpu_custom_call", output_to_operand_aliasing={{0}: (17, {}), {1}: (18, {}), {2}: (19, {}), {3}: (20, {}),... | custom-call | flops 983040000 | bytes 6000000 | tf_op jit(solution)/shard_map/attend_back/pallas_call | solution.py:411
  420.6 17.6 %collective-permute-done.31 = bf16[4,192,768]{2,1,0:T(8,128)(2,1)S(1)} collective-permute-done((bf16[4,192,768]{2,1,0:T(8,128)(2,1)}, bf16[4,192,768]{2,1,0:T(8,128)(2,1)S(1)}, u32[]{:S(2)}, u32[]{:S(2)}) %collective-permute-start.31) | collective-permute-done | bytes 1179680 | tf_op jit(solution)/shard_map/ppermute | solution.py:50
  451.1 5.6 collective-permute-start.46
  458.8 6.0 %pool_back.3 = (bf16[2,2,256,768]{3,2,1,0:T(8,128)(2,1)S(1)}, f32[2,8,768]{2,1,0:T(8,128)S(1)}) custom-call(bf16[320,256]{1,0:T(8,128)(2,1)S(1)} %copy-done.17, bf16[256,320]{1,0:T(8,128)(2,1)S(1)} %copy-done.24, f32[2,8,768]{2,1,0:T(8,128)S(1)} %copy-done.32, bf16[2,256,2304]{2,1,0:T(8,128)(2,1)} %bitcast.363, ...), custom_call_target="tpu_custom_call" | custom-call | flops 1572864000 | bytes 9000000 | tf_op jit(solution)/shard_map/pool_back/pallas_call | solution.py:649
  482.9 7.3 %collective-permute-done.48 = bf16[1,96,3072]{2,1,0:T(8,128)(2,1)S(1)} collective-permute-done((bf16[1,96,3072]{2,1,0:T(8,128)(2,1)S(1)}, bf16[1,96,3072]{2,1,0:T(8,128)(2,1)S(1)}, u32[]{:S(2)}, u32[]{:S(2)}) %collective-permute-start.48) | collective-permute-done | bytes 589856 | tf_op jit(solution)/shard_map/ppermute | solution.py:50
  491.7 10.8 %collective-permute-done.50 = bf16[1,96,3072]{2,1,0:T(8,128)(2,1)S(1)} collective-permute-done((bf16[1,96,3072]{2,1,0:T(8,128)(2,1)S(1)}, bf16[1,96,3072]{2,1,0:T(8,128)(2,1)S(1)}, u32[]{:S(2)}, u32[]{:S(2)}) %collective-permute-start.50) | collective-permute-done | bytes 589856 | tf_op jit(solution)/shard_map/ppermute | solution.py:50
  527.1 7.3 %collective-permute-done.54 = bf16[1,24,3072]{2,1,0:T(8,128)(2,1)S(1)} collective-permute-done((bf16[1,24,3072]{2,1,0:T(8,128)(2,1)S(1)}, bf16[1,24,3072]{2,1,0:T(8,128)(2,1)S(1)}, u32[]{:S(2)}, u32[]{:S(2)}) %collective-permute-start.54) | collective-permute-done | bytes 147488 | tf_op jit(solution)/shard_map/ppermute | solution.py:50
  540.0 5.9 %units_back.1 = f32[48,3072]{1,0:T(8,128)} custom-call(bf16[4,384,1536]{2,1,0:T(8,128)(2,1)S(1)} %add_convert_fusion.spread_ref, f32[48,3072]{1,0:T(8,128)S(1)} %pad_maximum_fusion.7.refs_0_.refs_1_.refs_2_.refs_3_, f32[48,3072]{1,0:T(8,128)S(1)} %pad_maximum_fusion.7.refs_0_.refs_1_.refs_2_.refs_3_, ...), custom_call_target="tpu_custom_call" | custom-call | tf_op jit(solution)/shard_map/units_back/pallas_call | solution.py:1068
  549.8 5.5 collective-permute-done.45
  (548 shorter events, 239.2 us)
Async XLA Ops:
  7.4 137.9 %all-gather.3.cloned.1.call-start = ((), (), s32[]{:S(2)}) async-start(), calls=%async_computation | async-start | bytes 10948608 | tf_op jit(solution)/shard_map/all_gather | solution.py:1285
  24.2 202.6 %all-gather.5.cloned.1.call-start = ((), (), s32[]{:S(2)}) async-start(), calls=%async_computation.1 | async-start | bytes 9732096 | tf_op jit(solution)/shard_map/all_gather | solution.py:1285
  48.2 31.7 %collective-permute-start.5 = (bf16[1,192,2432]{2,1,0:T(8,128)(2,1)S(1)}, bf16[1,192,2432]{2,1,0:T(8,128)(2,1)S(1)}, u32[]{:S(2)}, u32[]{:S(2)}) collective-permute-start(bf16[1,192,2432]{2,1,0:T(8,128)(2,1)S(1)} %bitcast.423), channel_id=1, source_target_pairs={{0,4},{2,6},{4,0},{6,2},{8,12},{10,14},{12,8},{14,10},{16,20},{18,... | collective-permute-start | bytes 2801672 | tf_op jit(solution)/shard_map/ppermute | solution.py:50
  112.2 25.5 %collective-permute-start.10 = (bf16[1,96,3072]{2,1,0:T(8,128)(2,1)S(1)}, bf16[1,96,3072]{2,1,0:T(8,128)(2,1)}, u32[]{:S(2)}, u32[]{:S(2)}) collective-permute-start(bf16[1,96,3072]{2,1,0:T(8,128)(2,1)S(1)} %bitcast.443), channel_id=1, source_target_pairs={{0,4},{2,6},{4,0},{6,2},{8,12},{10,14},{12,8},{14,10},{16,20},{18,... | collective-permute-start | bytes 1769480 | tf_op jit(solution)/shard_map/ppermute | solution.py:50
  139.4 34.9 %collective-permute-start.11 = (bf16[1,192,3072]{2,1,0:T(8,128)(2,1)S(1)}, bf16[1,192,3072]{2,1,0:T(8,128)(2,1)}, u32[]{:S(2)}, u32[]{:S(2)}) collective-permute-start(bf16[1,192,3072]{2,1,0:T(8,128)(2,1)S(1)} %bitcast.418), channel_id=1, source_target_pairs={{0,1},{1,0},{2,3},{3,2},{4,5},{5,4},{6,7},{7,6},{8,9},{9,8},{10,11... | collective-permute-start | bytes 3538952 | tf_op jit(solution)/shard_map/ppermute | solution.py:50
  265.8 35.8 %collective-permute-start.16 = (bf16[4,384,768]{2,1,0:T(8,128)(2,1)}, bf16[4,384,768]{2,1,0:T(8,128)(2,1)S(1)}, u32[]{:S(2)}, u32[]{:S(2)}) collective-permute-start(bf16[4,384,768]{2,1,0:T(8,128)(2,1)} %bitcast.519), channel_id=1, source_target_pairs={{0,2},{2,0},{4,6},{6,4},{8,10},{10,8},{12,14},{14,12},{16,18},{18,... | collective-permute-start | bytes 7077896 | tf_op jit(solution)/shard_map/ppermute | solution.py:50
  276.9 24.7 %collective-permute-start.17 = (bf16[1,384,3072]{2,1,0:T(8,128)(2,1)}, bf16[1,384,3072]{2,1,0:T(8,128)(2,1)}, u32[]{:S(2)}, u32[]{:S(2)}) collective-permute-start(bf16[1,384,3072]{2,1,0:T(8,128)(2,1)} %bitcast.518), channel_id=1, source_target_pairs={{0,2},{2,0},{4,6},{6,4},{8,10},{10,8},{12,14},{14,12},{16,18},{18,... | collective-permute-start | bytes 7077896 | tf_op jit(solution)/shard_map/ppermute | solution.py:50
  298.1 17.4 %collective-permute-start.19 = (bf16[2,2,144,768]{3,2,1,0:T(8,128)(2,1)}, bf16[2,2,144,768]{3,2,1,0:T(8,128)(2,1)S(1)}, u32[]{:S(2)}, u32[]{:S(2)}) collective-permute-start(bf16[2,2,144,768]{3,2,1,0:T(8,128)(2,1)} %get-tuple-element.333), channel_id=1, source_target_pairs={{2,0},{4,2},{6,4},{8,6},{10,8},{12,10},{14,12},{16,14},{18,16},{20... | collective-permute-start | bytes 2654216 | tf_op jit(solution)/shard_map/ppermute | solution.py:171
  331.3 39.6 %collective-permute-start.23 = (bf16[1,384,3072]{2,1,0:T(8,128)(2,1)}, bf16[1,384,3072]{2,1,0:T(8,128)(2,1)S(1)}, u32[]{:S(2)}, u32[]{:S(2)}) collective-permute-start(bf16[1,384,3072]{2,1,0:T(8,128)(2,1)} %bitcast.520), channel_id=1, source_target_pairs={{0,2},{2,0},{4,6},{6,4},{8,10},{10,8},{12,14},{14,12},{16,18},{18,... | collective-permute-start | bytes 7077896 | tf_op jit(solution)/shard_map/ppermute | solution.py:50
  340.3 29.3 %collective-permute-start.21 = (bf16[4,192,768]{2,1,0:T(8,128)(2,1)}, bf16[4,192,768]{2,1,0:T(8,128)(2,1)}, u32[]{:S(2)}, u32[]{:S(2)}) collective-permute-start(bf16[4,192,768]{2,1,0:T(8,128)(2,1)} %get-tuple-element.355), channel_id=1, source_target_pairs={{0,4},{2,6},{4,0},{6,2},{8,12},{10,14},{12,8},{14,10},{16,20},{18,... | collective-permute-start | bytes 3538952 | tf_op jit(solution)/shard_map/ppermute | solution.py:50
  342.6 28.2 %collective-permute-start.22 = (bf16[1,192,3072]{2,1,0:T(8,128)(2,1)S(1)}, bf16[1,192,3072]{2,1,0:T(8,128)(2,1)}, u32[]{:S(2)}, u32[]{:S(2)}) collective-permute-start(bf16[1,192,3072]{2,1,0:T(8,128)(2,1)S(1)} %bitcast.451), channel_id=1, source_target_pairs={{0,1},{1,0},{2,3},{3,2},{4,5},{5,4},{6,7},{7,6},{8,9},{9,8},{10,11... | collective-permute-start | bytes 3538952 | tf_op jit(solution)/shard_map/ppermute | solution.py:50
  376.9 17.4 %collective-permute-start.26 = (bf16[4,384,768]{2,1,0:T(8,128)(2,1)}, bf16[4,384,768]{2,1,0:T(8,128)(2,1)}, u32[]{:S(2)}, u32[]{:S(2)}) collective-permute-start(bf16[4,384,768]{2,1,0:T(8,128)(2,1)} %bitcast.89), channel_id=1, source_target_pairs={{0,2},{2,0},{4,6},{6,4},{8,10},{10,8},{12,14},{14,12},{16,18},{18,... | collective-permute-start | bytes 7077896 | tf_op jit(solution)/shard_map/ppermute | solution.py:50
  376.9 17.4 %collective-permute-start.27 = (bf16[1,384,3072]{2,1,0:T(8,128)(2,1)}, bf16[1,384,3072]{2,1,0:T(8,128)(2,1)S(1)}, u32[]{:S(2)}, u32[]{:S(2)}) collective-permute-start(bf16[1,384,3072]{2,1,0:T(8,128)(2,1)} %bitcast.90), channel_id=1, source_target_pairs={{0,2},{2,0},{4,6},{6,4},{8,10},{10,8},{12,14},{14,12},{16,18},{18,... | collective-permute-start | bytes 7077896 | tf_op jit(solution)/shard_map/ppermute | solution.py:50
  379.7 39.4 %collective-permute-start.30 = (bf16[1,192,3072]{2,1,0:T(8,128)(2,1)}, bf16[1,192,3072]{2,1,0:T(8,128)(2,1)}, u32[]{:S(2)}, u32[]{:S(2)}) collective-permute-start(bf16[1,192,3072]{2,1,0:T(8,128)(2,1)} %bitcast.88), channel_id=1, source_target_pairs={{0,8},{2,10},{4,12},{6,14},{8,0},{10,2},{12,4},{14,6},{16,24},{18,... | collective-permute-start | bytes 3538952 | tf_op jit(solution)/shard_map/ppermute | solution.py:50
  403.7 34.6 %collective-permute-start.31 = (bf16[4,192,768]{2,1,0:T(8,128)(2,1)}, bf16[4,192,768]{2,1,0:T(8,128)(2,1)S(1)}, u32[]{:S(2)}, u32[]{:S(2)}) collective-permute-start(bf16[4,192,768]{2,1,0:T(8,128)(2,1)} %get-tuple-element.390), channel_id=1, source_target_pairs={{0,4},{2,6},{4,0},{6,2},{8,12},{10,14},{12,8},{14,10},{16,20},{18,... | collective-permute-start | bytes 3538952 | tf_op jit(solution)/shard_map/ppermute | solution.py:50
  404.2 34.1 %collective-permute-start.32 = (bf16[1,192,3072]{2,1,0:T(8,128)(2,1)}, bf16[1,192,3072]{2,1,0:T(8,128)(2,1)S(1)}, u32[]{:S(2)}, u32[]{:S(2)}) collective-permute-start(bf16[1,192,3072]{2,1,0:T(8,128)(2,1)} %bitcast.103), channel_id=1, source_target_pairs={{0,1},{1,0},{2,3},{3,2},{4,5},{5,4},{6,7},{7,6},{8,9},{9,8},{10,11... | collective-permute-start | bytes 3538952 | tf_op jit(solution)/shard_map/ppermute | solution.py:50
  419.1 37.7 %collective-permute-start.34 = (bf16[2,2,144,768]{3,2,1,0:T(8,128)(2,1)}, bf16[2,2,144,768]{3,2,1,0:T(8,128)(2,1)S(1)}, u32[]{:S(2)}, u32[]{:S(2)}) collective-permute-start(bf16[2,2,144,768]{3,2,1,0:T(8,128)(2,1)} %get-tuple-element.396), channel_id=1, source_target_pairs={{2,0},{4,2},{6,4},{8,6},{10,8},{12,10},{14,12},{16,14},{18,16},{20... | collective-permute-start | bytes 2654216 | tf_op jit(solution)/shard_map/ppermute | solution.py:171
  439.1 18.5 %collective-permute-start.33 = (bf16[2,2,128,768]{3,2,1,0:T(8,128)(2,1)S(1)}, bf16[2,2,128,768]{3,2,1,0:T(8,128)(2,1)}, u32[]{:S(2)}, u32[]{:S(2)}) collective-permute-start(bf16[2,2,128,768]{3,2,1,0:T(8,128)(2,1)S(1)} %get-tuple-element.395.rest_0_), channel_id=1, source_target_pairs={{0,2},{2,4},{4,6},{6,8},{8,10},{10,12},{12,14},{14,16},{16,18},{18... | collective-permute-start | bytes 2359304 | tf_op jit(solution)/shard_map/ppermute | solution.py:171
  451.1 28.6 %collective-permute-start.46 = (bf16[4,24,768]{2,1,0:T(8,128)(2,1)S(1)}, bf16[4,24,768]{2,1,0:T(8,128)(2,1)S(1)}, u32[]{:S(2)}, u32[]{:S(2)}) collective-permute-start(bf16[4,24,768]{2,1,0:T(8,128)(2,1)S(1)} %copy-done.115), channel_id=1, source_target_pairs={{0,16},{2,18},{4,20},{6,22},{8,24},{10,26},{12,28},{14,30},{16,0},... | collective-permute-start | bytes 442376 | tf_op jit(solution)/shard_map/ppermute | solution.py:50
  456.7 24.4 %collective-permute-start.47 = (bf16[1,24,3072]{2,1,0:T(8,128)(2,1)S(1)}, bf16[1,24,3072]{2,1,0:T(8,128)(2,1)S(1)}, u32[]{:S(2)}, u32[]{:S(2)}) collective-permute-start(bf16[1,24,3072]{2,1,0:T(8,128)(2,1)S(1)} %fusion.63), channel_id=1, source_target_pairs={{0,16},{2,18},{4,20},{6,22},{8,24},{10,26},{12,28},{14,30},{16,0},... | collective-permute-start | bytes 442376 | tf_op jit(solution)/shard_map/ppermute | solution.py:50
  474.1 16.2 %collective-permute-start.48 = (bf16[1,96,3072]{2,1,0:T(8,128)(2,1)S(1)}, bf16[1,96,3072]{2,1,0:T(8,128)(2,1)S(1)}, u32[]{:S(2)}, u32[]{:S(2)}) collective-permute-start(bf16[1,96,3072]{2,1,0:T(8,128)(2,1)S(1)} %get-tuple-element.438), channel_id=1, source_target_pairs={{0,4},{2,6},{4,0},{6,2},{8,12},{10,14},{12,8},{14,10},{16,20},{18,... | collective-permute-start | bytes 1769480 | tf_op jit(solution)/shard_map/ppermute | solution.py:50
  475.5 16.2 %collective-permute-start.49 = (bf16[4,96,768]{2,1,0:T(8,128)(2,1)S(1)}, bf16[4,96,768]{2,1,0:T(8,128)(2,1)S(1)}, u32[]{:S(2)}, u32[]{:S(2)}) collective-permute-start(bf16[4,96,768]{2,1,0:T(8,128)(2,1)S(1)} %get-tuple-element.439), channel_id=1, source_target_pairs={{0,1},{1,0},{2,3},{3,2},{4,5},{5,4},{6,7},{7,6},{8,9},{9,8},{10,11... | collective-permute-start | bytes 1769480 | tf_op jit(solution)/shard_map/ppermute | solution.py:50
  476.2 26.3 %collective-permute-start.50 = (bf16[1,96,3072]{2,1,0:T(8,128)(2,1)S(1)}, bf16[1,96,3072]{2,1,0:T(8,128)(2,1)S(1)}, u32[]{:S(2)}, u32[]{:S(2)}) collective-permute-start(bf16[1,96,3072]{2,1,0:T(8,128)(2,1)S(1)} %get-tuple-element.440), channel_id=1, source_target_pairs={{0,4},{2,6},{4,0},{6,2},{8,12},{10,14},{12,8},{14,10},{16,20},{18,... | collective-permute-start | bytes 1769480 | tf_op jit(solution)/shard_map/ppermute | solution.py:50
  479.7 26.1 %collective-permute-start.38 = (bf16[1,192,1664]{2,1,0:T(8,128)(2,1)S(1)}, bf16[1,192,1664]{2,1,0:T(8,128)(2,1)S(1)}, u32[]{:S(2)}, u32[]{:S(2)}) collective-permute-start(bf16[1,192,1664]{2,1,0:T(8,128)(2,1)S(1)} %bitcast.470), channel_id=1, source_target_pairs={{0,1},{1,0},{2,3},{3,2},{4,5},{5,4},{6,7},{7,6},{8,9},{9,8},{10,11... | collective-permute-start | bytes 1916936 | tf_op jit(solution)/shard_map/ppermute | solution.py:50
  481.1 24.7 %collective-permute-start.39 = (bf16[1,192,1536]{2,1,0:T(8,128)(2,1)S(1)}, bf16[1,192,1536]{2,1,0:T(8,128)(2,1)S(1)}, u32[]{:S(2)}, u32[]{:S(2)}) collective-permute-start(bf16[1,192,1536]{2,1,0:T(8,128)(2,1)S(1)} %bitcast.471), channel_id=1, source_target_pairs={{0,8},{2,10},{4,12},{6,14},{8,0},{10,2},{12,4},{14,6},{16,24},{18,... | collective-permute-start | bytes 1769480 | tf_op jit(solution)/shard_map/ppermute | solution.py:50
  506.1 18.2 %collective-permute-start.40 = (bf16[1,96,1664]{2,1,0:T(8,128)(2,1)S(1)}, bf16[1,96,1664]{2,1,0:T(8,128)(2,1)S(1)}, u32[]{:S(2)}, u32[]{:S(2)}) collective-permute-start(bf16[1,96,1664]{2,1,0:T(8,128)(2,1)S(1)} %get-tuple-element.425), channel_id=1, source_target_pairs={{0,4},{2,6},{4,0},{6,2},{8,12},{10,14},{12,8},{14,10},{16,20},{18,... | collective-permute-start | bytes 958472 | tf_op jit(solution)/shard_map/ppermute | solution.py:50
  507.2 17.1 %collective-permute-start.41 = (bf16[1,96,1536]{2,1,0:T(8,128)(2,1)S(1)}, bf16[1,96,1536]{2,1,0:T(8,128)(2,1)S(1)}, u32[]{:S(2)}, u32[]{:S(2)}) collective-permute-start(bf16[1,96,1536]{2,1,0:T(8,128)(2,1)S(1)} %get-tuple-element.426), channel_id=1, source_target_pairs={{0,4},{2,6},{4,0},{6,2},{8,12},{10,14},{12,8},{14,10},{16,20},{18,... | collective-permute-start | bytes 884744 | tf_op jit(solution)/shard_map/ppermute | solution.py:50
  518.4 16.1 %collective-permute-start.54 = (bf16[1,24,3072]{2,1,0:T(8,128)(2,1)S(1)}, bf16[1,24,3072]{2,1,0:T(8,128)(2,1)S(1)}, u32[]{:S(2)}, u32[]{:S(2)}) collective-permute-start(bf16[1,24,3072]{2,1,0:T(8,128)(2,1)S(1)} %fusion.66), channel_id=1, source_target_pairs={{0,16},{2,18},{4,20},{6,22},{8,24},{10,26},{12,28},{14,30},{16,0},... | collective-permute-start | bytes 442376 | tf_op jit(solution)/shard_map/ppermute | solution.py:50
  521.4 16.2 %collective-permute-start.55 = (bf16[4,24,768]{2,1,0:T(8,128)(2,1)S(1)}, bf16[4,24,768]{2,1,0:T(8,128)(2,1)S(1)}, u32[]{:S(2)}, u32[]{:S(2)}) collective-permute-start(bf16[4,24,768]{2,1,0:T(8,128)(2,1)S(1)} %fusion.67), channel_id=1, source_target_pairs={{0,16},{2,18},{4,20},{6,22},{8,24},{10,26},{12,28},{14,30},{16,0},... | collective-permute-start | bytes 442376 | tf_op jit(solution)/shard_map/ppermute | solution.py:50
  521.5 18.3 %collective-permute-start.56 = (bf16[1,24,3072]{2,1,0:T(8,128)(2,1)S(1)}, bf16[1,24,3072]{2,1,0:T(8,128)(2,1)S(1)}, u32[]{:S(2)}, u32[]{:S(2)}) collective-permute-start(bf16[1,24,3072]{2,1,0:T(8,128)(2,1)S(1)} %fusion.68), channel_id=1, source_target_pairs={{0,16},{2,18},{4,20},{6,22},{8,24},{10,26},{12,28},{14,30},{16,0},... | collective-permute-start | bytes 442376 | tf_op jit(solution)/shard_map/ppermute | solution.py:50
  524.5 21.4 %collective-permute-start.42 = (bf16[1,48,1664]{2,1,0:T(8,128)(2,1)S(1)}, bf16[1,48,1664]{2,1,0:T(8,128)(2,1)S(1)}, u32[]{:S(2)}, u32[]{:S(2)}) collective-permute-start(bf16[1,48,1664]{2,1,0:T(8,128)(2,1)S(1)} %bitcast.503), channel_id=1, source_target_pairs={{0,8},{2,10},{4,12},{6,14},{8,0},{10,2},{12,4},{14,6},{16,24},{18,... | collective-permute-start | bytes 479240 | tf_op jit(solution)/shard_map/ppermute | solution.py:50
  526.0 19.9 %collective-permute-start.43 = (bf16[1,48,1536]{2,1,0:T(8,128)(2,1)S(1)}, bf16[1,48,1536]{2,1,0:T(8,128)(2,1)S(1)}, u32[]{:S(2)}, u32[]{:S(2)}) collective-permute-start(bf16[1,48,1536]{2,1,0:T(8,128)(2,1)S(1)} %get-tuple-element.430), channel_id=1, source_target_pairs={{0,1},{1,0},{2,3},{3,2},{4,5},{5,4},{6,7},{7,6},{8,9},{9,8},{10,11... | collective-permute-start | bytes 442376 | tf_op jit(solution)/shard_map/ppermute | solution.py:50
  (162 other events, 1373.9 us)
Sparse Core Ops, SparseCore 0:
  24.3 99.4 all-gather.2
  126.7 100.1 all-gather.4
